TPU v7x, 32 devices: a whole 2x2x4 slice. The times are simulated.
32 devices in a mesh: ctx: 8 (over y, x, core), kv: 4 (over z).
Axes of the slice: x: 2, y: 2, z: 4, core: 2. Of those that a mesh axis runs over, the one named last changes fastest.
Arguments:
- prompt_in: bfloat16 [128, 8192], P(None, 'ctx'), may hold values from -6 to 6
- step_in: bfloat16 [3, 32, 8192], P(None, None, 'ctx'), may hold values from -6 to 6
- norm_gain: bfloat16 [8192], P('ctx'), may hold values from 0.099609375 to 1.8984375
- query_weight: bfloat16 [8192, 4096], P('ctx', 'kv'), may hold values from -0.125 to 0.125
- key_weight: bfloat16 [8192, 512], P('ctx', 'kv'), may hold values from -0.125 to 0.125
- value_weight: bfloat16 [8192, 512], P('ctx', 'kv'), may hold values from -0.0625 to 0.0625
- out_weight: bfloat16 [4096, 8192], P('kv', 'ctx'), may hold values from -0.125 to 0.125
- key_cache: bfloat16 [4, 65536, 128], P('kv', 'ctx'), may hold values from -540 to 540
- value_cache: bfloat16 [4, 65536, 128], P('kv', 'ctx'), may hold values from -5 to 5
- cache_lengths: int32 [8], P('ctx'), may hold values from 2048 to 8192
- visible: int32 [32], replicated, may hold values from 1 to 128, as said below
Outputs:
- prompt_out: bfloat16 [128, 8192], P('kv', 'ctx')
- step_out: bfloat16 [3, 32, 8192], P(None, 'kv', 'ctx')
Inputs may be any that keep to these rules, and one draw needn't show every extreme that they name: `visible`: prompt tokens seen by each decode row.
All inputs are finite; a program needn't handle non-finite values.
Results may differ from a plain program's by a relative error of at most 0.035.
Values may be sent and summed in bfloat16 or wider, within the bound.
No kernel may reach another device: no remote copies, remote signals or barrier semaphores. Data moves between devices by JAX's collectives and lax.ppermute only.
A program may use at most 192 MiB of HBM per device.

v0:
```python
import jax
import jax.numpy as jnp
from jax import lax
from jax.sharding import PartitionSpec as P

D = 8192
HD = 128


EPSILON = 1e-05


def normalize_rows(inputs, norm_gain):
    widened = inputs.astype(jnp.float32)
    scaled = (widened * norm_gain.astype(jnp.float32)).astype(jnp.bfloat16)
    squares = jnp.sum(widened * widened, axis=-1)
    return (scaled, squares)


def shard_attention(queries, key_shard, value_shard, length, extra_pairs, extra_mask):
    flat_rows, head_size = queries.shape
    block_rows = 512 if flat_rows % 512 == 0 else flat_rows
    blocks = flat_rows // block_rows
    extra_count = extra_pairs.shape[0]
    slots_live = lax.broadcasted_iota(jnp.int32, (1, key_shard.shape[0]), 1) < length
    extra_keys = extra_pairs[:, :head_size]
    extra_values = extra_pairs[:, head_size:]
    factor = head_size ** (-0.5)

    def one_block(operands):
        query_block, mask_block = operands
        cache_scores = (
            jnp.einsum("fd,cd->fc", query_block, key_shard, preferred_element_type=jnp.float32)
            * factor
        )
        extra_scores = (
            jnp.einsum("fd,ed->fe", query_block, extra_keys, preferred_element_type=jnp.float32)
            * factor
        )
        cache_scores = jnp.where(slots_live, cache_scores, -jnp.inf)
        extra_scores = jnp.where(mask_block, extra_scores, -jnp.inf)
        highest = jnp.maximum(jnp.max(cache_scores, axis=1), jnp.max(extra_scores, axis=1))
        cache_weights = jnp.exp(cache_scores - highest[:, None]).astype(jnp.bfloat16)
        extra_weights = jnp.exp(extra_scores - highest[:, None]).astype(jnp.bfloat16)
        totals = jnp.sum(cache_weights, axis=1, dtype=jnp.float32) + jnp.sum(
            extra_weights, axis=1, dtype=jnp.float32
        )
        mixture = jnp.dot(cache_weights, value_shard, preferred_element_type=jnp.float32)
        mixture = mixture + jnp.dot(extra_weights, extra_values, preferred_element_type=jnp.float32)
        return (highest, totals, mixture)

    highest, totals, mixture = lax.map(
        one_block,
        (
            queries.reshape(blocks, block_rows, head_size),
            extra_mask.reshape(blocks, block_rows, extra_count),
        ),
    )
    return (
        highest.reshape(flat_rows),
        totals.reshape(flat_rows),
        mixture.reshape(flat_rows, head_size),
    )


def run_section(
    inputs,
    limits,
    owner_rows,
    owner_steps,
    store_fn,
    stores,
    norm_gain,
    query_weight,
    pair_weight,
    out_weight,
    key_shard,
    value_shard,
    length,
):
    step_sets, row_count, _ = inputs.shape
    device_place = lax.axis_index("ctx")
    owned_rows = row_count // lax.axis_size("ctx")
    scaled, squares = normalize_rows(inputs, norm_gain)
    query_part = jnp.einsum("srd,de->sre", scaled, query_weight, preferred_element_type=jnp.float32)
    pair_part = jnp.einsum("srd,de->rse", scaled, pair_weight, preferred_element_type=jnp.float32)
    query_sum, square_sum = lax.psum((query_part, squares), "ctx")
    pair_sum = lax.psum_scatter(
        pair_part.astype(jnp.bfloat16), "ctx", scatter_dimension=0, tiled=True
    ).astype(jnp.float32)
    inverse = lax.rsqrt(square_sum / D + EPSILON)
    queries = (query_sum * inverse[:, :, None]).astype(jnp.bfloat16)
    own_inverse = jnp.swapaxes(
        lax.dynamic_slice_in_dim(inverse, device_place * owned_rows, owned_rows, 1), 0, 1
    )
    pair_rows = (pair_sum * own_inverse[:, :, None]).astype(jnp.bfloat16)
    prompt_pairs, own_pairs = store_fn(pair_rows, stores)
    extra_pairs = jnp.concatenate(
        [prompt_pairs, own_pairs.reshape(-1, own_pairs.shape[-1])], axis=0
    )
    prompt_own = prompt_pairs.shape[0]
    rows_own = own_pairs.shape[0]
    step_total = own_pairs.shape[1]
    prompt_index = device_place * prompt_own + lax.broadcasted_iota(
        jnp.int32, (1, 1, prompt_own), 2
    )
    seen_prompt = prompt_index < limits[:, :, None]
    slot_ids = lax.broadcasted_iota(jnp.int32, (1, 1, rows_own * step_total), 2)
    slot_row = device_place * rows_own + slot_ids // step_total
    slot_step = slot_ids % step_total
    seen_own = (slot_row == owner_rows[:, :, None]) & (slot_step <= owner_steps[:, :, None])
    seen_keys = jnp.concatenate([seen_prompt, seen_own], axis=2)
    heads_per = queries.shape[2] // HD
    extra_count = seen_keys.shape[2]
    extra_mask = jnp.broadcast_to(
        seen_keys[:, :, None, :], (step_sets, row_count, heads_per, extra_count)
    )
    extra_mask = extra_mask.reshape(step_sets * row_count * heads_per, extra_count)
    flat_queries = queries.reshape(step_sets * row_count * heads_per, HD)
    highest, totals, mixture = shard_attention(
        flat_queries, key_shard, value_shard, length, extra_pairs, extra_mask
    )
    overall = lax.pmax(highest, "ctx")
    rescale = jnp.exp(highest - overall)
    totals, mixture = (
        lax.psum((totals * rescale).astype(jnp.bfloat16), "ctx").astype(jnp.float32),
        lax.psum((mixture * rescale[:, None]).astype(jnp.bfloat16), "ctx").astype(jnp.float32),
    )
    attended = (mixture / totals[:, None]).astype(jnp.bfloat16)
    attended = attended.reshape(step_sets, row_count, heads_per * HD)
    my_share = lax.psum_scatter(
        jnp.einsum("srk,kd->rsd", attended, out_weight, preferred_element_type=jnp.float32).astype(
            jnp.bfloat16
        ),
        "kv",
        scatter_dimension=0,
        tiled=True,
    ).astype(jnp.float32)
    return (jnp.swapaxes(my_share, 0, 1).astype(jnp.bfloat16), (prompt_pairs, own_pairs))


def on_device(
    prompt_in,
    step_in,
    norm_gain,
    query_weight,
    key_weight,
    value_weight,
    out_weight,
    key_cache,
    value_cache,
    cache_lengths,
    visible,
):
    ctx_count = lax.axis_size("ctx")
    prompt_total = prompt_in.shape[0]
    row_total = visible.shape[0]
    step_total = step_in.shape[0]
    prompt_own = prompt_total // ctx_count
    rows_own = row_total // ctx_count
    pair_weight = jnp.concatenate([key_weight, value_weight], axis=1)
    pair_width = pair_weight.shape[1]
    shared = (
        norm_gain,
        query_weight,
        pair_weight,
        out_weight,
        key_cache[0],
        value_cache[0],
        cache_lengths[0],
    )
    stores = (
        jnp.zeros((prompt_own, pair_width), jnp.bfloat16),
        jnp.zeros((rows_own, step_total, pair_width), jnp.bfloat16),
    )

    def keep_prompt(pair_rows, current):
        return (pair_rows[:, 0, :], current[1])

    prompt_limits = lax.broadcasted_iota(jnp.int32, (1, prompt_total), 1) + 1
    nobody = jnp.full((1, prompt_total), -1, jnp.int32)
    prompt_out, stores = run_section(
        prompt_in[None], prompt_limits, nobody, nobody, keep_prompt, stores, *shared
    )
    row_ids = lax.broadcasted_iota(jnp.int32, (1, row_total), 1)
    outputs = []
    for step_index in range(step_total):

        def keep_one(pair_rows, current, step_index=step_index):
            return (
                current[0],
                lax.dynamic_update_slice_in_dim(current[1], pair_rows, step_index, 1),
            )

        step_ids = jnp.full((1, row_total), step_index, jnp.int32)
        result, stores = run_section(
            step_in[step_index : step_index + 1],
            visible[None, :],
            row_ids,
            step_ids,
            keep_one,
            stores,
            *shared
        )
        outputs.append(result)
    step_out = jnp.concatenate(outputs, axis=0)
    return (prompt_out[0], step_out)


def solution(mesh):
    placed = (
        P(None, "ctx"),
        P(None, None, "ctx"),
        P("ctx"),
        P("ctx", "kv"),
        P("ctx", "kv"),
        P("ctx", "kv"),
        P("kv", "ctx"),
        P("kv", "ctx", None),
        P("kv", "ctx", None),
        P("ctx"),
        P(),
    )
    return jax.shard_map(
        on_device,
        mesh=mesh,
        in_specs=placed,
        out_specs=(P("kv", "ctx"), P(None, "kv", "ctx")),
        check_vma=False,
    )
```

profile of v0, /device:TPU:0, one launch (start us, length us, event | category | flops | bytes accessed | tf_op | source)
XLA Modules:
  0.0 360.4 jit_solution(5557264532386437198)
XLA Ops:
  12.3 2.0 convolution_bitcast_fusion.2
  19.5 15.1 %all-reduce.6 = (f32[1,128]{1,0:T(1,128)S(1)}, f32[1,32]{1,0:T(1,128)S(1)}, f32[1,32]{1,0:T(1,128)S(1)}, f32[1,32]{1,0:T(1,128)S(1)}) all-reduce(f32[1,128]{1,0:T(1,128)S(1)} %bitcast.217, f32[1,32]{1,0:T(1,128)S(1)} %bitcast.219, f32[1,32]{1,0:T(1,128)S(1)} %bitcast.220, ...), channel_id=1, replica_groups=mesh['ctx'=8,'kv'=4] {'ctx'}, use_global_device_ids=true, to_apply=%region_2.0 | all-reduce | flops 224 | bytes 1792 | tf_op jit(solution)/shard_map/psum | solution.py:87
  36.5 22.9 %all-reduce.10 = (bf16[32,1,256]{2,0,1:T(8,128)(2,1)S(1)}, bf16[32,1,256]{2,0,1:T(8,128)(2,1)S(1)}, bf16[32,1,256]{2,0,1:T(8,128)(2,1)S(1)}) all-reduce(bf16[32,1,256]{2,0,1:T(8,128)(2,1)S(1)} %fusion.30, bf16[32,1,256]{2,0,1:T(8,128)(2,1)S(1)} %fusion.31, ...), channel_id=4, replica_groups=mesh['ctx'=8,'kv'=4] {'ctx'}, use_global_device_ids=true, to_apply=%region_18.19.clone | all-reduce | flops 24576 | bytes 98304
  61.3 6.7 %all-reduce.16.cloned.1.call-done = bf16[128,1,256]{2,1,0:T(2,128)(2,1)} async-done(((bf16[128,1,256]{2,1,0:T(2,128)(2,1)}), bf16[128,1,256]{2,1,0:T(2,128)(2,1)}) %all-reduce.16.cloned.1.call-update) | async-done | bytes 65552
  68.9 58.8 %all-reduce.18.cloned.1.call-done = (f32[1,128,1024]{2,1,0:T(8,128)}, f32[1,32,1024]{2,1,0:T(8,128)}, f32[1,32,1024]{2,1,0:T(8,128)}, f32[1,32,1024]{2,1,0:T(8,128)}) async-done(((f32[1,128,1024]{2,1,0:T(8,128)}, f32[1,32,1024]{2,1,0:T(8,128)}, f32[1,32,1024]{2,1,0:T(8,128)}, f32[1,32,1024]{2,1,0:T(8,128)}), (f32[1,128,1024]{2,1,0:T(8,128)}, f32[1,32,1024]{2,1,0:T(8,128)}, f32[1,32,1024]{2,1,0:T(8,128)}, ...) | async-done | bytes 917520 | tf_op jit(solution)/shard_map/psum | solution.py:87
  129.0 4.5 %fusion.96 = (f32[256]{0:T(256)S(1)}, f32[256,8192]{1,0:T(8,128)}) fusion(bf16[256,128]{1,0:T(8,128)(2,1)S(1)} %squeeze.46, bf16[1,8192,128]{2,1,0:T(8,128)(2,1)S(1)} %copy-done.2, pred[8192]{0:T(1024)(128)(4,1)S(1)} %iota_compare_fusion), kind=kOutput, calls=%fused_computation.196 | convolution fusion | flops 543162112 | bytes 10560512 | tf_op jit(solution)/shard_map/while/body/eval_jaxpr/fd,cd->fc/dot_general | solution.py:33
  133.8 4.5 %fusion.98 = (f32[256]{0:T(256)S(1)}, f32[256,8192]{1,0:T(8,128)}) fusion(bf16[256,128]{1,0:T(8,128)(2,1)S(1)} %squeeze.45, bf16[1,8192,128]{2,1,0:T(8,128)(2,1)S(1)} %copy-done.2, pred[8192]{0:T(1024)(128)(4,1)S(1)} %iota_compare_fusion), kind=kOutput, calls=%fused_computation.198 | convolution fusion | flops 543162112 | bytes 10560512 | tf_op jit(solution)/shard_map/while/body/eval_jaxpr/fd,cd->fc/dot_general | solution.py:33
  138.8 4.5 %fusion.94 = (f32[256]{0:T(256)S(1)}, f32[256,8192]{1,0:T(8,128)}) fusion(bf16[256,128]{1,0:T(8,128)(2,1)S(1)} %squeeze.47, bf16[1,8192,128]{2,1,0:T(8,128)(2,1)S(1)} %copy-done.2, pred[8192]{0:T(1024)(128)(4,1)S(1)} %iota_compare_fusion), kind=kOutput, calls=%fused_computation.194 | convolution fusion | flops 543162112 | bytes 10560512 | tf_op jit(solution)/shard_map/while/body/eval_jaxpr/fd,cd->fc/dot_general | solution.py:33
  143.9 35.5 %while.3 = (s32[]{:T(128)}, f32[2,512]{1,0:T(2,128)S(1)}, f32[2,512]{1,0:T(2,128)S(1)}, f32[2,512,128]{2,1,0:T(8,128)}, bf16[2,512,128]{2,1,0:T(8,128)(2,1)S(1)}...) while((s32[]{:T(128)}, f32[2,512]{1,0:T(2,128)S(1)}, ...), condition=%wide.region_9.10_spmd.clone, body=%wide.region_4.9_spmd.clone.sunk | while | flops 2192774144 | bytes 60042448 | solution.py:52
  144.9 2.7 fusion.145
  147.6 6.6 %convert_reduce_fusion.10 = (f32[512]{0:T(512)S(1)}, bf16[512,8192]{1,0:T(8,128)(2,1)}) fusion(f32[512]{0:T(512)S(1)} %max.55, f32[512,8192]{1,0:T(8,128)S(1)} %get-tuple-element.411, pred[8192]{0:T(1024)(128)(4,1)S(1)} %compare_reduce_fusion.2), kind=kLoop, calls=%fused_computation.1.clone.1 | loop fusion | flops 25165312 | bytes 25178112 | tf_op jit(solution)/shard_map/while/body/eval_jaxpr/reduce_sum | solution.py:45
  154.3 6.4 %fusion.147 = f32[512,128]{1,0:T(8,128)S(1)} fusion(bf16[512,8192]{1,0:T(8,128)(2,1)} %get-tuple-element.414, bf16[8192,128]{1,0:T(8,128)(2,1)} %get-tuple-element.449), kind=kOutput, calls=%fused_computation.200.clone.1 | convolution fusion | flops 1073741824 | bytes 10747904 | tf_op jit(solution)/shard_map/while/body/eval_jaxpr/dot_general | solution.py:48
  162.6 2.7 fusion.145
  165.3 6.6 %convert_reduce_fusion.10 = (f32[512]{0:T(512)S(1)}, bf16[512,8192]{1,0:T(8,128)(2,1)}) fusion(f32[512]{0:T(512)S(1)} %max.55, f32[512,8192]{1,0:T(8,128)S(1)} %get-tuple-element.411, pred[8192]{0:T(1024)(128)(4,1)S(1)} %compare_reduce_fusion.2), kind=kLoop, calls=%fused_computation.1.clone.1 | loop fusion | flops 25165312 | bytes 25178112 | tf_op jit(solution)/shard_map/while/body/eval_jaxpr/reduce_sum | solution.py:45
  172.0 6.4 %fusion.147 = f32[512,128]{1,0:T(8,128)S(1)} fusion(bf16[512,8192]{1,0:T(8,128)(2,1)} %get-tuple-element.414, bf16[8192,128]{1,0:T(8,128)(2,1)} %get-tuple-element.449), kind=kOutput, calls=%fused_computation.200.clone.1 | convolution fusion | flops 1073741824 | bytes 10747904 | tf_op jit(solution)/shard_map/while/body/eval_jaxpr/dot_general | solution.py:48
  179.4 7.5 %convert_reduce_fusion.3 = (f32[256]{0:T(256)S(1)}, bf16[256,8192]{1,0:T(8,128)(2,1)}) fusion(f32[256,8192]{1,0:T(8,128)} %get-tuple-element.321, f32[256]{0:T(256)S(1)} %max.50), kind=kLoop, calls=%fused_computation.28 | loop fusion | flops 8388352 | bytes 12584960 | tf_op jit(solution)/shard_map/while/body/eval_jaxpr/reduce_sum | solution.py:45
  186.9 3.9 %convert_reduce_fusion.4 = (f32[256]{0:T(256)S(1)}, bf16[256,8192]{1,0:T(8,128)(2,1)}) fusion(f32[256,8192]{1,0:T(8,128)S(1)} %copy-done.3, f32[256]{0:T(256)S(1)} %max.49), kind=kLoop, calls=%fused_computation.30 | loop fusion | flops 8388352 | bytes 12584960 | tf_op jit(solution)/shard_map/while/body/eval_jaxpr/reduce_sum | solution.py:45
  190.8 3.8 %convert_reduce_fusion.2 = (f32[256]{0:T(256)S(1)}, bf16[256,8192]{1,0:T(8,128)(2,1)}) fusion(f32[256,8192]{1,0:T(8,128)S(1)} %bitcast.201, f32[256]{0:T(256)S(1)} %max.51), kind=kLoop, calls=%fused_computation.26 | loop fusion | flops 8388352 | bytes 12584960 | tf_op jit(solution)/shard_map/while/body/eval_jaxpr/reduce_sum | solution.py:45
  194.6 12.0 %all-reduce.8 = (f32[1024]{0:T(1024)S(1)}, f32[256]{0:T(256)S(1)}, f32[256]{0:T(256)S(1)}, f32[256]{0:T(256)S(1)}) all-reduce(f32[1024]{0:T(1024)S(1)} %bitcast.209, f32[256]{0:T(256)S(1)} %max.51, f32[256]{0:T(256)S(1)} %max.50, f32[256]{0:T(256)S(1)} %max.49), channel_id=1, replica_groups=mesh['ctx'=8,'kv'=4] {'ctx'}, use_global_device_ids=true, to_apply=%region_10.11 | all-reduce | flops 1792 | bytes 14336 | tf_op jit(solution)/shard_map/pmax | solution.py:123
  207.6 4.5 %fusion.20 = bf16[256,128]{1,0:T(8,128)(2,1)} fusion(f32[256,128]{1,0:T(8,128)S(1)} %fusion.65, bf16[256,8192]{1,0:T(8,128)(2,1)} %get-tuple-element.285, f32[256]{0:T(256)S(1)} %get-tuple-element.283, bf16[1,8192,128]{2,1,0:T(8,128)(2,1)S(1)} %bitcast.203), kind=kOutput, calls=%fused_computation.44 | convolution fusion | flops 536969216 | bytes 6489088 | tf_op jit(solution)/shard_map/while/body/eval_jaxpr/dot_general | solution.py:48
  212.1 1.9 fusion.21
  214.3 1.9 fusion.22
  216.2 11.8 %all-reduce.9 = (bf16[1024]{0:T(1024)(128)(2,1)S(1)}, bf16[256]{0:T(256)(128)(2,1)S(1)}, bf16[256]{0:T(256)(128)(2,1)S(1)}, bf16[256]{0:T(256)(128)(2,1)S(1)}) all-reduce(bf16[1024]{0:T(1024)(128)(2,1)S(1)} %get-tuple-element.294, bf16[256]{0:T(256)(128)(2,1)S(1)} %get-tuple-element.290, ...), channel_id=1, replica_groups=mesh['ctx'=8,'kv'=4] {'ctx'}, use_global_device_ids=true, to_apply=%region_12.13 | all-reduce | flops 1792 | bytes 7168 | tf_op jit(solution)/shard_map/psum | solution.py:126
  228.1 42.4 %all-reduce.20.cloned.1.call-done = (bf16[1024,128]{1,0:T(8,128)(2,1)}, bf16[256,128]{1,0:T(8,128)(2,1)}, bf16[256,128]{1,0:T(8,128)(2,1)}, bf16[256,128]{1,0:T(8,128)(2,1)}) async-done(((bf16[1024,128]{1,0:T(8,128)(2,1)}, bf16[256,128]{1,0:T(8,128)(2,1)}, bf16[256,128]{1,0:T(8,128)(2,1)}, bf16[256,128]{1,0:T(8,128)(2,1)}), (bf16[1024,128]{1,0:T(8,128)(2,1)}, bf16[256,128]{1,0:T(8,128)(2,1)}, ...) | async-done | bytes 458768 | tf_op jit(solution)/shard_map/psum | solution.py:127
  272.8 2.8 fusion.25
  277.7 2.7 fusion.24
  280.4 2.7 fusion.23
  283.2 2.7 fusion.16
  286.0 8.2 %reduce-scatter.14.cloned.1.call-done = bf16[8,1,1024]{2,0,1:T(8,128)(2,1)} async-done(((bf16[32,1,1024]{2,0,1:T(8,128)(2,1)}), bf16[8,1,1024]{2,0,1:T(8,128)(2,1)}) %reduce-scatter.14.cloned.1.call-update) | async-done | bytes 16400 | tf_op jit(solution)/shard_map/reduce_scatter | solution.py:131
  294.2 19.2 %reduce-scatter.12.cloned.1.call-done = bf16[8,1,1024]{2,0,1:T(8,128)(2,1)} async-done(((bf16[32,1,1024]{2,0,1:T(8,128)(2,1)}), bf16[8,1,1024]{2,0,1:T(8,128)(2,1)}) %reduce-scatter.12.cloned.1.call-update) | async-done | bytes 16400 | tf_op jit(solution)/shard_map/reduce_scatter | solution.py:131
  313.4 19.4 %reduce-scatter.10.cloned.1.call-done = bf16[8,1,1024]{2,0,1:T(8,128)(2,1)} async-done(((bf16[32,1,1024]{2,0,1:T(8,128)(2,1)}), bf16[8,1,1024]{2,0,1:T(8,128)(2,1)}) %reduce-scatter.10.cloned.1.call-update) | async-done | bytes 16400 | tf_op jit(solution)/shard_map/reduce_scatter | solution.py:131
  334.2 19.3 %reduce-scatter.8.cloned.1.call-done = bf16[32,1,1024]{2,0,1:T(8,128)(2,1)} async-done(((bf16[128,1,1024]{2,0,1:T(8,128)(2,1)}), bf16[32,1,1024]{2,0,1:T(8,128)(2,1)}) %reduce-scatter.8.cloned.1.call-update) | async-done | bytes 65552 | tf_op jit(solution)/shard_map/reduce_scatter | solution.py:131
  (168 shorter events, 26.7 us)
Async XLA Ops:
  7.2 5.1 %copy-start = (bf16[1024,1024]{1,0:T(8,128)(2,1)S(1)}, bf16[1024,1024]{1,0:T(8,128)(2,1)}, u32[]{:S(2)}) copy-start(bf16[1024,1024]{1,0:T(8,128)(2,1)} %param.16) | copy-start | bytes 6291460
  7.2 8.2 %copy-start.7 = (bf16[128,1024]{1,0:T(8,128)(2,1)S(1)}, bf16[128,1024]{1,0:T(8,128)(2,1)}, u32[]{:S(2)}) copy-start(bf16[128,1024]{1,0:T(8,128)(2,1)} %param.13) | copy-start | bytes 786436
  7.2 7.1 %copy-start.8 = (bf16[3,32,1024]{2,1,0:T(8,128)(2,1)S(1)}, bf16[3,32,1024]{2,1,0:T(8,128)(2,1)}, u32[]{:S(2)}) copy-start(bf16[3,32,1024]{2,1,0:T(8,128)(2,1)} %param.14) | copy-start | bytes 589828
  7.2 60.9 %all-reduce.16.cloned.1.call-start = ((), (), s32[]{:S(2)}) async-start(), calls=%async_computation.8 | async-start | bytes 262144
  12.3 115.4 %all-reduce.18.cloned.1.call-start = ((), (), s32[]{:S(2)}) async-start(), calls=%async_computation.9 | async-start | bytes 1835008 | tf_op jit(solution)/shard_map/psum | solution.py:87
  15.4 19.4 %copy-start.14 = (s32[32]{0:T(128)S(1)}, s32[32]{0:T(128)}, u32[]{:S(2)}) copy-start(s32[32]{0:T(128)} %param.23) | copy-start | bytes 388
  15.4 19.7 %copy-start.15 = (u32[32]{0:T(128)S(1)}, u32[32]{0:T(128)}, u32[]{:S(2)}) copy-start(u32[32]{0:T(128)} %constant.161) | copy-start | bytes 388
  17.8 111.1 %copy-start.2 = (bf16[1,8192,128]{2,1,0:T(8,128)(2,1)S(1)}, bf16[1,8192,128]{2,1,0:T(8,128)(2,1)}, u32[]{:S(2)}) copy-start(bf16[1,8192,128]{2,1,0:T(8,128)(2,1)} %param.20) | copy-start | bytes 6291460
  17.9 252.7 %all-reduce.20.cloned.1.call-start = ((), (), s32[]{:S(2)}) async-start(), calls=%async_computation.10 | async-start | bytes 917504 | tf_op jit(solution)/shard_map/psum | solution.py:127
  129.0 4.7 %copy-start.13 = (f32[1,32,1024]{2,1,0:T(8,128)S(1)}, f32[1,32,1024]{2,1,0:T(8,128)}, u32[]{:S(2)}) copy-start(f32[1,32,1024]{2,1,0:T(8,128)} %get-tuple-element.264) | copy-start | bytes 393220
  138.8 4.9 %copy-start.12 = (f32[1,128,1024]{2,1,0:T(8,128)S(1)}, f32[1,128,1024]{2,1,0:T(8,128)}, u32[]{:S(2)}) copy-start(f32[1,128,1024]{2,1,0:T(8,128)} %get-tuple-element.261) | copy-start | bytes 1572868
  154.3 6.4 %copy-start.9 = (f32[2,512,128]{2,1,0:T(8,128)S(1)}, f32[2,512,128]{2,1,0:T(8,128)}, u32[]{:S(2)}) copy-start(f32[2,512,128]{2,1,0:T(8,128)} %get-tuple-element.431) | copy-start | bytes 1572868 | tf_op jit(solution)/shard_map/while
  160.9 0.8 copy-start.10
  172.0 6.4 %copy-start.9 = (f32[2,512,128]{2,1,0:T(8,128)S(1)}, f32[2,512,128]{2,1,0:T(8,128)}, u32[]{:S(2)}) copy-start(f32[2,512,128]{2,1,0:T(8,128)} %get-tuple-element.431) | copy-start | bytes 1572868 | tf_op jit(solution)/shard_map/while
  178.6 0.8 copy-start.10
  179.4 7.5 %copy-start.3 = (f32[256,8192]{1,0:T(8,128)S(1)}, f32[256,8192]{1,0:T(8,128)}, u32[]{:S(2)}) copy-start(f32[256,8192]{1,0:T(8,128)} %get-tuple-element.325) | copy-start | bytes 25165828
  179.4 11.4 %slice-start = ((s8[8388608]{0:T(1024)(128)(4,1)}), s8[4194304]{0:T(1024)(128)(4,1)S(1)}, s32[]{:S(2)}) async-start(s8[8388608]{0:T(1024)(128)(4,1)} %bitcast.200), calls=%async_computation.11 | async-start | bytes 8388608
  186.9 3.9 %slice-start.1 = ((s8[8388608]{0:T(1024)(128)(4,1)}), s8[4194304]{0:T(1024)(128)(4,1)S(1)}, s32[]{:S(2)}) async-start(s8[8388608]{0:T(1024)(128)(4,1)} %bitcast.200), calls=%async_computation.12 | async-start | bytes 8388608
  190.8 15.9 %copy-start.11 = (f32[2,512,128]{2,1,0:T(8,128)S(1)}, f32[2,512,128]{2,1,0:T(8,128)}, u32[]{:S(2)}) copy-start(f32[2,512,128]{2,1,0:T(8,128)} %get-tuple-element.138) | copy-start | bytes 1572868
  190.8 16.8 %copy-start.4 = (bf16[8192,128]{1,0:T(8,128)(2,1)S(1)}, bf16[8192,128]{1,0:T(8,128)(2,1)}, u32[]{:S(2)}) copy-start(bf16[8192,128]{1,0:T(8,128)(2,1)} %get-tuple-element.475) | copy-start | bytes 6291460
  206.7 5.4 %copy-start.6 = (bf16[256,8192]{1,0:T(8,128)(2,1)S(1)}, bf16[256,8192]{1,0:T(8,128)(2,1)}, u32[]{:S(2)}) copy-start(bf16[256,8192]{1,0:T(8,128)(2,1)} %get-tuple-element.289) | copy-start | bytes 12582916
  212.1 2.2 copy-start.5
  216.2 78.0 %reduce-scatter.14.cloned.1.call-start = ((), (), s32[]{:S(2)}) async-start(), calls=%async_computation.7 | async-start | bytes 81920 | tf_op jit(solution)/shard_map/reduce_scatter | solution.py:131
  272.8 80.7 %copy-start.1 = (bf16[1024,1024]{1,0:T(8,128)(2,1)S(1)}, bf16[1024,1024]{1,0:T(8,128)(2,1)}, u32[]{:S(2)}) copy-start(bf16[1024,1024]{1,0:T(8,128)(2,1)} %param.16) | copy-start | bytes 6291460
  275.7 37.7 %reduce-scatter.12.cloned.1.call-start = ((), (), s32[]{:S(2)}) async-start(), calls=%async_computation.6 | async-start | bytes 81920 | tf_op jit(solution)/shard_map/reduce_scatter | solution.py:131
  280.4 52.4 %reduce-scatter.10.cloned.1.call-start = ((), (), s32[]{:S(2)}) async-start(), calls=%async_computation.5 | async-start | bytes 81920 | tf_op jit(solution)/shard_map/reduce_scatter | solution.py:131
  283.2 70.4 %reduce-scatter.8.cloned.1.call-start = ((), (), s32[]{:S(2)}) async-start(), calls=%async_computation.4 | async-start | bytes 327680 | tf_op jit(solution)/shard_map/reduce_scatter | solution.py:131
Sparse Core Ops, SparseCore 0:
  12.4 55.6 all-reduce.15
  71.9 55.6 all-reduce.17
  216.3 54.1 all-reduce.19
  275.8 18.3 reduce-scatter.13
  296.2 17.0 reduce-scatter.11
  315.5 17.2 reduce-scatter.9
  335.6 17.8 reduce-scatter.7
where the time goes:
time: 361 us; the launch traced here: 360 us
  waiting for transfers between devices  174 us (48%)
  blocking collectives  61.9 us (17%)
  matrix products  60 us (17%)
  other arithmetic  39.5 us (11%)
  between operations  16.5 us (5%)
  local copies, waits for them, and re-layouts  7.83 us (2%)
    reduce_scatter x4, waiting for transfers between devices, run_section(): lax.psum_scatter(jnp.einsum('srk,kd->rsd', attended, out_weight, preferre...  66.2 us
    psum x1, waiting for transfers between devices, run_section(): query_sum, square_sum = lax.psum((query_part, squares), 'ctx')  58.8 us
    psum x1, waiting for transfers between devices, run_section(): lax.psum((mixture * rescale[:, None]).astype(jnp.bfloat16), 'ctx')  42.4 us
    reduce_sum x5, other arithmetic, one_block(): jnp.sum(cache_weights, axis=1, dtype=jnp.float32)  28.4 us
    unnamed x1, blocking collectives  22.9 us
    dot_general x5, matrix products, one_block(): jnp.dot(cache_weights, value_shard, preferred_element_type=jnp.float32)  21 us
    dot_general x5, matrix products, one_block(): jnp.einsum('fd,cd->fc', query_block, key_shard, preferred_element_type=jn...  18.8 us
    psum x1, blocking collectives, run_section(): query_sum, square_sum = lax.psum((query_part, squares), 'ctx')  15.1 us
  transfers between devices with their start and end apart: 7, of which 7 were waited for; matrix products, arithmetic and copies ran while one was open for 6% of the time, Pallas kernels for 0%

commit v1 on v0

v1 whole, which is shorter than its diff:
```python
import functools

import jax
import jax.numpy as jnp
from jax import lax
from jax.experimental import pallas as pl
from jax.experimental.pallas import tpu as pltpu
from jax.sharding import PartitionSpec as P

HD = 128
EPSILON = 1e-05
MASKED = -1e30
LOG2E = 1.4426950408889634
STAT_ROWS = 16
AT_ONCE = 3
VMEM_BYTES = 50 * 2**20
BF16 = jnp.bfloat16
F32 = jnp.float32


def up(count, multiple):
    return -(-count // multiple) * multiple


def split3(x):
    high = x.astype(BF16).astype(F32)
    rest = x - high
    middle = rest.astype(BF16).astype(F32)
    return high, middle, rest - middle


def column_to_rows(column):
    count = column.shape[0]
    rows = []
    for start in range(0, count, 128):
        size = min(128, count - start)
        part = jnp.broadcast_to(column[start : start + size], (size, 128))
        on = lax.broadcasted_iota(jnp.int32, (size, 128), 0) == lax.broadcasted_iota(
            jnp.int32, (size, 128), 1
        )
        rows.append(jnp.sum(jnp.where(on, part, 0.0), axis=0, keepdims=True))
    return jnp.concatenate(rows, axis=0)


def rows_to_column(rows, index):
    total = 0.0
    for k in range(rows.shape[0]):
        lanes = lax.broadcasted_iota(jnp.int32, (index.shape[0], 128), 1) + 128 * k
        total = total + jnp.sum(
            jnp.where(lanes == index, rows[k : k + 1, :], 0.0), axis=1, keepdims=True
        )
    return total


def stack_stats(rows_list):
    parts = []
    for rows in rows_list:
        parts.extend(split3(rows))
    used = sum(part.shape[0] for part in parts)
    parts.append(jnp.zeros((STAT_ROWS - used, 128), F32))
    return jnp.concatenate(parts, axis=0)


def read_stats(block, count, kinds):
    out = []
    for kind in range(kinds):
        base = kind * 3 * count
        out.append(
            block[base : base + count]
            + block[base + count : base + 2 * count]
            + block[base + 2 * count : base + 3 * count]
        )
    return out


def call(kernel, out_shape, args, name, flops, smem=0, grant=VMEM_BYTES, scratch=()):
    whole = pl.BlockSpec(memory_space=pltpu.VMEM)
    scalar = pl.BlockSpec(memory_space=pltpu.SMEM)
    return pl.pallas_call(
        kernel,
        out_shape=out_shape,
        in_specs=[scalar] * smem + [whole] * (len(args) - smem),
        out_specs=jax.tree.map(lambda _: whole, out_shape),
        scratch_shapes=list(scratch),
        compiler_params=pltpu.CompilerParams(vmem_limit_bytes=grant),
        cost_estimate=pl.CostEstimate(
            flops=int(flops), bytes_accessed=1 << 20, transcendentals=0
        ),
        name=name,
    )(*args)


def shape(rows, columns, dtype, *lead):
    return jax.ShapeDtypeStruct(tuple(lead) + (rows, columns), dtype)


class Sizes:
    def __init__(self, prompt_in, step_in, query_weight, visible, devices, groups):
        self.n = devices
        self.groups = groups
        self.prompt = prompt_in.shape[0]
        self.steps = step_in.shape[0]
        self.row_total = visible.shape[0]
        self.rows = self.prompt + self.steps * self.row_total
        self.width = prompt_in.shape[1]
        self.heads = query_weight.shape[1] // HD
        self.halves = devices // self.heads
        self.piece = self.rows // self.halves
        self.stat_lines = up(self.piece, 128) // 128
        self.square_lines = up(self.rows, 128) // 128
        self.prompt_own = self.prompt // devices
        self.rows_own = self.row_total // devices
        self.decode_own = self.rows_own * self.steps
        self.decode_slots = up(self.decode_own, 16)
        self.prompt_slots = up(self.prompt_own, 16)
        self.slots = self.prompt_slots + self.decode_slots
        self.message = self.piece + STAT_ROWS
        self.project = self.piece + 2 * self.slots + STAT_ROWS


def project_kernel(z, me_ref, xp_ref, xs_ref, gain_ref, wq_ref, wk_ref, wv_ref, even_ref, odd_ref, scaled_ref, kvp_ref, kvd_ref):
    me = me_ref[0]
    gain = gain_ref[...].astype(F32)
    squares = []
    for ref, base, size in (
        (xp_ref, 0, z.prompt),
        (xs_ref, z.prompt, z.steps * z.row_total),
    ):
        wide = ref[...].astype(F32)
        squares.append(jnp.sum(wide * wide, axis=1, keepdims=True))
        scaled_ref[base : base + size, :] = (wide * gain).astype(BF16)
    square_rows = column_to_rows(jnp.concatenate(squares, axis=0))
    pad = jnp.zeros((STAT_ROWS - z.square_lines, 128), F32)
    stats_plain = jnp.concatenate([square_rows, pad], axis=0)
    stats_split = stack_stats([square_rows])
    decode = z.steps * z.row_total
    count = z.n * z.decode_slots
    place = lax.broadcasted_iota(jnp.int32, (count, decode), 0)
    source = lax.broadcasted_iota(jnp.int32, (count, decode), 1)
    slot = place % z.decode_slots
    wanted = (
        (slot // z.rows_own) * z.row_total
        + (place // z.decode_slots) * z.rows_own
        + slot % z.rows_own
    )
    pick = ((wanted == source) & (slot < z.decode_own)).astype(F32).astype(BF16)
    ordered = jnp.dot(
        pick, scaled_ref[z.prompt : z.rows, :], preferred_element_type=F32
    ).astype(BF16)
    for c, ref in enumerate((wk_ref, wv_ref)):
        kvp_ref[:, c * HD : (c + 1) * HD] = jnp.dot(
            scaled_ref[0 : z.prompt, :], ref[...], preferred_element_type=F32
        )
        kvd_ref[:, c * HD : (c + 1) * HD] = jnp.dot(ordered, ref[...], preferred_element_type=F32)
    for d in range(z.n):
        owner = jnp.bitwise_xor(me, d)
        head = owner % z.heads
        half = owner // z.heads
        rows = scaled_ref[pl.ds(pl.multiple_of(half * z.piece, 16), z.piece), :]
        part = jnp.dot(
            rows,
            wq_ref[:, pl.ds(pl.multiple_of(head * HD, HD), HD)],
            preferred_element_type=F32,
        )
        kvp = kvp_ref[pl.ds(pl.multiple_of(owner * z.prompt_own, 8), z.prompt_own), :]
        kvd = kvd_ref[pl.ds(pl.multiple_of(owner * z.decode_slots, 8), z.decode_slots), :]
        ref = odd_ref if d % 2 else even_ref
        stats = stats_split if d % 2 else stats_plain
        everything = jnp.concatenate(
            [part, kvp[:, :HD], kvd[:, :HD], kvp[:, HD:], kvd[:, HD:], stats], axis=0
        )
        ref[d // 2] = everything.astype(ref.dtype)


def pair_sum_kernel(z, even_ref, got_ref, own_ref, *send_refs):
    body = z.project - STAT_ROWS
    for i in range(z.n // 2):
        got = got_ref[i].astype(F32)
        total = even_ref[i, 0:body, :] + got[0:body]
        squares = (
            even_ref[i, body : body + z.square_lines, :]
            + read_stats(got[body:], z.square_lines, 1)[0]
        )
        if i == 0:
            pad = jnp.zeros((STAT_ROWS - z.square_lines, 128), F32)
            own_ref[...] = jnp.concatenate([total, squares, pad], axis=0)
        else:
            send_refs[i - 1][...] = jnp.concatenate(
                [total, stack_stats([squares])], axis=0
            ).astype(BF16)


def finish_kernel(z, features, me_ref, own_ref, *refs):
    got_refs = refs[: z.n // 2 - 1]
    query_ref, key_ref, value_ref = refs[z.n // 2 - 1 :]
    me = me_ref[0]
    body = z.project - STAT_ROWS
    total = own_ref[0:body, :]
    squares = own_ref[body : body + z.square_lines, :]
    for ref in got_refs:
        got = ref[...].astype(F32)
        total = total + got[0:body]
        squares = squares + read_stats(got[body:], z.square_lines, 1)[0]
    inverse = lax.rsqrt(squares / features + EPSILON)
    rows = lax.broadcasted_iota(jnp.int32, (z.piece, 1), 0) + (me // z.heads) * z.piece
    factor = HD ** (-0.5) * LOG2E
    query_ref[...] = (total[0 : z.piece] * (rows_to_column(inverse, rows) * factor)).astype(BF16)
    slot = lax.broadcasted_iota(jnp.int32, (z.slots, 1), 0)
    late = slot - z.prompt_slots
    index = jnp.where(
        slot < z.prompt_slots,
        me * z.prompt_own + slot,
        z.prompt
        + (late // z.rows_own) * z.row_total
        + me * z.rows_own
        + late % z.rows_own,
    )
    own = rows_to_column(inverse, index)
    key_ref[...] = (total[z.piece : z.piece + z.slots] * own).astype(BF16)
    value_ref[...] = (total[z.piece + z.slots : z.piece + 2 * z.slots] * own).astype(BF16)


def attention_kernel(z, pieces, stacked, chunk, me_ref, *refs):
    key_ref, value_ref, bias_ref, extra_key_ref, extra_value_ref, extra_bias_ref = refs[:6]
    query_refs = refs[6 : 6 + len(pieces)]
    out_refs = refs[6 + len(pieces) :]
    me = me_ref[0]
    over = (((1,), (1,)), ((), ()))
    for i, d in enumerate(pieces):
        query = query_refs[i][...]
        half = jnp.bitwise_xor(me, d) // z.heads
        extra_bias = extra_bias_ref[pl.ds(pl.multiple_of(half * z.piece, 8), z.piece), :]
        found = []
        blocks = [
            (key_ref, value_ref, start, chunk) for start in range(0, key_ref.shape[0], chunk)
        ]
        blocks.append((extra_key_ref, extra_value_ref, 0, z.slots))
        for keys, values, start, size in blocks:
            score = lax.dot_general(
                query, keys[start : start + size, :], over, preferred_element_type=F32
            )
            if keys is key_ref:
                score = score + bias_ref[:, start : start + size]
            else:
                score = score + extra_bias
            top = jnp.max(score, axis=1, keepdims=True)
            weight = jnp.exp2(score - top)
            total = jnp.sum(weight, axis=1, keepdims=True)
            mixed = jnp.dot(
                weight.astype(BF16), values[start : start + size, :], preferred_element_type=F32
            )
            found.append((top, total, mixed))
        highest = functools.reduce(jnp.maximum, [top for top, _, _ in found])
        total = 0.0
        mixed = 0.0
        for top, block_total, block_mixed in found:
            scale = jnp.exp2(top - highest)
            total = total + block_total * scale
            mixed = mixed + block_mixed * scale
        stats = stack_stats([column_to_rows(highest), column_to_rows(total)])
        message = jnp.concatenate([mixed, stats], axis=0).astype(BF16)
        if stacked:
            out_refs[0][i] = message
        else:
            out_refs[i][...] = message


def merge(z, messages):
    blocks = []
    for message in messages:
        wide = message.astype(F32)
        top, total = read_stats(wide[z.piece :], z.stat_lines, 2)
        blocks.append((top, total, wide[0 : z.piece]))
    highest = functools.reduce(jnp.maximum, [top for top, _, _ in blocks])
    index = lax.broadcasted_iota(jnp.int32, (z.piece, 1), 0)
    total = 0.0
    mixed = 0.0
    for top, block_total, block_mixed in blocks:
        scale = jnp.exp2(top - highest)
        total = total + block_total * scale
        mixed = mixed + block_mixed * rows_to_column(scale, index)
    return highest, total, mixed


def pair_merge_kernel(z, sets, first_ref, got_first_ref, *refs):
    mine_refs = refs[: len(sets)]
    got_refs = refs[len(sets) : 2 * len(sets)]
    own_ref, *send_refs = refs[2 * len(sets) :]
    places = [(s, k) for s, size in enumerate(sets) for k in range(size)]
    for i in range(z.n // 2):
        if i == 0:
            mine, theirs = first_ref[...], got_first_ref[...]
        else:
            s, k = places[i - 1]
            mine, theirs = mine_refs[s][k], got_refs[s][k]
        highest, total, mixed = merge(z, [mine, theirs])
        message = jnp.concatenate([mixed, stack_stats([highest, total])], axis=0).astype(BF16)
        if i == 0:
            own_ref[...] = message
        else:
            send_refs[i - 1][...] = message


def final_merge_kernel(z, *refs):
    out_ref = refs[-1]
    _, total, mixed = merge(z, [ref[...] for ref in refs[:-1]])
    index = lax.broadcasted_iota(jnp.int32, (z.piece, 1), 0)
    out_ref[...] = (mixed / rows_to_column(total, index)).astype(BF16)


def output_kernel(z, me_ref, weight_ref, *refs):
    piece_refs = refs[: z.n]
    out_refs = refs[z.n : z.n + z.groups]
    sum_ref = refs[-1]
    me = me_ref[0]
    place = me_ref[1]
    columns = weight_ref.shape[1]
    if z.halves > 1:
        sum_ref[...] = jnp.zeros_like(sum_ref)
    total = None
    for d in range(z.n):
        owner = jnp.bitwise_xor(me, d)
        head = owner % z.heads
        product = jnp.dot(
            piece_refs[d][...],
            weight_ref[pl.ds(pl.multiple_of(head * HD, HD), HD), :],
            preferred_element_type=F32,
        )
        if z.halves == 1:
            total = product if total is None else total + product
        else:
            where = pl.ds(pl.multiple_of((owner // z.heads) * z.piece, 8), z.piece)
            sum_ref[where, :] = sum_ref[where, :] + product
    if z.halves == 1:
        sum_ref[...] = total
    prompt_share = z.prompt // z.groups
    step_share = z.row_total // z.groups
    for e in range(z.groups):
        target = jnp.bitwise_xor(place, e)
        rows = [sum_ref[pl.ds(pl.multiple_of(target * prompt_share, 8), prompt_share), :]]
        for s in range(z.steps):
            start = z.prompt + s * z.row_total + target * step_share
            rows.append(sum_ref[pl.ds(pl.multiple_of(start, 8), step_share), :])
        share = jnp.concatenate(rows, axis=0)
        out_refs[e][...] = jnp.concatenate(
            [share[:, : columns // 2], share[:, columns // 2 :]], axis=0
        ).astype(BF16)


def share_sum_kernel(z, *refs):
    prompt_ref, step_ref = refs[z.groups :]
    total = refs[0][...].astype(F32)
    for ref in refs[1 : z.groups]:
        total = total + ref[...].astype(F32)
    prompt_share = z.prompt // z.groups
    step_share = z.row_total // z.groups
    half = total.shape[0] // 2
    columns = total.shape[1]
    for c in range(2):
        rows = total[c * half : (c + 1) * half]
        where = slice(c * columns, (c + 1) * columns)
        prompt_ref[:, where] = rows[0:prompt_share].astype(BF16)
        for s in range(z.steps):
            start = prompt_share + s * step_share
            step_ref[s, :, where] = rows[start : start + step_share].astype(BF16)


def swap(x, axis, size, d):
    return lax.ppermute(x, axis, [(i, i ^ d) for i in range(size)])


def on_device(
    prompt_in,
    step_in,
    norm_gain,
    query_weight,
    key_weight,
    value_weight,
    out_weight,
    key_cache,
    value_cache,
    cache_lengths,
    visible,
):
    n = lax.axis_size("ctx")
    groups = lax.axis_size("kv")
    z = Sizes(prompt_in, step_in, query_weight, visible, n, groups)
    me = lax.axis_index("ctx").astype(jnp.int32)
    place = lax.axis_index("kv").astype(jnp.int32)
    where = jnp.stack([me, place])
    pairs = n // 2

    row = jnp.arange(z.rows, dtype=jnp.int32)
    is_prompt = row < z.prompt
    late = jnp.maximum(row - z.prompt, 0)
    limit = jnp.where(is_prompt, row + 1, visible[late % z.row_total])
    slot = jnp.arange(z.slots, dtype=jnp.int32)
    late_slot = jnp.maximum(slot - z.prompt_slots, 0)
    seen_prompt = (slot < z.prompt_own) & ((me * z.prompt_own + slot) < limit[:, None])
    seen_own = (
        (slot >= z.prompt_slots)
        & (late_slot < z.decode_own)
        & ~is_prompt[:, None]
        & ((me * z.rows_own + late_slot % z.rows_own) == (late % z.row_total)[:, None])
        & ((late_slot // z.rows_own) <= (late // z.row_total)[:, None])
    )
    extra_bias = jnp.where(seen_prompt | seen_own, 0.0, MASKED).astype(F32)
    cache_slots = key_cache.shape[1]
    live = lax.broadcasted_iota(jnp.int32, (1, cache_slots), 1) < cache_lengths[0]
    bias = jnp.where(live, 0.0, MASKED).astype(F32)

    even, odd = call(
        functools.partial(project_kernel, z),
        [shape(z.project, HD, F32, pairs), shape(z.project, HD, BF16, pairs)],
        (
            where,
            prompt_in,
            step_in.reshape(z.steps * z.row_total, z.width),
            norm_gain.reshape(1, z.width),
            query_weight,
            key_weight,
            value_weight,
        ),
        "project",
        2 * z.rows * z.width * (z.heads + 2) * HD,
        smem=1,
        scratch=[
            pltpu.VMEM((z.rows, z.width), BF16),
            pltpu.VMEM((z.prompt, 2 * HD), F32),
            pltpu.VMEM((z.n * z.decode_slots, 2 * HD), F32),
        ],
    )
    got = swap(odd, "ctx", n, 1)
    own, *sends = call(
        functools.partial(pair_sum_kernel, z),
        [shape(z.project, HD, F32)] + [shape(z.project, HD, BF16)] * (pairs - 1),
        (even, got),
        "pair_sum",
        1e6,
    )
    gots = [swap(send, "ctx", n, 2 * (i + 1)) for i, send in enumerate(sends)]
    query, extra_key, extra_value = call(
        functools.partial(finish_kernel, z, z.width * n),
        [shape(z.piece, HD, BF16), shape(z.slots, HD, BF16), shape(z.slots, HD, BF16)],
        (where, own, *gots),
        "finish",
        1e6,
        smem=1,
    )

    queries = {0: query}
    for i in range(1, pairs):
        queries[2 * i] = swap(query, "ctx", n, 2 * i)
    queries[1] = swap(query, "ctx", n, 1)
    for i in range(1, pairs):
        queries[2 * i + 1] = swap(queries[2 * i], "ctx", n, 1)

    def attend(pieces, stacked, name):
        message = shape(z.message, HD, BF16)
        outs = [shape(z.message, HD, BF16, len(pieces))] if stacked else [message] * len(pieces)
        chunk = 1024 if cache_slots % 1024 == 0 else cache_slots
        return call(
            functools.partial(attention_kernel, z, pieces, stacked, chunk),
            outs,
            (where, key_cache[0], value_cache[0], bias, extra_key, extra_value, extra_bias)
            + tuple(queries[d] for d in pieces),
            name,
            8 * len(pieces) * z.piece * cache_slots * HD,
            smem=1,
        )

    first, first_odd = attend((0, 1), False, "attend_chip")
    odd = list(range(3, n, 2))
    sets = [tuple(odd[k : k + AT_ONCE]) for k in range(0, len(odd), AT_ONCE)]
    rest_odd = [attend(pieces, True, f"attend_odd{k}")[0] for k, pieces in enumerate(sets)]
    got_first = swap(first_odd, "ctx", n, 1)
    got_rest = [swap(block, "ctx", n, 1) for block in rest_odd]
    rest = [
        attend(tuple(d - 1 for d in pieces), True, f"attend_even{k}")[0]
        for k, pieces in enumerate(sets)
    ]

    message = shape(z.message, HD, BF16)
    own, *sends = call(
        functools.partial(pair_merge_kernel, z, [len(pieces) for pieces in sets]),
        [message] * pairs,
        (first, got_first, *rest, *got_rest),
        "pair_merge",
        1e6,
    )
    gots = [swap(send, "ctx", n, 2 * (i + 1)) for i, send in enumerate(sends)]
    (attended,) = call(
        functools.partial(final_merge_kernel, z),
        [shape(z.piece, HD, BF16)],
        (own, *gots),
        "final_merge",
        1e6,
    )
    heads = {0: attended}
    for i in range(1, pairs):
        heads[2 * i] = swap(attended, "ctx", n, 2 * i)
    heads[1] = swap(attended, "ctx", n, 1)
    for i in range(1, pairs):
        heads[2 * i + 1] = swap(heads[2 * i], "ctx", n, 1)

    columns = out_weight.shape[1]
    share_rows = 2 * z.rows // groups
    shares = call(
        functools.partial(output_kernel, z),
        [shape(share_rows, columns // 2, BF16)] * groups,
        (where, out_weight) + tuple(heads[d] for d in range(n)),
        "output",
        2 * z.rows * z.heads * HD * columns,
        smem=1,
        scratch=[pltpu.VMEM((z.rows, columns), F32)],
    )
    shares = [shares[0]] + [swap(shares[e], "kv", groups, e) for e in range(1, groups)]
    prompt_out, step_out = call(
        functools.partial(share_sum_kernel, z),
        [
            shape(z.prompt // groups, columns, BF16),
            shape(z.row_total // groups, columns, BF16, z.steps),
        ],
        tuple(shares),
        "share_sum",
        1e6,
    )
    return (prompt_out, step_out)


def solution(mesh):
    placed = (
        P(None, "ctx"),
        P(None, None, "ctx"),
        P("ctx"),
        P("ctx", "kv"),
        P("ctx", "kv"),
        P("ctx", "kv"),
        P("kv", "ctx"),
        P("kv", "ctx", None),
        P("kv", "ctx", None),
        P("ctx"),
        P(),
    )
    return jax.shard_map(
        on_device,
        mesh=mesh,
        in_specs=placed,
        out_specs=(P("kv", "ctx"), P(None, "kv", "ctx")),
        check_vma=False,
    )
```

time: 361 us -> 120 us (0.33)
  waiting for transfers between devices: 174 us -> 25.6 us
  blocking collectives: 61.9 us -> 0 us
  matrix products: 60 us -> 0 us
  Pallas kernels: 0 us -> 42.3 us
  starting transfers between devices: 0.29 us -> 20.5 us
  other arithmetic: 39.5 us -> 21.5 us
  between operations: 16.5 us -> 1.5 us
    psum x2 -> x0, waiting for transfers between devices: 101 us -> none  [the longest x1 58.8 us: run_section(): query_sum, square_sum = lax.psum((query_part, squares), 'ctx')]
    reduce_scatter x4 -> x0, waiting for transfers between devices: 66.2 us -> none  [run_section(): lax.psum_scatter(jnp.einsum('srk,kd->rsd', attended, out_weight, preferre...]
    dot_general x32 -> x0, matrix products: 60 us -> none  [the longest x5 21 us: one_block(): jnp.dot(cache_weights, value_shard, preferred_element_type=jnp.float32)]
    pallas_call x0 -> x10, Pallas kernels: none -> 42.3 us  [call(): pl.pallas_call(kernel, out_shape=out_shape, in_specs=[scalar] * smem + [w...]
    reduce_sum x12 -> x0, other arithmetic: 28.8 us -> none  [the longest x5 28.4 us: one_block(): jnp.sum(cache_weights, axis=1, dtype=jnp.float32)]
    psum x2 -> x0, blocking collectives: 27 us -> none  [the longest x1 15.1 us: run_section(): query_sum, square_sum = lax.psum((query_part, squares), 'ctx')]
    ppermute x0 -> x26, waiting for transfers between devices: none -> 25.6 us  [swap(): return lax.ppermute(x, axis, [(i, i ^ d) for i in range(size)])]
    unnamed x1 -> x0, blocking collectives: 22.9 us -> none
  transfers between devices with their start and end apart: 7 -> 26, of which waited for: 7 -> 15; matrix products, arithmetic and copies ran while one was open for 6% -> 19% of each run, Pallas kernels for 0% -> 30%
where the time goes in v1:
time: 120 us; the launch traced here: 119 us
  Pallas kernels  42.3 us (35%)
  waiting for transfers between devices  25.6 us (21%)
  other arithmetic  21.5 us (18%)
  starting transfers between devices  20.5 us (17%)
  local copies, waits for them, and re-layouts  7.51 us (6%)
  between operations  1.5 us (1%)
    pallas_call x10, Pallas kernels, call(): pl.pallas_call(kernel, out_shape=out_shape, in_specs=[scalar] * smem + [w...  42.3 us
    ppermute x26, waiting for transfers between devices, swap(): return lax.ppermute(x, axis, [(i, i ^ d) for i in range(size)])  25.6 us
    ppermute x26, starting transfers between devices, swap(): return lax.ppermute(x, axis, [(i, i ^ d) for i in range(size)])  20.5 us
    select_n x1, other arithmetic, on_device(): limit = jnp.where(is_prompt, row + 1, visible[late % z.row_total])  15.7 us
    gather x26, other arithmetic, on_device(): limit = jnp.where(is_prompt, row + 1, visible[late % z.row_total])  5.44 us
    unnamed x16, local copies, waits for them, and re-layouts  5.38 us
  transfers between devices with their start and end apart: 26, of which 15 were waited for; matrix products, arithmetic and copies ran while one was open for 19% of the time, Pallas kernels for 30%

profile of v1, /device:TPU:0, one launch (start us, length us, event | category | flops | bytes accessed | tf_op | source)
XLA Modules:
  0.0 118.9 jit_solution(18362325070129569571)
XLA Ops:
  1.4 1.6 %copy-done = bf16[1024,1024]{1,0:T(8,128)(2,1)S(1)} copy-done((bf16[1024,1024]{1,0:T(8,128)(2,1)S(1)}, bf16[1024,1024]{1,0:T(8,128)(2,1)}, u32[]{:S(2)}) %copy-start) | copy-done | bytes 2097176
  3.0 0.9 copy-done.2
  4.0 0.9 copy-done.3
  4.9 0.9 copy-done.4
  5.9 0.9 copy-done.5
  6.8 2.1 %project.1 = (f32[4,304,128]{2,1,0:T(8,128)S(1)}, bf16[4,304,128]{2,1,0:T(8,128)(2,1)S(1)}) custom-call(s32[2]{0:T(128)S(1)} %pad_add_fusion.me_ref, bf16[128,1024]{1,0:T(8,128)(2,1)S(1)} %copy-done.2, bf16[96,1024]{1,0:T(8,128)(2,1)S(1)} %bitcast.40, bf16[1,1024]{1,0:T(2,128)(2,1)S(1)} %reshape.121.gain_ref, bf16[1024,1024]{1,0:T(8,128)(2,1)S(1)} %copy-done, ...), custom_call_target="tpu_custom_call" | custom-call | flops 587202560 | bytes 1048576 | tf_op jit(solution)/shard_map/project/pallas_call | solution.py:79
  12.7 4.3 %compare_select_fusion.2 = s32[224,1]{0,1:T(1,128)S(1)} fusion(s32[]{:T(128)} %bitcast.31, s32[]{:T(128)} %bitcast.32, s32[]{:T(128)} %bitcast.33, s32[]{:T(128)} %bitcast.34, s32[]{:T(128)} %bitcast.35, s32[]{:T(128)} %bitcast.37, s32[]{:T(128)} %bitcast.36), kind=kLoop, calls=%fused_computation.28 | loop fusion | flops 5152 | bytes 924 | tf_op jit(solution)/shard_map/gather | solution.py:396
  17.1 15.7 %select_select_fusion = s32[224]{0:T(256)S(1)} fusion(pred[224]{0:T(512)(128)(4,1)S(1)} %compare_reduce_fusion, pred[224]{0:T(512)(128)(4,1)S(1)} %compare_reduce_fusion.1, pred[224]{0:T(512)(128)(4,1)S(1)} %compare_reduce_fusion.2, pred[224]{0:T(512)(128)(4,1)S(1)} %compare_reduce_fusion.3, pred[224]{0:T(512)(128)(4,1)S(1)} %compare_reduce_fusion.4, ...), kind=kLoop, calls=%fused_computation.40 | loop fusion | flops 6272 | bytes 7492 | tf_op jit(solution)/shard_map/jit(_where)/select_n | solution.py:396
  32.9 2.6 %collective-permute-start.1 = (bf16[304,128]{1,0:T(8,128)(2,1)S(1)}, bf16[304,128]{1,0:T(8,128)(2,1)S(1)}, u32[]{:S(2)}, u32[]{:S(2)}) collective-permute-start(bf16[304,128]{1,0:T(8,128)(2,1)S(1)} %get-tuple-element.24), channel_id=1, source_target_pairs={{0,8},{4,12},{8,0},{12,4},{16,24},{20,28},{24,16},{28,20},{1,9},{5... | collective-permute-start | bytes 233480 | tf_op jit(solution)/shard_map/ppermute | solution.py:369
  35.5 1.5 %collective-permute-start.2 = (bf16[304,128]{1,0:T(8,128)(2,1)S(1)}, bf16[304,128]{1,0:T(8,128)(2,1)S(1)}, u32[]{:S(2)}, u32[]{:S(2)}) collective-permute-start(bf16[304,128]{1,0:T(8,128)(2,1)S(1)} %get-tuple-element.25), channel_id=1, source_target_pairs={{0,16},{4,20},{8,24},{12,28},{16,0},{20,4},{24,8},{28,12},{1,17},{... | collective-permute-start | bytes 233480 | tf_op jit(solution)/shard_map/ppermute | solution.py:369
  37.0 1.5 %collective-permute-done.1.refs_0_ = bf16[304,128]{1,0:T(8,128)(2,1)S(1)} collective-permute-done((bf16[304,128]{1,0:T(8,128)(2,1)S(1)}, bf16[304,128]{1,0:T(8,128)(2,1)S(1)}, u32[]{:S(2)}, u32[]{:S(2)}) %collective-permute-start.1) | collective-permute-done | bytes 77856 | tf_op jit(solution)/shard_map/ppermute | solution.py:369
  38.5 2.2 %collective-permute-done.2.refs_1_ = bf16[304,128]{1,0:T(8,128)(2,1)S(1)} collective-permute-done((bf16[304,128]{1,0:T(8,128)(2,1)S(1)}, bf16[304,128]{1,0:T(8,128)(2,1)S(1)}, u32[]{:S(2)}, u32[]{:S(2)}) %collective-permute-start.2) | collective-permute-done | bytes 77856 | tf_op jit(solution)/shard_map/ppermute | solution.py:369
  40.7 1.6 %collective-permute-done.3.refs_2_ = bf16[304,128]{1,0:T(8,128)(2,1)S(1)} collective-permute-done((bf16[304,128]{1,0:T(8,128)(2,1)S(1)}, bf16[304,128]{1,0:T(8,128)(2,1)S(1)}, u32[]{:S(2)}, u32[]{:S(2)}) %collective-permute-start.3) | collective-permute-done | bytes 77856 | tf_op jit(solution)/shard_map/ppermute | solution.py:369
  44.5 2.1 %collective-permute-start.8 = (bf16[224,128]{1,0:T(8,128)(2,1)S(1)}, bf16[224,128]{1,0:T(8,128)(2,1)S(1)}, u32[]{:S(2)}, u32[]{:S(2)}) collective-permute-start(bf16[224,128]{1,0:T(8,128)(2,1)S(1)} %get-tuple-element.29.refs_6_), channel_id=1, source_target_pairs={{0,24},{4,28},{8,16},{12,20},{16,8},{20,12},{24,0},{28,4},{1,25},{... | collective-permute-start | bytes 172040 | tf_op jit(solution)/shard_map/ppermute | solution.py:369
  47.9 1.7 %collective-permute-done.8.refs_8_ = bf16[224,128]{1,0:T(8,128)(2,1)S(1)} collective-permute-done((bf16[224,128]{1,0:T(8,128)(2,1)S(1)}, bf16[224,128]{1,0:T(8,128)(2,1)S(1)}, u32[]{:S(2)}, u32[]{:S(2)}) %collective-permute-start.8) | collective-permute-done | bytes 57376 | tf_op jit(solution)/shard_map/ppermute | solution.py:369
  49.6 9.2 %attend_chip.1 = (bf16[240,128]{1,0:T(8,128)(2,1)S(1)}, bf16[240,128]{1,0:T(8,128)(2,1)S(1)}) custom-call(s32[2]{0:T(128)S(1)} %pad_add_fusion.me_ref, bf16[8192,128]{1,0:T(8,128)(2,1)S(1)} %bitcast.41, bf16[8192,128]{1,0:T(8,128)(2,1)} %bitcast.45, f32[1,8192]{1,0:T(1,128)S(1)} %compare_select_fusion.refs_2_, ...), custom_call_target="tpu_custom_call" | custom-call | flops 3758096384 | bytes 1048576 | tf_op jit(solution)/shard_map/attend_chip/pallas_call | solution.py:79
  59.5 13.3 %attend_odd0.1 = bf16[3,240,128]{2,1,0:T(8,128)(2,1)S(1)} custom-call(s32[2]{0:T(128)S(1)} %pad_add_fusion.me_ref, bf16[8192,128]{1,0:T(8,128)(2,1)S(1)} %bitcast.42, bf16[8192,128]{1,0:T(8,128)(2,1)} %bitcast.46, f32[1,8192]{1,0:T(1,128)S(1)} %compare_select_fusion.refs_2_, bf16[32,128]{1,0:T(8,128)(2,1)S(1)} %get-tuple-element.27.refs_3_, ...), custom_call_target="tpu_custom_call" | custom-call | flops 5637144576 | bytes 1048576 | tf_op jit(solution)/shard_map/attend_odd0/pallas_call | solution.py:79
  72.9 13.5 %attend_even0.1.refs_0_ = bf16[3,240,128]{2,1,0:T(8,128)(2,1)S(1)} custom-call(s32[2]{0:T(128)S(1)} %pad_add_fusion.me_ref, bf16[8192,128]{1,0:T(8,128)(2,1)S(1)} %bitcast.43, bf16[8192,128]{1,0:T(8,128)(2,1)} %bitcast.47, f32[1,8192]{1,0:T(1,128)S(1)} %compare_select_fusion.refs_2_, bf16[32,128]{1,0:T(8,128)(2,1)S(1)} %get-tuple-element.27.refs_3_, ...), custom_call_target="tpu_custom_call" | custom-call | flops 5637144576 | bytes 1048576 | tf_op jit(solution)/shard_map/attend_even0/pallas_call | solution.py:79
  87.0 1.5 %collective-permute-start.13 = (bf16[240,128]{1,0:T(8,128)(2,1)S(1)}, bf16[240,128]{1,0:T(8,128)(2,1)S(1)}, u32[]{:S(2)}, u32[]{:S(2)}) collective-permute-start(bf16[240,128]{1,0:T(8,128)(2,1)S(1)} %get-tuple-element.33), channel_id=1, source_target_pairs={{0,8},{4,12},{8,0},{12,4},{16,24},{20,28},{24,16},{28,20},{1,9},{5... | collective-permute-start | bytes 184328 | tf_op jit(solution)/shard_map/ppermute | solution.py:369
  88.5 1.2 collective-permute-start.14
  90.5 0.9 collective-permute-done.13.refs_1_
  91.4 1.4 %collective-permute-done.14.refs_2_ = bf16[240,128]{1,0:T(8,128)(2,1)S(1)} collective-permute-done((bf16[240,128]{1,0:T(8,128)(2,1)S(1)}, bf16[240,128]{1,0:T(8,128)(2,1)S(1)}, u32[]{:S(2)}, u32[]{:S(2)}) %collective-permute-start.14) | collective-permute-done | bytes 61472 | tf_op jit(solution)/shard_map/ppermute | solution.py:369
  92.7 2.1 %collective-permute-done.15.refs_3_ = bf16[240,128]{1,0:T(8,128)(2,1)S(1)} collective-permute-done((bf16[240,128]{1,0:T(8,128)(2,1)S(1)}, bf16[240,128]{1,0:T(8,128)(2,1)S(1)}, u32[]{:S(2)}, u32[]{:S(2)}) %collective-permute-start.15) | collective-permute-done | bytes 61472 | tf_op jit(solution)/shard_map/ppermute | solution.py:369
  95.8 0.8 collective-permute-start.19
  96.7 2.1 %collective-permute-start.21 = (bf16[224,128]{1,0:T(8,128)(2,1)S(1)}, bf16[224,128]{1,0:T(8,128)(2,1)S(1)}, u32[]{:S(2)}, u32[]{:S(2)}) collective-permute-start(bf16[224,128]{1,0:T(8,128)(2,1)S(1)} %final_merge.1.refs_0_), channel_id=1, source_target_pairs={{0,24},{4,28},{8,16},{12,20},{16,8},{20,12},{24,0},{28,4},{1,25},{... | collective-permute-start | bytes 172040 | tf_op jit(solution)/shard_map/ppermute | solution.py:369
  100.0 1.7 %collective-permute-done.21.refs_6_ = bf16[224,128]{1,0:T(8,128)(2,1)S(1)} collective-permute-done((bf16[224,128]{1,0:T(8,128)(2,1)S(1)}, bf16[224,128]{1,0:T(8,128)(2,1)S(1)}, u32[]{:S(2)}, u32[]{:S(2)}) %collective-permute-start.21) | collective-permute-done | bytes 57376 | tf_op jit(solution)/shard_map/ppermute | solution.py:369
  101.8 1.2 %collective-permute-done.22.refs_7_ = bf16[224,128]{1,0:T(8,128)(2,1)S(1)} collective-permute-done((bf16[224,128]{1,0:T(8,128)(2,1)S(1)}, bf16[224,128]{1,0:T(8,128)(2,1)S(1)}, u32[]{:S(2)}, u32[]{:S(2)}) %collective-permute-start.22) | collective-permute-done | bytes 57376 | tf_op jit(solution)/shard_map/ppermute | solution.py:369
  103.0 1.7 %output.1 = (bf16[112,512]{1,0:T(8,128)(2,1)S(1)}, bf16[112,512]{1,0:T(8,128)(2,1)S(1)}, bf16[112,512]{1,0:T(8,128)(2,1)S(1)}, bf16[112,512]{1,0:T(8,128)(2,1)S(1)}) custom-call(s32[2]{0:T(128)S(1)} %pad_add_fusion.me_ref, bf16[1024,1024]{1,0:T(8,128)(2,1)S(1)} %copy-done.1, bf16[224,128]{1,0:T(8,128)(2,1)S(1)} %final_merge.1.refs_0_, ...), custom_call_target="tpu_custom_call" | custom-call | flops 469762048 | bytes 1048576 | tf_op jit(solution)/shard_map/output/pallas_call | solution.py:79
  104.7 1.6 %collective-permute-start.23 = (bf16[112,512]{1,0:T(8,128)(2,1)S(1)}, bf16[112,512]{1,0:T(8,128)(2,1)S(1)}, u32[]{:S(2)}, u32[]{:S(2)}) collective-permute-start(bf16[112,512]{1,0:T(8,128)(2,1)S(1)} %get-tuple-element.37), channel_id=1, source_target_pairs={{0,1},{1,0},{2,3},{3,2},{4,5},{5,4},{6,7},{7,6},{8,9},{9,8},{10,11... | collective-permute-start | bytes 344072 | tf_op jit(solution)/shard_map/ppermute | solution.py:369
  106.3 2.6 %collective-permute-start.24 = (bf16[112,512]{1,0:T(8,128)(2,1)S(1)}, bf16[112,512]{1,0:T(8,128)(2,1)S(1)}, u32[]{:S(2)}, u32[]{:S(2)}) collective-permute-start(bf16[112,512]{1,0:T(8,128)(2,1)S(1)} %get-tuple-element.38), channel_id=1, source_target_pairs={{0,2},{1,3},{2,0},{3,1},{4,6},{5,7},{6,4},{7,5},{8,10},{9,11},{10,... | collective-permute-start | bytes 344072 | tf_op jit(solution)/shard_map/ppermute | solution.py:369
  109.1 2.3 %collective-permute-done.23.refs_1_ = bf16[112,512]{1,0:T(8,128)(2,1)S(1)} collective-permute-done((bf16[112,512]{1,0:T(8,128)(2,1)S(1)}, bf16[112,512]{1,0:T(8,128)(2,1)S(1)}, u32[]{:S(2)}, u32[]{:S(2)}) %collective-permute-start.23) | collective-permute-done | bytes 114720 | tf_op jit(solution)/shard_map/ppermute | solution.py:369
  111.5 6.7 %collective-permute-done.24.refs_2_ = bf16[112,512]{1,0:T(8,128)(2,1)S(1)} collective-permute-done((bf16[112,512]{1,0:T(8,128)(2,1)S(1)}, bf16[112,512]{1,0:T(8,128)(2,1)S(1)}, u32[]{:S(2)}, u32[]{:S(2)}) %collective-permute-start.24) | collective-permute-done | bytes 114720 | tf_op jit(solution)/shard_map/ppermute | solution.py:369
  (84 shorter events, 12.8 us)
Async XLA Ops:
  0.6 9.9 %copy-start.7 = (s32[32]{0:T(128)S(1)}, s32[32]{0:T(128)}, u32[]{:S(2)}) copy-start(s32[32]{0:T(128)} %param.21) | copy-start | bytes 388
  1.4 1.6 %copy-start = (bf16[1024,1024]{1,0:T(8,128)(2,1)S(1)}, bf16[1024,1024]{1,0:T(8,128)(2,1)}, u32[]{:S(2)}) copy-start(bf16[1024,1024]{1,0:T(8,128)(2,1)} %wq_ref.1) | copy-start | bytes 6291460
  3.0 0.9 copy-start.2
  4.0 0.9 copy-start.3
  6.8 42.8 %copy-start.6 = (bf16[1,8192,128]{2,1,0:T(8,128)(2,1)S(1)}, bf16[1,8192,128]{2,1,0:T(8,128)(2,1)}, u32[]{:S(2)}) copy-start(bf16[1,8192,128]{2,1,0:T(8,128)(2,1)} %param.18) | copy-start | bytes 6291460
  8.9 23.9 %collective-permute-start = (bf16[4,304,128]{2,1,0:T(8,128)(2,1)S(1)}, bf16[4,304,128]{2,1,0:T(8,128)(2,1)S(1)}, u32[]{:S(2)}, u32[]{:S(2)}) collective-permute-start(bf16[4,304,128]{2,1,0:T(8,128)(2,1)S(1)} %get-tuple-element.22), channel_id=1, source_target_pairs={{0,4},{4,0},{8,12},{12,8},{16,20},{20,16},{24,28},{28,24},{1,5},{5... | collective-permute-start | bytes 933896 | tf_op jit(solution)/shard_map/ppermute | solution.py:369
  32.9 5.6 %collective-permute-start.1 = (bf16[304,128]{1,0:T(8,128)(2,1)S(1)}, bf16[304,128]{1,0:T(8,128)(2,1)S(1)}, u32[]{:S(2)}, u32[]{:S(2)}) collective-permute-start(bf16[304,128]{1,0:T(8,128)(2,1)S(1)} %get-tuple-element.24), channel_id=1, source_target_pairs={{0,8},{4,12},{8,0},{12,4},{16,24},{20,28},{24,16},{28,20},{1,9},{5... | collective-permute-start | bytes 233480 | tf_op jit(solution)/shard_map/ppermute | solution.py:369
  35.5 5.2 %collective-permute-start.2 = (bf16[304,128]{1,0:T(8,128)(2,1)S(1)}, bf16[304,128]{1,0:T(8,128)(2,1)S(1)}, u32[]{:S(2)}, u32[]{:S(2)}) collective-permute-start(bf16[304,128]{1,0:T(8,128)(2,1)S(1)} %get-tuple-element.25), channel_id=1, source_target_pairs={{0,16},{4,20},{8,24},{12,28},{16,0},{20,4},{24,8},{28,12},{1,17},{... | collective-permute-start | bytes 233480 | tf_op jit(solution)/shard_map/ppermute | solution.py:369
  37.0 5.3 %collective-permute-start.3 = (bf16[304,128]{1,0:T(8,128)(2,1)S(1)}, bf16[304,128]{1,0:T(8,128)(2,1)S(1)}, u32[]{:S(2)}, u32[]{:S(2)}) collective-permute-start(bf16[304,128]{1,0:T(8,128)(2,1)S(1)} %get-tuple-element.26), channel_id=1, source_target_pairs={{0,24},{4,28},{8,16},{12,20},{16,8},{20,12},{24,0},{28,4},{1,25},{... | collective-permute-start | bytes 233480 | tf_op jit(solution)/shard_map/ppermute | solution.py:369
  43.0 6.6 %collective-permute-start.4 = (bf16[224,128]{1,0:T(8,128)(2,1)S(1)}, bf16[224,128]{1,0:T(8,128)(2,1)S(1)}, u32[]{:S(2)}, u32[]{:S(2)}) collective-permute-start(bf16[224,128]{1,0:T(8,128)(2,1)S(1)} %get-tuple-element.29.refs_6_), channel_id=1, source_target_pairs={{0,4},{4,0},{8,12},{12,8},{16,20},{20,16},{24,28},{28,24},{1,5},{5... | collective-permute-start | bytes 172040 | tf_op jit(solution)/shard_map/ppermute | solution.py:369
  43.1 4.3 %collective-permute-start.6 = (bf16[224,128]{1,0:T(8,128)(2,1)S(1)}, bf16[224,128]{1,0:T(8,128)(2,1)S(1)}, u32[]{:S(2)}, u32[]{:S(2)}) collective-permute-start(bf16[224,128]{1,0:T(8,128)(2,1)S(1)} %get-tuple-element.29.refs_6_), channel_id=1, source_target_pairs={{0,8},{4,12},{8,0},{12,4},{16,24},{20,28},{24,16},{28,20},{1,9},{5... | collective-permute-start | bytes 172040 | tf_op jit(solution)/shard_map/ppermute | solution.py:369
  43.7 4.2 %collective-permute-start.7 = (bf16[224,128]{1,0:T(8,128)(2,1)S(1)}, bf16[224,128]{1,0:T(8,128)(2,1)S(1)}, u32[]{:S(2)}, u32[]{:S(2)}) collective-permute-start(bf16[224,128]{1,0:T(8,128)(2,1)S(1)} %get-tuple-element.29.refs_6_), channel_id=1, source_target_pairs={{0,16},{4,20},{8,24},{12,28},{16,0},{20,4},{24,8},{28,12},{1,17},{... | collective-permute-start | bytes 172040 | tf_op jit(solution)/shard_map/ppermute | solution.py:369
  44.5 5.1 %collective-permute-start.8 = (bf16[224,128]{1,0:T(8,128)(2,1)S(1)}, bf16[224,128]{1,0:T(8,128)(2,1)S(1)}, u32[]{:S(2)}, u32[]{:S(2)}) collective-permute-start(bf16[224,128]{1,0:T(8,128)(2,1)S(1)} %get-tuple-element.29.refs_6_), channel_id=1, source_target_pairs={{0,24},{4,28},{8,16},{12,20},{16,8},{20,12},{24,0},{28,4},{1,25},{... | collective-permute-start | bytes 172040 | tf_op jit(solution)/shard_map/ppermute | solution.py:369
  47.4 12.0 %collective-permute-start.9 = (bf16[224,128]{1,0:T(8,128)(2,1)S(1)}, bf16[224,128]{1,0:T(8,128)(2,1)S(1)}, u32[]{:S(2)}, u32[]{:S(2)}) collective-permute-start(bf16[224,128]{1,0:T(8,128)(2,1)S(1)} %collective-permute-done.6.refs_6_), channel_id=1, source_target_pairs={{0,4},{4,0},{8,12},{12,8},{16,20},{20,16},{24,28},{28,24},{1,5},{5... | collective-permute-start | bytes 172040 | tf_op jit(solution)/shard_map/ppermute | solution.py:369
  47.9 11.6 %collective-permute-start.10 = (bf16[224,128]{1,0:T(8,128)(2,1)S(1)}, bf16[224,128]{1,0:T(8,128)(2,1)S(1)}, u32[]{:S(2)}, u32[]{:S(2)}) collective-permute-start(bf16[224,128]{1,0:T(8,128)(2,1)S(1)} %collective-permute-done.7.refs_7_), channel_id=1, source_target_pairs={{0,4},{4,0},{8,12},{12,8},{16,20},{20,16},{24,28},{28,24},{1,5},{5... | collective-permute-start | bytes 172040 | tf_op jit(solution)/shard_map/ppermute | solution.py:369
  49.6 9.8 %collective-permute-start.11 = (bf16[224,128]{1,0:T(8,128)(2,1)S(1)}, bf16[224,128]{1,0:T(8,128)(2,1)S(1)}, u32[]{:S(2)}, u32[]{:S(2)}) collective-permute-start(bf16[224,128]{1,0:T(8,128)(2,1)S(1)} %collective-permute-done.8.refs_8_), channel_id=1, source_target_pairs={{0,4},{4,0},{8,12},{12,8},{16,20},{20,16},{24,28},{28,24},{1,5},{5... | collective-permute-start | bytes 172040 | tf_op jit(solution)/shard_map/ppermute | solution.py:369
  58.9 27.5 %collective-permute-start.5 = (bf16[240,128]{1,0:T(8,128)(2,1)S(1)}, bf16[240,128]{1,0:T(8,128)(2,1)S(1)}, u32[]{:S(2)}, u32[]{:S(2)}) collective-permute-start(bf16[240,128]{1,0:T(8,128)(2,1)S(1)} %get-tuple-element.31), channel_id=1, source_target_pairs={{0,4},{4,0},{8,12},{12,8},{16,20},{20,16},{24,28},{28,24},{1,5},{5... | collective-permute-start | bytes 184328 | tf_op jit(solution)/shard_map/ppermute | solution.py:369
  72.8 30.2 %copy-start.1 = (bf16[1024,1024]{1,0:T(8,128)(2,1)S(1)}, bf16[1024,1024]{1,0:T(8,128)(2,1)}, u32[]{:S(2)}) copy-start(bf16[1024,1024]{1,0:T(8,128)(2,1)} %weight_ref.1) | copy-start | bytes 6291460
  72.8 13.6 %collective-permute-start.12 = (bf16[3,240,128]{2,1,0:T(8,128)(2,1)S(1)}, bf16[3,240,128]{2,1,0:T(8,128)(2,1)S(1)}, u32[]{:S(2)}, u32[]{:S(2)}) collective-permute-start(bf16[3,240,128]{2,1,0:T(8,128)(2,1)S(1)} %attend_odd0.1), channel_id=1, source_target_pairs={{0,4},{4,0},{8,12},{12,8},{16,20},{20,16},{24,28},{28,24},{1,5},{5... | collective-permute-start | bytes 552968 | tf_op jit(solution)/shard_map/ppermute | solution.py:369
  87.0 4.4 %collective-permute-start.13 = (bf16[240,128]{1,0:T(8,128)(2,1)S(1)}, bf16[240,128]{1,0:T(8,128)(2,1)S(1)}, u32[]{:S(2)}, u32[]{:S(2)}) collective-permute-start(bf16[240,128]{1,0:T(8,128)(2,1)S(1)} %get-tuple-element.33), channel_id=1, source_target_pairs={{0,8},{4,12},{8,0},{12,4},{16,24},{20,28},{24,16},{28,20},{1,9},{5... | collective-permute-start | bytes 184328 | tf_op jit(solution)/shard_map/ppermute | solution.py:369
  88.5 4.2 %collective-permute-start.14 = (bf16[240,128]{1,0:T(8,128)(2,1)S(1)}, bf16[240,128]{1,0:T(8,128)(2,1)S(1)}, u32[]{:S(2)}, u32[]{:S(2)}) collective-permute-start(bf16[240,128]{1,0:T(8,128)(2,1)S(1)} %get-tuple-element.34), channel_id=1, source_target_pairs={{0,16},{4,20},{8,24},{12,28},{16,0},{20,4},{24,8},{28,12},{1,17},{... | collective-permute-start | bytes 184328 | tf_op jit(solution)/shard_map/ppermute | solution.py:369
  89.7 5.1 %collective-permute-start.15 = (bf16[240,128]{1,0:T(8,128)(2,1)S(1)}, bf16[240,128]{1,0:T(8,128)(2,1)S(1)}, u32[]{:S(2)}, u32[]{:S(2)}) collective-permute-start(bf16[240,128]{1,0:T(8,128)(2,1)S(1)} %get-tuple-element.35), channel_id=1, source_target_pairs={{0,24},{4,28},{8,16},{12,20},{16,8},{20,12},{24,0},{28,4},{1,25},{... | collective-permute-start | bytes 184328 | tf_op jit(solution)/shard_map/ppermute | solution.py:369
  95.2 4.2 %collective-permute-start.17 = (bf16[224,128]{1,0:T(8,128)(2,1)S(1)}, bf16[224,128]{1,0:T(8,128)(2,1)S(1)}, u32[]{:S(2)}, u32[]{:S(2)}) collective-permute-start(bf16[224,128]{1,0:T(8,128)(2,1)S(1)} %final_merge.1.refs_0_), channel_id=1, source_target_pairs={{0,8},{4,12},{8,0},{12,4},{16,24},{20,28},{24,16},{28,20},{1,9},{5... | collective-permute-start | bytes 172040 | tf_op jit(solution)/shard_map/ppermute | solution.py:369
  95.8 4.2 %collective-permute-start.19 = (bf16[224,128]{1,0:T(8,128)(2,1)S(1)}, bf16[224,128]{1,0:T(8,128)(2,1)S(1)}, u32[]{:S(2)}, u32[]{:S(2)}) collective-permute-start(bf16[224,128]{1,0:T(8,128)(2,1)S(1)} %final_merge.1.refs_0_), channel_id=1, source_target_pairs={{0,16},{4,20},{8,24},{12,28},{16,0},{20,4},{24,8},{28,12},{1,17},{... | collective-permute-start | bytes 172040 | tf_op jit(solution)/shard_map/ppermute | solution.py:369
  96.7 5.1 %collective-permute-start.21 = (bf16[224,128]{1,0:T(8,128)(2,1)S(1)}, bf16[224,128]{1,0:T(8,128)(2,1)S(1)}, u32[]{:S(2)}, u32[]{:S(2)}) collective-permute-start(bf16[224,128]{1,0:T(8,128)(2,1)S(1)} %final_merge.1.refs_0_), channel_id=1, source_target_pairs={{0,24},{4,28},{8,16},{12,20},{16,8},{20,12},{24,0},{28,4},{1,25},{... | collective-permute-start | bytes 172040 | tf_op jit(solution)/shard_map/ppermute | solution.py:369
  98.8 3.0 %collective-permute-start.16 = (bf16[224,128]{1,0:T(8,128)(2,1)S(1)}, bf16[224,128]{1,0:T(8,128)(2,1)S(1)}, u32[]{:S(2)}, u32[]{:S(2)}) collective-permute-start(bf16[224,128]{1,0:T(8,128)(2,1)S(1)} %final_merge.1.refs_0_), channel_id=1, source_target_pairs={{0,4},{4,0},{8,12},{12,8},{16,20},{20,16},{24,28},{28,24},{1,5},{5... | collective-permute-start | bytes 172040 | tf_op jit(solution)/shard_map/ppermute | solution.py:369
  99.5 2.3 %collective-permute-start.18 = (bf16[224,128]{1,0:T(8,128)(2,1)S(1)}, bf16[224,128]{1,0:T(8,128)(2,1)S(1)}, u32[]{:S(2)}, u32[]{:S(2)}) collective-permute-start(bf16[224,128]{1,0:T(8,128)(2,1)S(1)} %collective-permute-done.17.refs_2_), channel_id=1, source_target_pairs={{0,4},{4,0},{8,12},{12,8},{16,20},{20,16},{24,28},{28,24},{1,5},{5... | collective-permute-start | bytes 172040 | tf_op jit(solution)/shard_map/ppermute | solution.py:369
  100.0 1.8 %collective-permute-start.20 = (bf16[224,128]{1,0:T(8,128)(2,1)S(1)}, bf16[224,128]{1,0:T(8,128)(2,1)S(1)}, u32[]{:S(2)}, u32[]{:S(2)}) collective-permute-start(bf16[224,128]{1,0:T(8,128)(2,1)S(1)} %collective-permute-done.19.refs_4_), channel_id=1, source_target_pairs={{0,4},{4,0},{8,12},{12,8},{16,20},{20,16},{24,28},{28,24},{1,5},{5... | collective-permute-start | bytes 172040 | tf_op jit(solution)/shard_map/ppermute | solution.py:369
  101.8 1.2 %collective-permute-start.22 = (bf16[224,128]{1,0:T(8,128)(2,1)S(1)}, bf16[224,128]{1,0:T(8,128)(2,1)S(1)}, u32[]{:S(2)}, u32[]{:S(2)}) collective-permute-start(bf16[224,128]{1,0:T(8,128)(2,1)S(1)} %collective-permute-done.21.refs_6_), channel_id=1, source_target_pairs={{0,4},{4,0},{8,12},{12,8},{16,20},{20,16},{24,28},{28,24},{1,5},{5... | collective-permute-start | bytes 172040 | tf_op jit(solution)/shard_map/ppermute | solution.py:369
  104.7 6.8 %collective-permute-start.23 = (bf16[112,512]{1,0:T(8,128)(2,1)S(1)}, bf16[112,512]{1,0:T(8,128)(2,1)S(1)}, u32[]{:S(2)}, u32[]{:S(2)}) collective-permute-start(bf16[112,512]{1,0:T(8,128)(2,1)S(1)} %get-tuple-element.37), channel_id=1, source_target_pairs={{0,1},{1,0},{2,3},{3,2},{4,5},{5,4},{6,7},{7,6},{8,9},{9,8},{10,11... | collective-permute-start | bytes 344072 | tf_op jit(solution)/shard_map/ppermute | solution.py:369
  106.3 11.8 %collective-permute-start.24 = (bf16[112,512]{1,0:T(8,128)(2,1)S(1)}, bf16[112,512]{1,0:T(8,128)(2,1)S(1)}, u32[]{:S(2)}, u32[]{:S(2)}) collective-permute-start(bf16[112,512]{1,0:T(8,128)(2,1)S(1)} %get-tuple-element.38), channel_id=1, source_target_pairs={{0,2},{1,3},{2,0},{3,1},{4,6},{5,7},{6,4},{7,5},{8,10},{9,11},{10,... | collective-permute-start | bytes 344072 | tf_op jit(solution)/shard_map/ppermute | solution.py:369
  108.9 9.3 %collective-permute-start.25 = (bf16[112,512]{1,0:T(8,128)(2,1)S(1)}, bf16[112,512]{1,0:T(8,128)(2,1)S(1)}, u32[]{:S(2)}, u32[]{:S(2)}) collective-permute-start(bf16[112,512]{1,0:T(8,128)(2,1)S(1)} %get-tuple-element.39), channel_id=1, source_target_pairs={{0,3},{1,2},{2,1},{3,0},{4,7},{5,6},{6,5},{7,4},{8,11},{9,10},{10,... | collective-permute-start | bytes 344072 | tf_op jit(solution)/shard_map/ppermute | solution.py:369
  (2 other events, 1.9 us)

commit v2 on v1

--- a/solution.py
+++ b/solution.py
@@ -13,7 +13,7 @@
 LOG2E = 1.4426950408889634
 STAT_ROWS = 16
 AT_ONCE = 3
-VMEM_BYTES = 50 * 2**20
+VMEM_BYTES = 20 * 2**20
 BF16 = jnp.bfloat16
 F32 = jnp.float32
 
@@ -73,13 +73,15 @@
     return out
 
 
-def call(kernel, out_shape, args, name, flops, smem=0, grant=VMEM_BYTES, scratch=()):
+def call(kernel, out_shape, args, name, flops, smem=0, far=0, grant=VMEM_BYTES, scratch=()):
     whole = pl.BlockSpec(memory_space=pltpu.VMEM)
     scalar = pl.BlockSpec(memory_space=pltpu.SMEM)
     return pl.pallas_call(
         kernel,
         out_shape=out_shape,
-        in_specs=[scalar] * smem + [whole] * (len(args) - smem),
+        in_specs=[scalar] * smem
+        + [whole] * (len(args) - smem - far)
+        + [pl.BlockSpec(memory_space=pltpu.HBM)] * far,
         out_specs=jax.tree.map(lambda _: whole, out_shape),
         scratch_shapes=list(scratch),
         compiler_params=pltpu.CompilerParams(vmem_limit_bytes=grant),
@@ -118,14 +120,31 @@
         self.project = self.piece + 2 * self.slots + STAT_ROWS
 
 
-def project_kernel(z, me_ref, xp_ref, xs_ref, gain_ref, wq_ref, wk_ref, wv_ref, even_ref, odd_ref, scaled_ref, kvp_ref, kvd_ref):
-    me = me_ref[0]
+def project_kernel(z, gain_ref, xp_hbm, xs_hbm, wq_hbm, wk_hbm, wv_hbm, even_ref, odd_ref, xp_ref, xs_ref, wq_ref, wk_ref, wv_ref, scaled_ref, query_ref, kvp_ref, kvd_ref, sems):
+    me = lax.axis_index("ctx")
+    depth = z.width // 2
+    loads = [
+        pltpu.make_async_copy(xp_hbm, xp_ref, sems.at[0]),
+        pltpu.make_async_copy(xs_hbm, xs_ref, sems.at[1]),
+        pltpu.make_async_copy(wk_hbm, wk_ref, sems.at[2]),
+        pltpu.make_async_copy(wv_hbm, wv_ref, sems.at[3]),
+    ]
+    loads += [
+        pltpu.make_async_copy(wq_hbm.at[pl.ds(k * depth, depth), :], wq_ref.at[k], sems.at[4 + k])
+        for k in range(2)
+    ]
+    for load in loads:
+        load.start()
     gain = gain_ref[...].astype(F32)
+    gain = jnp.concatenate([gain[k : k + 1, :] for k in range(gain.shape[0])], axis=1)
     squares = []
-    for ref, base, size in (
-        (xp_ref, 0, z.prompt),
-        (xs_ref, z.prompt, z.steps * z.row_total),
+    for k, (ref, base, size) in enumerate(
+        (
+            (xp_ref, 0, z.prompt),
+            (xs_ref, z.prompt, z.steps * z.row_total),
+        )
     ):
+        loads[k].wait()
         wide = ref[...].astype(F32)
         squares.append(jnp.sum(wide * wide, axis=1, keepdims=True))
         scaled_ref[base : base + size, :] = (wide * gain).astype(BF16)
@@ -148,20 +167,24 @@
         pick, scaled_ref[z.prompt : z.rows, :], preferred_element_type=F32
     ).astype(BF16)
     for c, ref in enumerate((wk_ref, wv_ref)):
+        loads[2 + c].wait()
         kvp_ref[:, c * HD : (c + 1) * HD] = jnp.dot(
             scaled_ref[0 : z.prompt, :], ref[...], preferred_element_type=F32
         )
         kvd_ref[:, c * HD : (c + 1) * HD] = jnp.dot(ordered, ref[...], preferred_element_type=F32)
+    loads[4].wait()
+    product = jnp.dot(scaled_ref[:, :depth], wq_ref[0], preferred_element_type=F32)
+    loads[5].wait()
+    query_ref[...] = product + jnp.dot(
+        scaled_ref[:, depth:], wq_ref[1], preferred_element_type=F32
+    )
     for d in range(z.n):
         owner = jnp.bitwise_xor(me, d)
-        head = owner % z.heads
         half = owner // z.heads
-        rows = scaled_ref[pl.ds(pl.multiple_of(half * z.piece, 16), z.piece), :]
-        part = jnp.dot(
-            rows,
-            wq_ref[:, pl.ds(pl.multiple_of(head * HD, HD), HD)],
-            preferred_element_type=F32,
-        )
+        part = query_ref[
+            pl.ds(pl.multiple_of(half * z.piece, 8), z.piece),
+            pl.ds(pl.multiple_of(owner % z.heads * HD, HD), HD),
+        ]
         kvp = kvp_ref[pl.ds(pl.multiple_of(owner * z.prompt_own, 8), z.prompt_own), :]
         kvd = kvd_ref[pl.ds(pl.multiple_of(owner * z.decode_slots, 8), z.decode_slots), :]
         ref = odd_ref if d % 2 else even_ref
@@ -190,10 +213,10 @@
             ).astype(BF16)
 
 
-def finish_kernel(z, features, me_ref, own_ref, *refs):
+def finish_kernel(z, features, own_ref, *refs):
     got_refs = refs[: z.n // 2 - 1]
     query_ref, key_ref, value_ref = refs[z.n // 2 - 1 :]
-    me = me_ref[0]
+    me = lax.axis_index("ctx")
     body = z.project - STAT_ROWS
     total = own_ref[0:body, :]
     squares = own_ref[body : body + z.square_lines, :]
@@ -220,11 +243,37 @@
     value_ref[...] = (total[z.piece + z.slots : z.piece + 2 * z.slots] * own).astype(BF16)
 
 
-def attention_kernel(z, pieces, stacked, chunk, me_ref, *refs):
+def mask_kernel(z, length_ref, visible_ref, bias_ref, extra_ref):
+    me = lax.axis_index("ctx")
+    live = lax.broadcasted_iota(jnp.int32, bias_ref.shape, 1) < length_ref[0]
+    bias_ref[...] = jnp.where(live, 0.0, MASKED)
+    row = lax.broadcasted_iota(jnp.int32, (z.rows, 1), 0)
+    late = row - z.prompt
+    step = late // z.row_total
+    place = late - step * z.row_total
+    lanes = lax.broadcasted_iota(jnp.int32, (z.rows, z.row_total), 1)
+    allowed = jnp.sum(
+        jnp.where(lanes == place, visible_ref[...].astype(F32), 0.0), axis=1, keepdims=True
+    )
+    limit = jnp.where(late < 0, row + 1, allowed.astype(jnp.int32))
+    slot = lax.broadcasted_iota(jnp.int32, (z.rows, z.slots), 1)
+    late_slot = slot - z.prompt_slots
+    from_prompt = (slot < z.prompt_own) & (me * z.prompt_own + slot < limit)
+    from_decode = (
+        (late_slot >= 0)
+        & (late_slot < z.decode_own)
+        & (late >= 0)
+        & (me * z.rows_own + late_slot % z.rows_own == place)
+        & (late_slot // z.rows_own <= step)
+    )
+    extra_ref[...] = jnp.where(from_prompt | from_decode, 0.0, MASKED)
+
+
+def attention_kernel(z, pieces, stacked, chunk, *refs):
     key_ref, value_ref, bias_ref, extra_key_ref, extra_value_ref, extra_bias_ref = refs[:6]
     query_refs = refs[6 : 6 + len(pieces)]
     out_refs = refs[6 + len(pieces) :]
-    me = me_ref[0]
+    me = lax.axis_index("ctx")
     over = (((1,), (1,)), ((), ()))
     for i, d in enumerate(pieces):
         query = query_refs[i][...]
@@ -244,21 +293,17 @@
             else:
                 score = score + extra_bias
             top = jnp.max(score, axis=1, keepdims=True)
-            weight = jnp.exp2(score - top)
-            total = jnp.sum(weight, axis=1, keepdims=True)
-            mixed = jnp.dot(
-                weight.astype(BF16), values[start : start + size, :], preferred_element_type=F32
+            weight = jnp.exp2(score - top).astype(BF16)
+            beside = jnp.concatenate(
+                [values[start : start + size, :], jnp.ones((size, HD), BF16)], axis=1
             )
-            found.append((top, total, mixed))
-        highest = functools.reduce(jnp.maximum, [top for top, _, _ in found])
-        total = 0.0
+            found.append((top, jnp.dot(weight, beside, preferred_element_type=F32)))
+        highest = functools.reduce(jnp.maximum, [top for top, _ in found])
         mixed = 0.0
-        for top, block_total, block_mixed in found:
-            scale = jnp.exp2(top - highest)
-            total = total + block_total * scale
-            mixed = mixed + block_mixed * scale
-        stats = stack_stats([column_to_rows(highest), column_to_rows(total)])
-        message = jnp.concatenate([mixed, stats], axis=0).astype(BF16)
+        for top, block in found:
+            mixed = mixed + block * jnp.exp2(top - highest)
+        stats = stack_stats([column_to_rows(highest), column_to_rows(mixed[:, HD : HD + 1])])
+        message = jnp.concatenate([mixed[:, :HD], stats], axis=0).astype(BF16)
         if stacked:
             out_refs[0][i] = message
         else:
@@ -282,23 +327,14 @@
     return highest, total, mixed
 
 
-def pair_merge_kernel(z, sets, first_ref, got_first_ref, *refs):
+def pair_merge_kernel(z, sets, *refs):
     mine_refs = refs[: len(sets)]
     got_refs = refs[len(sets) : 2 * len(sets)]
-    own_ref, *send_refs = refs[2 * len(sets) :]
+    send_refs = refs[2 * len(sets) :]
     places = [(s, k) for s, size in enumerate(sets) for k in range(size)]
-    for i in range(z.n // 2):
-        if i == 0:
-            mine, theirs = first_ref[...], got_first_ref[...]
-        else:
-            s, k = places[i - 1]
-            mine, theirs = mine_refs[s][k], got_refs[s][k]
-        highest, total, mixed = merge(z, [mine, theirs])
-        message = jnp.concatenate([mixed, stack_stats([highest, total])], axis=0).astype(BF16)
-        if i == 0:
-            own_ref[...] = message
-        else:
-            send_refs[i - 1][...] = message
+    for send_ref, (s, k) in zip(send_refs, places):
+        highest, total, mixed = merge(z, [mine_refs[s][k], got_refs[s][k]])
+        send_ref[...] = jnp.concatenate([mixed, stack_stats([highest, total])], axis=0).astype(BF16)
 
 
 def final_merge_kernel(z, *refs):
@@ -308,22 +344,28 @@
     out_ref[...] = (mixed / rows_to_column(total, index)).astype(BF16)
 
 
-def output_kernel(z, me_ref, weight_ref, *refs):
+def output_kernel(z, weight_ref, *refs):
     piece_refs = refs[: z.n]
     out_refs = refs[z.n : z.n + z.groups]
     sum_ref = refs[-1]
-    me = me_ref[0]
-    place = me_ref[1]
+    me = lax.axis_index("ctx")
+    place = lax.axis_index("kv")
     columns = weight_ref.shape[1]
     if z.halves > 1:
         sum_ref[...] = jnp.zeros_like(sum_ref)
     total = None
-    for d in range(z.n):
+    swapped = me % 2 == 1
+    for d in range(0, z.n, 2):
         owner = jnp.bitwise_xor(me, d)
-        head = owner % z.heads
+        first, second = piece_refs[d][...], piece_refs[d + 1][...]
+        both = jnp.where(
+            swapped,
+            jnp.concatenate([second, first], axis=1),
+            jnp.concatenate([first, second], axis=1),
+        )
         product = jnp.dot(
-            piece_refs[d][...],
-            weight_ref[pl.ds(pl.multiple_of(head * HD, HD), HD), :],
+            both,
+            weight_ref[pl.ds(pl.multiple_of(owner % z.heads // 2 * 2 * HD, 2 * HD), 2 * HD), :],
             preferred_element_type=F32,
         )
         if z.halves == 1:
@@ -385,49 +427,44 @@
     n = lax.axis_size("ctx")
     groups = lax.axis_size("kv")
     z = Sizes(prompt_in, step_in, query_weight, visible, n, groups)
-    me = lax.axis_index("ctx").astype(jnp.int32)
-    place = lax.axis_index("kv").astype(jnp.int32)
-    where = jnp.stack([me, place])
     pairs = n // 2
 
-    row = jnp.arange(z.rows, dtype=jnp.int32)
-    is_prompt = row < z.prompt
-    late = jnp.maximum(row - z.prompt, 0)
-    limit = jnp.where(is_prompt, row + 1, visible[late % z.row_total])
-    slot = jnp.arange(z.slots, dtype=jnp.int32)
-    late_slot = jnp.maximum(slot - z.prompt_slots, 0)
-    seen_prompt = (slot < z.prompt_own) & ((me * z.prompt_own + slot) < limit[:, None])
-    seen_own = (
-        (slot >= z.prompt_slots)
-        & (late_slot < z.decode_own)
-        & ~is_prompt[:, None]
-        & ((me * z.rows_own + late_slot % z.rows_own) == (late % z.row_total)[:, None])
-        & ((late_slot // z.rows_own) <= (late // z.row_total)[:, None])
-    )
-    extra_bias = jnp.where(seen_prompt | seen_own, 0.0, MASKED).astype(F32)
     cache_slots = key_cache.shape[1]
-    live = lax.broadcasted_iota(jnp.int32, (1, cache_slots), 1) < cache_lengths[0]
-    bias = jnp.where(live, 0.0, MASKED).astype(F32)
+    def masks(lengths, seen):
+        return call(
+            functools.partial(mask_kernel, z),
+            [shape(1, cache_slots, F32), shape(z.rows, z.slots, F32)],
+            (lengths, seen.reshape(1, z.row_total)),
+            "masks",
+            1e6,
+            smem=1,
+        )
 
     even, odd = call(
         functools.partial(project_kernel, z),
         [shape(z.project, HD, F32, pairs), shape(z.project, HD, BF16, pairs)],
         (
-            where,
+            norm_gain.reshape(z.width // 128, 128),
             prompt_in,
             step_in.reshape(z.steps * z.row_total, z.width),
-            norm_gain.reshape(1, z.width),
             query_weight,
             key_weight,
             value_weight,
         ),
         "project",
         2 * z.rows * z.width * (z.heads + 2) * HD,
-        smem=1,
+        far=5,
         scratch=[
+            pltpu.VMEM((z.prompt, z.width), BF16),
+            pltpu.VMEM((z.steps * z.row_total, z.width), BF16),
+            pltpu.VMEM((2, z.width // 2, z.heads * HD), BF16),
+            pltpu.VMEM((z.width, HD), BF16),
+            pltpu.VMEM((z.width, HD), BF16),
             pltpu.VMEM((z.rows, z.width), BF16),
+            pltpu.VMEM((z.rows, z.heads * HD), F32),
             pltpu.VMEM((z.prompt, 2 * HD), F32),
             pltpu.VMEM((z.n * z.decode_slots, 2 * HD), F32),
+            pltpu.SemaphoreType.DMA((6,)),
         ],
     )
     got = swap(odd, "ctx", n, 1)
@@ -438,22 +475,21 @@
         "pair_sum",
         1e6,
     )
+    visible, *sends = lax.optimization_barrier((visible, *sends))
     gots = [swap(send, "ctx", n, 2 * (i + 1)) for i, send in enumerate(sends)]
+    bias, extra_bias = masks(cache_lengths, visible)
+    own, bias, extra_bias = lax.optimization_barrier((own, bias, extra_bias))
     query, extra_key, extra_value = call(
         functools.partial(finish_kernel, z, z.width * n),
         [shape(z.piece, HD, BF16), shape(z.slots, HD, BF16), shape(z.slots, HD, BF16)],
-        (where, own, *gots),
+        (own, *gots),
         "finish",
         1e6,
-        smem=1,
-    )
-
-    queries = {0: query}
+    )
+
+    queries = {1: swap(query, "ctx", n, 1)}
     for i in range(1, pairs):
         queries[2 * i] = swap(query, "ctx", n, 2 * i)
-    queries[1] = swap(query, "ctx", n, 1)
-    for i in range(1, pairs):
-        queries[2 * i + 1] = swap(queries[2 * i], "ctx", n, 1)
 
     def attend(pieces, stacked, name):
         message = shape(z.message, HD, BF16)
@@ -462,14 +498,19 @@
         return call(
             functools.partial(attention_kernel, z, pieces, stacked, chunk),
             outs,
-            (where, key_cache[0], value_cache[0], bias, extra_key, extra_value, extra_bias)
+            (key_cache[0], value_cache[0], bias, extra_key, extra_value, extra_bias)
             + tuple(queries[d] for d in pieces),
             name,
             8 * len(pieces) * z.piece * cache_slots * HD,
-            smem=1,
-        )
-
-    first, first_odd = attend((0, 1), False, "attend_chip")
+            )
+
+    (first_odd,) = attend((1,), False, "attend_core")
+    first_odd, *passed = lax.optimization_barrier(
+        (first_odd, *[queries[2 * i] for i in range(1, pairs)])
+    )
+    for i in range(1, pairs):
+        queries[2 * i] = passed[i - 1]
+        queries[2 * i + 1] = swap(queries[2 * i], "ctx", n, 1)
     odd = list(range(3, n, 2))
     sets = [tuple(odd[k : k + AT_ONCE]) for k in range(0, len(odd), AT_ONCE)]
     rest_odd = [attend(pieces, True, f"attend_odd{k}")[0] for k, pieces in enumerate(sets)]
@@ -481,18 +522,21 @@
     ]
 
     message = shape(z.message, HD, BF16)
-    own, *sends = call(
+    sends = call(
         functools.partial(pair_merge_kernel, z, [len(pieces) for pieces in sets]),
-        [message] * pairs,
-        (first, got_first, *rest, *got_rest),
+        [message] * (pairs - 1),
+        (*rest, *got_rest),
         "pair_merge",
         1e6,
     )
+    query, *sends = lax.optimization_barrier((query, *sends))
     gots = [swap(send, "ctx", n, 2 * (i + 1)) for i, send in enumerate(sends)]
+    queries[0] = query
+    (own,) = attend((0,), False, "attend_own")
     (attended,) = call(
         functools.partial(final_merge_kernel, z),
         [shape(z.piece, HD, BF16)],
-        (own, *gots),
+        (own, got_first, *gots),
         "final_merge",
         1e6,
     )
@@ -508,10 +552,9 @@
     shares = call(
         functools.partial(output_kernel, z),
         [shape(share_rows, columns // 2, BF16)] * groups,
-        (where, out_weight) + tuple(heads[d] for d in range(n)),
+        (out_weight,) + tuple(heads[d] for d in range(n)),
         "output",
         2 * z.rows * z.heads * HD * columns,
-        smem=1,
         scratch=[pltpu.VMEM((z.rows, columns), F32)],
     )
     shares = [shares[0]] + [swap(shares[e], "kv", groups, e) for e in range(1, groups)]

time: 120 us -> 78 us (0.65)
  other arithmetic: 21.5 us -> 0 us
  Pallas kernels: 42.3 us -> 27.3 us
  waiting for transfers between devices: 25.6 us -> 21.4 us
  local copies, waits for them, and re-layouts: 7.51 us -> 6.06 us
    select_n x5 -> x0, other arithmetic: 15.9 us -> none  [the longest x1 15.7 us: on_device(): limit = jnp.where(is_prompt, row + 1, visible[late % z.row_total])]
    pallas_call x10 -> x12, Pallas kernels: 42.3 us -> 27.3 us  [call(): pl.pallas_call(kernel, out_shape=out_shape, in_specs=[scalar] * smem + [w...]
    gather x26 -> x0, other arithmetic: 5.44 us -> none  [on_device(): limit = jnp.where(is_prompt, row + 1, visible[late % z.row_total])]
    ppermute x26, waiting for transfers between devices: 25.6 us -> 21.4 us  [swap(): return lax.ppermute(x, axis, [(i, i ^ d) for i in range(size)])]
    gather x2 -> x0, local copies, waits for them, and re-layouts: 1.44 us -> none  [on_device(): limit = jnp.where(is_prompt, row + 1, visible[late % z.row_total])]
    unnamed x16 -> x20, local copies, waits for them, and re-layouts: 5.38 us -> 6.06 us
  transfers between devices with their start and end apart: 26 -> 26, of which waited for: 15 -> 14; matrix products, arithmetic and copies ran while one was open for 19% -> 0% of each run, Pallas kernels for 30% -> 19%
where the time goes in v2:
time: 78 us; the launch traced here: 77.7 us
  Pallas kernels  27.3 us (35%)
  starting transfers between devices  21.5 us (28%)
  waiting for transfers between devices  21.4 us (27%)
  local copies, waits for them, and re-layouts  6.06 us (8%)
  between operations  1.47 us (2%)
    pallas_call x12, Pallas kernels, call(): pl.pallas_call(kernel, out_shape=out_shape, in_specs=[scalar] * smem + [w...  27.3 us
    ppermute x26, starting transfers between devices, swap(): return lax.ppermute(x, axis, [(i, i ^ d) for i in range(size)])  21.5 us
    ppermute x26, waiting for transfers between devices, swap(): return lax.ppermute(x, axis, [(i, i ^ d) for i in range(size)])  21.4 us
    unnamed x20, local copies, waits for them, and re-layouts  6.06 us
  transfers between devices with their start and end apart: 26, of which 14 were waited for; matrix products, arithmetic and copies ran while one was open for 0% of the time, Pallas kernels for 19%

profile of v2, /device:TPU:0, one launch (start us, length us, event | category | flops | bytes accessed | tf_op | source)
XLA Modules:
  0.0 77.7 jit_solution(2740214222547625440)
XLA Ops:
  0.7 1.6 %copy-done.1 = bf16[1024,1024]{1,0:T(8,128)(2,1)S(1)} copy-done((bf16[1024,1024]{1,0:T(8,128)(2,1)S(1)}, bf16[1024,1024]{1,0:T(8,128)(2,1)}, u32[]{:S(2)}) %copy-start.1) | copy-done | bytes 2097176
  2.2 0.9 %copy-done.2 = bf16[128,1024]{1,0:T(8,128)(2,1)S(1)} copy-done((bf16[128,1024]{1,0:T(8,128)(2,1)S(1)}, bf16[128,1024]{1,0:T(8,128)(2,1)}, u32[]{:S(2)}) %copy-start.2) | copy-done | bytes 262168
  3.2 0.9 %copy-done.3 = bf16[1024,128]{1,0:T(8,128)(2,1)S(1)} copy-done((bf16[1024,128]{1,0:T(8,128)(2,1)S(1)}, bf16[1024,128]{1,0:T(8,128)(2,1)}, u32[]{:S(2)}) %copy-start.3) | copy-done | bytes 262168
  4.1 0.9 %copy-done.4 = bf16[1024,128]{1,0:T(8,128)(2,1)S(1)} copy-done((bf16[1024,128]{1,0:T(8,128)(2,1)S(1)}, bf16[1024,128]{1,0:T(8,128)(2,1)}, u32[]{:S(2)}) %copy-start.4) | copy-done | bytes 262168
  5.1 0.9 %copy-done.5 = bf16[3,32,1024]{2,1,0:T(8,128)(2,1)S(1)} copy-done((bf16[3,32,1024]{2,1,0:T(8,128)(2,1)S(1)}, bf16[3,32,1024]{2,1,0:T(8,128)(2,1)}, u32[]{:S(2)}) %copy-start.5) | copy-done | bytes 196632
  6.7 2.3 %project.1 = (f32[4,304,128]{2,1,0:T(8,128)S(1)}, bf16[4,304,128]{2,1,0:T(8,128)(2,1)S(1)}) custom-call(bf16[8,128]{1,0:T(8,128)(2,1)S(1)} %bitcast.6, bf16[128,1024]{1,0:T(8,128)(2,1)S(1)} %copy-done.2, bf16[96,1024]{1,0:T(8,128)(2,1)S(1)} %bitcast.5, bf16[1024,1024]{1,0:T(8,128)(2,1)S(1)} %copy-done.1, bf16[1024,128]{1,0:T(8,128)(2,1)S(1)} %copy-done.3, ...), custom_call_target="tpu_custom_call" | custom-call | flops 587202560 | bytes 1048576 | tf_op jit(solution)/shard_map/project/pallas_call | solution.py:79
  9.6 1.2 %collective-permute-done.got_ref = bf16[4,304,128]{2,1,0:T(8,128)(2,1)S(1)} collective-permute-done((bf16[4,304,128]{2,1,0:T(8,128)(2,1)S(1)}, bf16[4,304,128]{2,1,0:T(8,128)(2,1)S(1)}, u32[]{:S(2)}, u32[]{:S(2)}) %collective-permute-start) | collective-permute-done | bytes 311328 | tf_op jit(solution)/shard_map/ppermute | solution.py:411
  10.9 2.9 %collective-permute-start.1 = (bf16[304,128]{1,0:T(8,128)(2,1)S(1)}, bf16[304,128]{1,0:T(8,128)(2,1)S(1)}, u32[]{:S(2)}, u32[]{:S(2)}) collective-permute-start(bf16[304,128]{1,0:T(8,128)(2,1)S(1)} %get-tuple-element.46), channel_id=1, source_target_pairs={{0,8},{4,12},{8,0},{12,4},{16,24},{20,28},{24,16},{28,20},{1,9},{5... | collective-permute-start | bytes 233480 | tf_op jit(solution)/shard_map/ppermute | solution.py:411
  13.8 1.5 %collective-permute-start.2 = (bf16[304,128]{1,0:T(8,128)(2,1)S(1)}, bf16[304,128]{1,0:T(8,128)(2,1)S(1)}, u32[]{:S(2)}, u32[]{:S(2)}) collective-permute-start(bf16[304,128]{1,0:T(8,128)(2,1)S(1)} %get-tuple-element.47), channel_id=1, source_target_pairs={{0,16},{4,20},{8,24},{12,28},{16,0},{20,4},{24,8},{28,12},{1,17},{... | collective-permute-start | bytes 233480 | tf_op jit(solution)/shard_map/ppermute | solution.py:411
  16.5 1.7 %collective-permute-done.2.refs_1_ = bf16[304,128]{1,0:T(8,128)(2,1)S(1)} collective-permute-done((bf16[304,128]{1,0:T(8,128)(2,1)S(1)}, bf16[304,128]{1,0:T(8,128)(2,1)S(1)}, u32[]{:S(2)}, u32[]{:S(2)}) %collective-permute-start.2) | collective-permute-done | bytes 77856 | tf_op jit(solution)/shard_map/ppermute | solution.py:411
  18.2 2.4 %collective-permute-done.3.refs_2_ = bf16[304,128]{1,0:T(8,128)(2,1)S(1)} collective-permute-done((bf16[304,128]{1,0:T(8,128)(2,1)S(1)}, bf16[304,128]{1,0:T(8,128)(2,1)S(1)}, u32[]{:S(2)}, u32[]{:S(2)}) %collective-permute-start.3) | collective-permute-done | bytes 77856 | tf_op jit(solution)/shard_map/ppermute | solution.py:411
  22.1 2.3 %collective-permute-start.7 = (bf16[224,128]{1,0:T(8,128)(2,1)S(1)}, bf16[224,128]{1,0:T(8,128)(2,1)S(1)}, u32[]{:S(2)}, u32[]{:S(2)}) collective-permute-start(bf16[224,128]{1,0:T(8,128)(2,1)S(1)} %get-tuple-element.59.refs_6_), channel_id=1, source_target_pairs={{0,24},{4,28},{8,16},{12,20},{16,8},{20,12},{24,0},{28,4},{1,25},{... | collective-permute-start | bytes 172040 | tf_op jit(solution)/shard_map/ppermute | solution.py:411
  24.4 3.0 %attend_core.1 = bf16[240,128]{1,0:T(8,128)(2,1)S(1)} custom-call(bf16[8192,128]{1,0:T(8,128)(2,1)S(1)} %bitcast.7, bf16[8192,128]{1,0:T(8,128)(2,1)S(1)} %bitcast.11, f32[1,8192]{1,0:T(1,128)S(1)} %get-tuple-element.44.refs_2_, bf16[32,128]{1,0:T(8,128)(2,1)S(1)} %get-tuple-element.49.refs_3_, bf16[32,128]{1,0:T(8,128)(2,1)S(1)} %get-tuple-element.50.refs_4_, ...), custom_call_target="tpu_custom_call" | custom-call | flops 1879048192 | bytes 1048576 | tf_op jit(solution)/shard_map/attend_core/pallas_call | solution.py:79
  29.2 8.3 %attend_odd0.1 = bf16[3,240,128]{2,1,0:T(8,128)(2,1)S(1)} custom-call(bf16[8192,128]{1,0:T(8,128)(2,1)S(1)} %bitcast.8, bf16[8192,128]{1,0:T(8,128)(2,1)S(1)} %bitcast.12, f32[1,8192]{1,0:T(1,128)S(1)} %get-tuple-element.44.refs_2_, bf16[32,128]{1,0:T(8,128)(2,1)S(1)} %get-tuple-element.49.refs_3_, bf16[32,128]{1,0:T(8,128)(2,1)S(1)} %get-tuple-element.50.refs_4_, ...), custom_call_target="tpu_custom_call" | custom-call | flops 5637144576 | bytes 1048576 | tf_op jit(solution)/shard_map/attend_odd0/pallas_call | solution.py:79
  37.8 8.1 %attend_even0.1.refs_0_ = bf16[3,240,128]{2,1,0:T(8,128)(2,1)S(1)} custom-call(bf16[8192,128]{1,0:T(8,128)(2,1)S(1)} %bitcast.9, bf16[8192,128]{1,0:T(8,128)(2,1)S(1)} %bitcast.13, f32[1,8192]{1,0:T(1,128)S(1)} %get-tuple-element.44.refs_2_, bf16[32,128]{1,0:T(8,128)(2,1)S(1)} %get-tuple-element.49.refs_3_, bf16[32,128]{1,0:T(8,128)(2,1)S(1)} %get-tuple-element.50.refs_4_, ...), custom_call_target="tpu_custom_call" | custom-call | flops 5637144576 | bytes 1048576 | tf_op jit(solution)/shard_map/attend_even0/pallas_call | solution.py:79
  46.7 1.4 %collective-permute-start.13 = (bf16[240,128]{1,0:T(8,128)(2,1)S(1)}, bf16[240,128]{1,0:T(8,128)(2,1)S(1)}, u32[]{:S(2)}, u32[]{:S(2)}) collective-permute-start(bf16[240,128]{1,0:T(8,128)(2,1)S(1)} %get-tuple-element.61), channel_id=1, source_target_pairs={{0,8},{4,12},{8,0},{12,4},{16,24},{20,28},{24,16},{28,20},{1,9},{5... | collective-permute-start | bytes 184328 | tf_op jit(solution)/shard_map/ppermute | solution.py:411
  48.1 1.2 %collective-permute-start.14 = (bf16[240,128]{1,0:T(8,128)(2,1)S(1)}, bf16[240,128]{1,0:T(8,128)(2,1)S(1)}, u32[]{:S(2)}, u32[]{:S(2)}) collective-permute-start(bf16[240,128]{1,0:T(8,128)(2,1)S(1)} %get-tuple-element.62), channel_id=1, source_target_pairs={{0,16},{4,20},{8,24},{12,28},{16,0},{20,4},{24,8},{28,12},{1,17},{... | collective-permute-start | bytes 184328 | tf_op jit(solution)/shard_map/ppermute | solution.py:411
  49.4 0.9 %collective-permute-start.15 = (bf16[240,128]{1,0:T(8,128)(2,1)S(1)}, bf16[240,128]{1,0:T(8,128)(2,1)S(1)}, u32[]{:S(2)}, u32[]{:S(2)}) collective-permute-start(bf16[240,128]{1,0:T(8,128)(2,1)S(1)} %get-tuple-element.63), channel_id=1, source_target_pairs={{0,24},{4,28},{8,16},{12,20},{16,8},{20,12},{24,0},{28,4},{1,25},{... | collective-permute-start | bytes 184328 | tf_op jit(solution)/shard_map/ppermute | solution.py:411
  50.3 2.9 %attend_own.1.refs_0_ = bf16[240,128]{1,0:T(8,128)(2,1)S(1)} custom-call(bf16[8192,128]{1,0:T(8,128)(2,1)S(1)} %bitcast.10, bf16[8192,128]{1,0:T(8,128)(2,1)S(1)} %bitcast.14, f32[1,8192]{1,0:T(1,128)S(1)} %get-tuple-element.44.refs_2_, bf16[32,128]{1,0:T(8,128)(2,1)S(1)} %get-tuple-element.49.refs_3_, bf16[32,128]{1,0:T(8,128)(2,1)S(1)} %get-tuple-element.50.refs_4_, ...), custom_call_target="tpu_custom_call" | custom-call | flops 1879048192 | bytes 1048576 | tf_op jit(solution)/shard_map/attend_own/pallas_call | solution.py:79
  53.3 1.2 %collective-permute-done.15.refs_4_ = bf16[240,128]{1,0:T(8,128)(2,1)S(1)} collective-permute-done((bf16[240,128]{1,0:T(8,128)(2,1)S(1)}, bf16[240,128]{1,0:T(8,128)(2,1)S(1)}, u32[]{:S(2)}, u32[]{:S(2)}) %collective-permute-start.15) | collective-permute-done | bytes 61472 | tf_op jit(solution)/shard_map/ppermute | solution.py:411
  55.6 0.9 %collective-permute-start.19 = (bf16[224,128]{1,0:T(8,128)(2,1)S(1)}, bf16[224,128]{1,0:T(8,128)(2,1)S(1)}, u32[]{:S(2)}, u32[]{:S(2)}) collective-permute-start(bf16[224,128]{1,0:T(8,128)(2,1)S(1)} %final_merge.1.refs_0_), channel_id=1, source_target_pairs={{0,16},{4,20},{8,24},{12,28},{16,0},{20,4},{24,8},{28,12},{1,17},{... | collective-permute-start | bytes 172040 | tf_op jit(solution)/shard_map/ppermute | solution.py:411
  56.5 2.0 %collective-permute-start.21 = (bf16[224,128]{1,0:T(8,128)(2,1)S(1)}, bf16[224,128]{1,0:T(8,128)(2,1)S(1)}, u32[]{:S(2)}, u32[]{:S(2)}) collective-permute-start(bf16[224,128]{1,0:T(8,128)(2,1)S(1)} %final_merge.1.refs_0_), channel_id=1, source_target_pairs={{0,24},{4,28},{8,16},{12,20},{16,8},{20,12},{24,0},{28,4},{1,25},{... | collective-permute-start | bytes 172040 | tf_op jit(solution)/shard_map/ppermute | solution.py:411
  58.5 0.7 collective-permute-done.17.refs_2_
  59.2 0.8 %collective-permute-done.19.refs_4_ = bf16[224,128]{1,0:T(8,128)(2,1)S(1)} collective-permute-done((bf16[224,128]{1,0:T(8,128)(2,1)S(1)}, bf16[224,128]{1,0:T(8,128)(2,1)S(1)}, u32[]{:S(2)}, u32[]{:S(2)}) %collective-permute-start.19) | collective-permute-done | bytes 57376 | tf_op jit(solution)/shard_map/ppermute | solution.py:411
  60.0 1.5 %collective-permute-done.21.refs_6_ = bf16[224,128]{1,0:T(8,128)(2,1)S(1)} collective-permute-done((bf16[224,128]{1,0:T(8,128)(2,1)S(1)}, bf16[224,128]{1,0:T(8,128)(2,1)S(1)}, u32[]{:S(2)}, u32[]{:S(2)}) %collective-permute-start.21) | collective-permute-done | bytes 57376 | tf_op jit(solution)/shard_map/ppermute | solution.py:411
  61.6 1.2 %collective-permute-done.22.refs_7_ = bf16[224,128]{1,0:T(8,128)(2,1)S(1)} collective-permute-done((bf16[224,128]{1,0:T(8,128)(2,1)S(1)}, bf16[224,128]{1,0:T(8,128)(2,1)S(1)}, u32[]{:S(2)}, u32[]{:S(2)}) %collective-permute-start.22) | collective-permute-done | bytes 57376 | tf_op jit(solution)/shard_map/ppermute | solution.py:411
  62.8 0.7 output.1
  63.5 1.7 %collective-permute-start.23 = (bf16[112,512]{1,0:T(8,128)(2,1)S(1)}, bf16[112,512]{1,0:T(8,128)(2,1)S(1)}, u32[]{:S(2)}, u32[]{:S(2)}) collective-permute-start(bf16[112,512]{1,0:T(8,128)(2,1)S(1)} %get-tuple-element.65), channel_id=1, source_target_pairs={{0,1},{1,0},{2,3},{3,2},{4,5},{5,4},{6,7},{7,6},{8,9},{9,8},{10,11... | collective-permute-start | bytes 344072 | tf_op jit(solution)/shard_map/ppermute | solution.py:411
  65.2 2.6 %collective-permute-start.24 = (bf16[112,512]{1,0:T(8,128)(2,1)S(1)}, bf16[112,512]{1,0:T(8,128)(2,1)S(1)}, u32[]{:S(2)}, u32[]{:S(2)}) collective-permute-start(bf16[112,512]{1,0:T(8,128)(2,1)S(1)} %get-tuple-element.66), channel_id=1, source_target_pairs={{0,2},{1,3},{2,0},{3,1},{4,6},{5,7},{6,4},{7,5},{8,10},{9,11},{10,... | collective-permute-start | bytes 344072 | tf_op jit(solution)/shard_map/ppermute | solution.py:411
  68.0 2.3 %collective-permute-done.23.refs_1_ = bf16[112,512]{1,0:T(8,128)(2,1)S(1)} collective-permute-done((bf16[112,512]{1,0:T(8,128)(2,1)S(1)}, bf16[112,512]{1,0:T(8,128)(2,1)S(1)}, u32[]{:S(2)}, u32[]{:S(2)}) %collective-permute-start.23) | collective-permute-done | bytes 114720 | tf_op jit(solution)/shard_map/ppermute | solution.py:411
  70.3 6.7 %collective-permute-done.24.refs_2_ = bf16[112,512]{1,0:T(8,128)(2,1)S(1)} collective-permute-done((bf16[112,512]{1,0:T(8,128)(2,1)S(1)}, bf16[112,512]{1,0:T(8,128)(2,1)S(1)}, u32[]{:S(2)}, u32[]{:S(2)}) %collective-permute-start.24) | collective-permute-done | bytes 114720 | tf_op jit(solution)/shard_map/ppermute | solution.py:411
  77.0 0.7 share_sum.1
  (52 shorter events, 7.5 us)
Async XLA Ops:
  0.6 15.4 %copy-start.9 = (s32[32]{0:T(128)S(1)}, s32[32]{0:T(128)}, u32[]{:S(2)}) copy-start(s32[32]{0:T(128)} %param.21) | copy-start | bytes 388
  0.6 1.6 %copy-start.1 = (bf16[1024,1024]{1,0:T(8,128)(2,1)S(1)}, bf16[1024,1024]{1,0:T(8,128)(2,1)}, u32[]{:S(2)}) copy-start(bf16[1024,1024]{1,0:T(8,128)(2,1)} %wq_hbm.1) | copy-start | bytes 6291460
  2.2 0.9 %copy-start.2 = (bf16[128,1024]{1,0:T(8,128)(2,1)S(1)}, bf16[128,1024]{1,0:T(8,128)(2,1)}, u32[]{:S(2)}) copy-start(bf16[128,1024]{1,0:T(8,128)(2,1)} %xp_hbm.1) | copy-start | bytes 786436
  6.7 17.7 %copy-start.7 = (bf16[1,8192,128]{2,1,0:T(8,128)(2,1)S(1)}, bf16[1,8192,128]{2,1,0:T(8,128)(2,1)}, u32[]{:S(2)}) copy-start(bf16[1,8192,128]{2,1,0:T(8,128)(2,1)} %param.18) | copy-start | bytes 6291460
  6.7 17.7 %copy-start.8 = (bf16[1,8192,128]{2,1,0:T(8,128)(2,1)S(1)}, bf16[1,8192,128]{2,1,0:T(8,128)(2,1)}, u32[]{:S(2)}) copy-start(bf16[1,8192,128]{2,1,0:T(8,128)(2,1)} %param.19) | copy-start | bytes 6291460
  9.0 1.8 %collective-permute-start = (bf16[4,304,128]{2,1,0:T(8,128)(2,1)S(1)}, bf16[4,304,128]{2,1,0:T(8,128)(2,1)S(1)}, u32[]{:S(2)}, u32[]{:S(2)}) collective-permute-start(bf16[4,304,128]{2,1,0:T(8,128)(2,1)S(1)} %get-tuple-element.36), channel_id=1, source_target_pairs={{0,4},{4,0},{8,12},{12,8},{16,20},{20,16},{24,28},{28,24},{1,5},{5... | collective-permute-start | bytes 933896 | tf_op jit(solution)/shard_map/ppermute | solution.py:411
  10.9 5.6 %collective-permute-start.1 = (bf16[304,128]{1,0:T(8,128)(2,1)S(1)}, bf16[304,128]{1,0:T(8,128)(2,1)S(1)}, u32[]{:S(2)}, u32[]{:S(2)}) collective-permute-start(bf16[304,128]{1,0:T(8,128)(2,1)S(1)} %get-tuple-element.46), channel_id=1, source_target_pairs={{0,8},{4,12},{8,0},{12,4},{16,24},{20,28},{24,16},{28,20},{1,9},{5... | collective-permute-start | bytes 233480 | tf_op jit(solution)/shard_map/ppermute | solution.py:411
  13.8 4.4 %collective-permute-start.2 = (bf16[304,128]{1,0:T(8,128)(2,1)S(1)}, bf16[304,128]{1,0:T(8,128)(2,1)S(1)}, u32[]{:S(2)}, u32[]{:S(2)}) collective-permute-start(bf16[304,128]{1,0:T(8,128)(2,1)S(1)} %get-tuple-element.47), channel_id=1, source_target_pairs={{0,16},{4,20},{8,24},{12,28},{16,0},{20,4},{24,8},{28,12},{1,17},{... | collective-permute-start | bytes 233480 | tf_op jit(solution)/shard_map/ppermute | solution.py:411
  15.3 5.3 %collective-permute-start.3 = (bf16[304,128]{1,0:T(8,128)(2,1)S(1)}, bf16[304,128]{1,0:T(8,128)(2,1)S(1)}, u32[]{:S(2)}, u32[]{:S(2)}) collective-permute-start(bf16[304,128]{1,0:T(8,128)(2,1)S(1)} %get-tuple-element.48), channel_id=1, source_target_pairs={{0,24},{4,28},{8,16},{12,20},{16,8},{20,12},{24,0},{28,4},{1,25},{... | collective-permute-start | bytes 233480 | tf_op jit(solution)/shard_map/ppermute | solution.py:411
  20.8 3.6 %collective-permute-start.4 = (bf16[224,128]{1,0:T(8,128)(2,1)S(1)}, bf16[224,128]{1,0:T(8,128)(2,1)S(1)}, u32[]{:S(2)}, u32[]{:S(2)}) collective-permute-start(bf16[224,128]{1,0:T(8,128)(2,1)S(1)} %get-tuple-element.59.refs_6_), channel_id=1, source_target_pairs={{0,4},{4,0},{8,12},{12,8},{16,20},{20,16},{24,28},{28,24},{1,5},{5... | collective-permute-start | bytes 172040 | tf_op jit(solution)/shard_map/ppermute | solution.py:411
  20.9 6.5 %collective-permute-start.5 = (bf16[224,128]{1,0:T(8,128)(2,1)S(1)}, bf16[224,128]{1,0:T(8,128)(2,1)S(1)}, u32[]{:S(2)}, u32[]{:S(2)}) collective-permute-start(bf16[224,128]{1,0:T(8,128)(2,1)S(1)} %get-tuple-element.59.refs_6_), channel_id=1, source_target_pairs={{0,8},{4,12},{8,0},{12,4},{16,24},{20,28},{24,16},{28,20},{1,9},{5... | collective-permute-start | bytes 172040 | tf_op jit(solution)/shard_map/ppermute | solution.py:411
  21.5 5.9 %collective-permute-start.6 = (bf16[224,128]{1,0:T(8,128)(2,1)S(1)}, bf16[224,128]{1,0:T(8,128)(2,1)S(1)}, u32[]{:S(2)}, u32[]{:S(2)}) collective-permute-start(bf16[224,128]{1,0:T(8,128)(2,1)S(1)} %get-tuple-element.59.refs_6_), channel_id=1, source_target_pairs={{0,16},{4,20},{8,24},{12,28},{16,0},{20,4},{24,8},{28,12},{1,17},{... | collective-permute-start | bytes 172040 | tf_op jit(solution)/shard_map/ppermute | solution.py:411
  22.1 5.3 %collective-permute-start.7 = (bf16[224,128]{1,0:T(8,128)(2,1)S(1)}, bf16[224,128]{1,0:T(8,128)(2,1)S(1)}, u32[]{:S(2)}, u32[]{:S(2)}) collective-permute-start(bf16[224,128]{1,0:T(8,128)(2,1)S(1)} %get-tuple-element.59.refs_6_), channel_id=1, source_target_pairs={{0,24},{4,28},{8,16},{12,20},{16,8},{20,12},{24,0},{28,4},{1,25},{... | collective-permute-start | bytes 172040 | tf_op jit(solution)/shard_map/ppermute | solution.py:411
  27.4 1.3 %collective-permute-start.10 = (bf16[224,128]{1,0:T(8,128)(2,1)S(1)}, bf16[224,128]{1,0:T(8,128)(2,1)S(1)}, u32[]{:S(2)}, u32[]{:S(2)}) collective-permute-start(bf16[224,128]{1,0:T(8,128)(2,1)S(1)} %collective-permute-done.7.refs_8_), channel_id=1, source_target_pairs={{0,4},{4,0},{8,12},{12,8},{16,20},{20,16},{24,28},{28,24},{1,5},{5... | collective-permute-start | bytes 172040 | tf_op jit(solution)/shard_map/ppermute | solution.py:411
  27.5 1.4 %collective-permute-start.8 = (bf16[224,128]{1,0:T(8,128)(2,1)S(1)}, bf16[224,128]{1,0:T(8,128)(2,1)S(1)}, u32[]{:S(2)}, u32[]{:S(2)}) collective-permute-start(bf16[224,128]{1,0:T(8,128)(2,1)S(1)} %collective-permute-done.5.refs_6_), channel_id=1, source_target_pairs={{0,4},{4,0},{8,12},{12,8},{16,20},{20,16},{24,28},{28,24},{1,5},{5... | collective-permute-start | bytes 172040 | tf_op jit(solution)/shard_map/ppermute | solution.py:411
  28.0 1.2 %collective-permute-start.9 = (bf16[224,128]{1,0:T(8,128)(2,1)S(1)}, bf16[224,128]{1,0:T(8,128)(2,1)S(1)}, u32[]{:S(2)}, u32[]{:S(2)}) collective-permute-start(bf16[224,128]{1,0:T(8,128)(2,1)S(1)} %collective-permute-done.6.refs_7_), channel_id=1, source_target_pairs={{0,4},{4,0},{8,12},{12,8},{16,20},{20,16},{24,28},{28,24},{1,5},{5... | collective-permute-start | bytes 172040 | tf_op jit(solution)/shard_map/ppermute | solution.py:411
  37.5 8.7 %collective-permute-start.11 = (bf16[3,240,128]{2,1,0:T(8,128)(2,1)S(1)}, bf16[3,240,128]{2,1,0:T(8,128)(2,1)S(1)}, u32[]{:S(2)}, u32[]{:S(2)}) collective-permute-start(bf16[3,240,128]{2,1,0:T(8,128)(2,1)S(1)} %attend_odd0.1), channel_id=1, source_target_pairs={{0,4},{4,0},{8,12},{12,8},{16,20},{20,16},{24,28},{28,24},{1,5},{5... | collective-permute-start | bytes 552968 | tf_op jit(solution)/shard_map/ppermute | solution.py:411
  45.9 7.4 %collective-permute-start.12 = (bf16[240,128]{1,0:T(8,128)(2,1)S(1)}, bf16[240,128]{1,0:T(8,128)(2,1)S(1)}, u32[]{:S(2)}, u32[]{:S(2)}) collective-permute-start(bf16[240,128]{1,0:T(8,128)(2,1)S(1)} %attend_core.1), channel_id=1, source_target_pairs={{0,4},{4,0},{8,12},{12,8},{16,20},{20,16},{24,28},{28,24},{1,5},{5... | collective-permute-start | bytes 184328 | tf_op jit(solution)/shard_map/ppermute | solution.py:411
  46.7 16.1 %copy-start = (bf16[1024,1024]{1,0:T(8,128)(2,1)S(1)}, bf16[1024,1024]{1,0:T(8,128)(2,1)}, u32[]{:S(2)}) copy-start(bf16[1024,1024]{1,0:T(8,128)(2,1)} %weight_ref.1) | copy-start | bytes 6291460
  46.7 6.5 %collective-permute-start.13 = (bf16[240,128]{1,0:T(8,128)(2,1)S(1)}, bf16[240,128]{1,0:T(8,128)(2,1)S(1)}, u32[]{:S(2)}, u32[]{:S(2)}) collective-permute-start(bf16[240,128]{1,0:T(8,128)(2,1)S(1)} %get-tuple-element.61), channel_id=1, source_target_pairs={{0,8},{4,12},{8,0},{12,4},{16,24},{20,28},{24,16},{28,20},{1,9},{5... | collective-permute-start | bytes 184328 | tf_op jit(solution)/shard_map/ppermute | solution.py:411
  48.1 5.1 %collective-permute-start.14 = (bf16[240,128]{1,0:T(8,128)(2,1)S(1)}, bf16[240,128]{1,0:T(8,128)(2,1)S(1)}, u32[]{:S(2)}, u32[]{:S(2)}) collective-permute-start(bf16[240,128]{1,0:T(8,128)(2,1)S(1)} %get-tuple-element.62), channel_id=1, source_target_pairs={{0,16},{4,20},{8,24},{12,28},{16,0},{20,4},{24,8},{28,12},{1,17},{... | collective-permute-start | bytes 184328 | tf_op jit(solution)/shard_map/ppermute | solution.py:411
  49.4 5.1 %collective-permute-start.15 = (bf16[240,128]{1,0:T(8,128)(2,1)S(1)}, bf16[240,128]{1,0:T(8,128)(2,1)S(1)}, u32[]{:S(2)}, u32[]{:S(2)}) collective-permute-start(bf16[240,128]{1,0:T(8,128)(2,1)S(1)} %get-tuple-element.63), channel_id=1, source_target_pairs={{0,24},{4,28},{8,16},{12,20},{16,8},{20,12},{24,0},{28,4},{1,25},{... | collective-permute-start | bytes 184328 | tf_op jit(solution)/shard_map/ppermute | solution.py:411
  55.0 4.2 %collective-permute-start.17 = (bf16[224,128]{1,0:T(8,128)(2,1)S(1)}, bf16[224,128]{1,0:T(8,128)(2,1)S(1)}, u32[]{:S(2)}, u32[]{:S(2)}) collective-permute-start(bf16[224,128]{1,0:T(8,128)(2,1)S(1)} %final_merge.1.refs_0_), channel_id=1, source_target_pairs={{0,8},{4,12},{8,0},{12,4},{16,24},{20,28},{24,16},{28,20},{1,9},{5... | collective-permute-start | bytes 172040 | tf_op jit(solution)/shard_map/ppermute | solution.py:411
  55.6 4.5 %collective-permute-start.19 = (bf16[224,128]{1,0:T(8,128)(2,1)S(1)}, bf16[224,128]{1,0:T(8,128)(2,1)S(1)}, u32[]{:S(2)}, u32[]{:S(2)}) collective-permute-start(bf16[224,128]{1,0:T(8,128)(2,1)S(1)} %final_merge.1.refs_0_), channel_id=1, source_target_pairs={{0,16},{4,20},{8,24},{12,28},{16,0},{20,4},{24,8},{28,12},{1,17},{... | collective-permute-start | bytes 172040 | tf_op jit(solution)/shard_map/ppermute | solution.py:411
  56.5 5.1 %collective-permute-start.21 = (bf16[224,128]{1,0:T(8,128)(2,1)S(1)}, bf16[224,128]{1,0:T(8,128)(2,1)S(1)}, u32[]{:S(2)}, u32[]{:S(2)}) collective-permute-start(bf16[224,128]{1,0:T(8,128)(2,1)S(1)} %final_merge.1.refs_0_), channel_id=1, source_target_pairs={{0,24},{4,28},{8,16},{12,20},{16,8},{20,12},{24,0},{28,4},{1,25},{... | collective-permute-start | bytes 172040 | tf_op jit(solution)/shard_map/ppermute | solution.py:411
  58.5 3.1 %collective-permute-start.16 = (bf16[224,128]{1,0:T(8,128)(2,1)S(1)}, bf16[224,128]{1,0:T(8,128)(2,1)S(1)}, u32[]{:S(2)}, u32[]{:S(2)}) collective-permute-start(bf16[224,128]{1,0:T(8,128)(2,1)S(1)} %final_merge.1.refs_0_), channel_id=1, source_target_pairs={{0,4},{4,0},{8,12},{12,8},{16,20},{20,16},{24,28},{28,24},{1,5},{5... | collective-permute-start | bytes 172040 | tf_op jit(solution)/shard_map/ppermute | solution.py:411
  59.2 2.4 %collective-permute-start.18 = (bf16[224,128]{1,0:T(8,128)(2,1)S(1)}, bf16[224,128]{1,0:T(8,128)(2,1)S(1)}, u32[]{:S(2)}, u32[]{:S(2)}) collective-permute-start(bf16[224,128]{1,0:T(8,128)(2,1)S(1)} %collective-permute-done.17.refs_2_), channel_id=1, source_target_pairs={{0,4},{4,0},{8,12},{12,8},{16,20},{20,16},{24,28},{28,24},{1,5},{5... | collective-permute-start | bytes 172040 | tf_op jit(solution)/shard_map/ppermute | solution.py:411
  60.0 1.6 %collective-permute-start.20 = (bf16[224,128]{1,0:T(8,128)(2,1)S(1)}, bf16[224,128]{1,0:T(8,128)(2,1)S(1)}, u32[]{:S(2)}, u32[]{:S(2)}) collective-permute-start(bf16[224,128]{1,0:T(8,128)(2,1)S(1)} %collective-permute-done.19.refs_4_), channel_id=1, source_target_pairs={{0,4},{4,0},{8,12},{12,8},{16,20},{20,16},{24,28},{28,24},{1,5},{5... | collective-permute-start | bytes 172040 | tf_op jit(solution)/shard_map/ppermute | solution.py:411
  61.6 1.2 %collective-permute-start.22 = (bf16[224,128]{1,0:T(8,128)(2,1)S(1)}, bf16[224,128]{1,0:T(8,128)(2,1)S(1)}, u32[]{:S(2)}, u32[]{:S(2)}) collective-permute-start(bf16[224,128]{1,0:T(8,128)(2,1)S(1)} %collective-permute-done.21.refs_6_), channel_id=1, source_target_pairs={{0,4},{4,0},{8,12},{12,8},{16,20},{20,16},{24,28},{28,24},{1,5},{5... | collective-permute-start | bytes 172040 | tf_op jit(solution)/shard_map/ppermute | solution.py:411
  63.5 6.8 %collective-permute-start.23 = (bf16[112,512]{1,0:T(8,128)(2,1)S(1)}, bf16[112,512]{1,0:T(8,128)(2,1)S(1)}, u32[]{:S(2)}, u32[]{:S(2)}) collective-permute-start(bf16[112,512]{1,0:T(8,128)(2,1)S(1)} %get-tuple-element.65), channel_id=1, source_target_pairs={{0,1},{1,0},{2,3},{3,2},{4,5},{5,4},{6,7},{7,6},{8,9},{9,8},{10,11... | collective-permute-start | bytes 344072 | tf_op jit(solution)/shard_map/ppermute | solution.py:411
  65.2 11.8 %collective-permute-start.24 = (bf16[112,512]{1,0:T(8,128)(2,1)S(1)}, bf16[112,512]{1,0:T(8,128)(2,1)S(1)}, u32[]{:S(2)}, u32[]{:S(2)}) collective-permute-start(bf16[112,512]{1,0:T(8,128)(2,1)S(1)} %get-tuple-element.66), channel_id=1, source_target_pairs={{0,2},{1,3},{2,0},{3,1},{4,6},{5,7},{6,4},{7,5},{8,10},{9,11},{10,... | collective-permute-start | bytes 344072 | tf_op jit(solution)/shard_map/ppermute | solution.py:411
  67.8 9.2 %collective-permute-start.25 = (bf16[112,512]{1,0:T(8,128)(2,1)S(1)}, bf16[112,512]{1,0:T(8,128)(2,1)S(1)}, u32[]{:S(2)}, u32[]{:S(2)}) collective-permute-start(bf16[112,512]{1,0:T(8,128)(2,1)S(1)} %get-tuple-element.67), channel_id=1, source_target_pairs={{0,3},{1,2},{2,1},{3,0},{4,7},{5,6},{6,5},{7,4},{8,11},{9,10},{10,... | collective-permute-start | bytes 344072 | tf_op jit(solution)/shard_map/ppermute | solution.py:411
  (4 other events, 3.5 us)

commit v3 on v2

--- a/solution.py
+++ b/solution.py
@@ -76,11 +76,15 @@
 def call(kernel, out_shape, args, name, flops, smem=0, far=0, grant=VMEM_BYTES, scratch=()):
     whole = pl.BlockSpec(memory_space=pltpu.VMEM)
     scalar = pl.BlockSpec(memory_space=pltpu.SMEM)
+    near = len(args) - far
+    args = args[:near] + tuple(
+        pltpu.with_memory_space_constraint(x, pltpu.HBM) for x in args[near:]
+    )
     return pl.pallas_call(
         kernel,
         out_shape=out_shape,
         in_specs=[scalar] * smem
-        + [whole] * (len(args) - smem - far)
+        + [whole] * (near - smem)
         + [pl.BlockSpec(memory_space=pltpu.HBM)] * far,
         out_specs=jax.tree.map(lambda _: whole, out_shape),
         scratch_shapes=list(scratch),
@@ -120,7 +124,7 @@
         self.project = self.piece + 2 * self.slots + STAT_ROWS
 
 
-def project_kernel(z, gain_ref, xp_hbm, xs_hbm, wq_hbm, wk_hbm, wv_hbm, even_ref, odd_ref, xp_ref, xs_ref, wq_ref, wk_ref, wv_ref, scaled_ref, query_ref, kvp_ref, kvd_ref, sems):
+def project_kernel(z, gain_hbm, xp_hbm, xs_hbm, wq_hbm, wk_hbm, wv_hbm, even_ref, odd_ref, gain_ref, xp_ref, xs_ref, wq_ref, wk_ref, wv_ref, scaled_ref, query_ref, kvp_ref, kvd_ref, sems):
     me = lax.axis_index("ctx")
     depth = z.width // 2
     loads = [
@@ -133,8 +137,11 @@
         pltpu.make_async_copy(wq_hbm.at[pl.ds(k * depth, depth), :], wq_ref.at[k], sems.at[4 + k])
         for k in range(2)
     ]
-    for load in loads:
+    loads.append(pltpu.make_async_copy(gain_hbm, gain_ref, sems.at[6]))
+    loads[6].start()
+    for load in loads[:6]:
         load.start()
+    loads[6].wait()
     gain = gain_ref[...].astype(F32)
     gain = jnp.concatenate([gain[k : k + 1, :] for k in range(gain.shape[0])], axis=1)
     squares = []
@@ -327,13 +334,14 @@
     return highest, total, mixed
 
 
-def pair_merge_kernel(z, sets, *refs):
-    mine_refs = refs[: len(sets)]
-    got_refs = refs[len(sets) : 2 * len(sets)]
-    send_refs = refs[2 * len(sets) :]
-    places = [(s, k) for s, size in enumerate(sets) for k in range(size)]
-    for send_ref, (s, k) in zip(send_refs, places):
-        highest, total, mixed = merge(z, [mine_refs[s][k], got_refs[s][k]])
+def pair_merge_kernel(z, mine_sets, got_sets, *refs):
+    count = len(mine_sets) + len(got_sets)
+    places = [
+        [ref.at[k] for ref, size in zip(block, sizes) for k in range(size)]
+        for block, sizes in ((refs, mine_sets), (refs[len(mine_sets) :], got_sets))
+    ]
+    for send_ref, mine_ref, got_ref in zip(refs[count:], *places):
+        highest, total, mixed = merge(z, [mine_ref[...], got_ref[...]])
         send_ref[...] = jnp.concatenate([mixed, stack_stats([highest, total])], axis=0).astype(BF16)
 
 
@@ -344,13 +352,14 @@
     out_ref[...] = (mixed / rows_to_column(total, index)).astype(BF16)
 
 
+def share_order(groups):
+    return list(range(2, groups)) + [1, 0]
+
+
 def output_kernel(z, weight_ref, *refs):
     piece_refs = refs[: z.n]
-    out_refs = refs[z.n : z.n + z.groups]
-    sum_ref = refs[-1]
+    *out_refs, sum_ref = refs[z.n :]
     me = lax.axis_index("ctx")
-    place = lax.axis_index("kv")
-    columns = weight_ref.shape[1]
     if z.halves > 1:
         sum_ref[...] = jnp.zeros_like(sum_ref)
     total = None
@@ -375,16 +384,18 @@
             sum_ref[where, :] = sum_ref[where, :] + product
     if z.halves == 1:
         sum_ref[...] = total
+    place = lax.axis_index("kv")
+    columns = sum_ref.shape[1]
     prompt_share = z.prompt // z.groups
     step_share = z.row_total // z.groups
-    for e in range(z.groups):
+    for out_ref, e in zip(out_refs, share_order(z.groups)):
         target = jnp.bitwise_xor(place, e)
         rows = [sum_ref[pl.ds(pl.multiple_of(target * prompt_share, 8), prompt_share), :]]
         for s in range(z.steps):
             start = z.prompt + s * z.row_total + target * step_share
             rows.append(sum_ref[pl.ds(pl.multiple_of(start, 8), step_share), :])
         share = jnp.concatenate(rows, axis=0)
-        out_refs[e][...] = jnp.concatenate(
+        out_ref[...] = jnp.concatenate(
             [share[:, : columns // 2], share[:, columns // 2 :]], axis=0
         ).astype(BF16)
 
@@ -453,8 +464,9 @@
         ),
         "project",
         2 * z.rows * z.width * (z.heads + 2) * HD,
-        far=5,
+        far=6,
         scratch=[
+            pltpu.VMEM((z.width // 128, 128), BF16),
             pltpu.VMEM((z.prompt, z.width), BF16),
             pltpu.VMEM((z.steps * z.row_total, z.width), BF16),
             pltpu.VMEM((2, z.width // 2, z.heads * HD), BF16),
@@ -464,7 +476,7 @@
             pltpu.VMEM((z.rows, z.heads * HD), F32),
             pltpu.VMEM((z.prompt, 2 * HD), F32),
             pltpu.VMEM((z.n * z.decode_slots, 2 * HD), F32),
-            pltpu.SemaphoreType.DMA((6,)),
+            pltpu.SemaphoreType.DMA((7,)),
         ],
     )
     got = swap(odd, "ctx", n, 1)
@@ -511,19 +523,25 @@
     for i in range(1, pairs):
         queries[2 * i] = passed[i - 1]
         queries[2 * i + 1] = swap(queries[2 * i], "ctx", n, 1)
-    odd = list(range(3, n, 2))
-    sets = [tuple(odd[k : k + AT_ONCE]) for k in range(0, len(odd), AT_ONCE)]
-    rest_odd = [attend(pieces, True, f"attend_odd{k}")[0] for k, pieces in enumerate(sets)]
+    odd = [tuple(range(3, n, 2)[k : k + AT_ONCE]) for k in range(0, pairs - 1, AT_ONCE)]
+    even = [(2,)] + [
+        tuple(range(4, n, 2)[k : k + AT_ONCE]) for k in range(0, pairs - 2, AT_ONCE)
+    ]
+    early = attend(even[0], True, "attend_near")
+    early, *passed = lax.optimization_barrier((early, *[queries[d] for d in range(3, n, 2)]))
+    queries.update(zip(range(3, n, 2), passed))
+    rest_odd = [attend(pieces, True, f"attend_odd{k}")[0] for k, pieces in enumerate(odd)]
     got_first = swap(first_odd, "ctx", n, 1)
     got_rest = [swap(block, "ctx", n, 1) for block in rest_odd]
-    rest = [
-        attend(tuple(d - 1 for d in pieces), True, f"attend_even{k}")[0]
-        for k, pieces in enumerate(sets)
+    rest = list(early) + [
+        attend(pieces, True, f"attend_even{k}")[0] for k, pieces in enumerate(even[1:])
     ]
 
     message = shape(z.message, HD, BF16)
     sends = call(
-        functools.partial(pair_merge_kernel, z, [len(pieces) for pieces in sets]),
+        functools.partial(
+            pair_merge_kernel, z, [len(x) for x in even], [len(x) for x in odd]
+        ),
         [message] * (pairs - 1),
         (*rest, *got_rest),
         "pair_merge",
@@ -549,15 +567,18 @@
 
     columns = out_weight.shape[1]
     share_rows = 2 * z.rows // groups
+    share = shape(share_rows, columns // 2, BF16)
     shares = call(
         functools.partial(output_kernel, z),
-        [shape(share_rows, columns // 2, BF16)] * groups,
+        [share] * groups,
         (out_weight,) + tuple(heads[d] for d in range(n)),
         "output",
         2 * z.rows * z.heads * HD * columns,
         scratch=[pltpu.VMEM((z.rows, columns), F32)],
     )
-    shares = [shares[0]] + [swap(shares[e], "kv", groups, e) for e in range(1, groups)]
+    shares = [
+        swap(x, "kv", groups, e) if e else x for x, e in zip(shares, share_order(groups))
+    ]
     prompt_out, step_out = call(
         functools.partial(share_sum_kernel, z),
         [

time: 78 us -> 70.7 us (0.906)
  local copies, waits for them, and re-layouts: 6.06 us -> 0.02 us
  waiting for transfers between devices: 21.4 us -> 19.5 us
  Pallas kernels: 27.3 us -> 28.3 us
    unnamed x20 -> x8, local copies, waits for them, and re-layouts: 6.06 us -> 0.02 us
    ppermute x26, waiting for transfers between devices: 21.4 us -> 19.5 us  [swap(): return lax.ppermute(x, axis, [(i, i ^ d) for i in range(size)])]
    pallas_call x12 -> x13, Pallas kernels: 27.3 us -> 28.3 us  [call(): pl.pallas_call(kernel, out_shape=out_shape, in_specs=[scalar] * smem + [w...]
  transfers between devices with their start and end apart: 26 -> 26, of which waited for: 14 -> 11; matrix products, arithmetic and copies ran while one was open for 0% -> 0% of each run, Pallas kernels for 19% -> 33%
where the time goes in v3:
time: 70.7 us; the launch traced here: 70.6 us
  Pallas kernels  28.3 us (40%)
  starting transfers between devices  21.3 us (30%)
  waiting for transfers between devices  19.5 us (28%)
  between operations  1.48 us (2%)
    pallas_call x13, Pallas kernels, call(): pl.pallas_call(kernel, out_shape=out_shape, in_specs=[scalar] * smem + [w...  28.3 us
    ppermute x26, starting transfers between devices, swap(): return lax.ppermute(x, axis, [(i, i ^ d) for i in range(size)])  21.3 us
    ppermute x26, waiting for transfers between devices, swap(): return lax.ppermute(x, axis, [(i, i ^ d) for i in range(size)])  19.5 us
  transfers between devices with their start and end apart: 26, of which 11 were waited for; matrix products, arithmetic and copies ran while one was open for 0% of the time, Pallas kernels for 33%

profile of v3, /device:TPU:0, one launch (start us, length us, event | category | flops | bytes accessed | tf_op | source)
XLA Modules:
  0.0 70.6 jit_solution(8853162068871346774)
XLA Ops:
  0.7 3.0 %project.1 = (f32[4,304,128]{2,1,0:T(8,128)S(1)}, bf16[4,304,128]{2,1,0:T(8,128)(2,1)S(1)}) custom-call(bf16[8,128]{1,0:T(8,128)(2,1)} %bitcast.17, bf16[128,1024]{1,0:T(8,128)(2,1)} %xp_hbm.1, bf16[96,1024]{1,0:T(8,128)(2,1)} %bitcast.16, bf16[1024,1024]{1,0:T(8,128)(2,1)} %wq_hbm.1, bf16[1024,128]{1,0:T(8,128)(2,1)} %wk_hbm.1, bf16[1024,128]{1,0:T(8,128)(2,1)} %wv_hbm.1), custom_call_target="tpu_custom_call" | custom-call | flops 587202560 | bytes 1048576 | tf_op jit(solution)/shard_map/project/pallas_call | solution.py:83
  3.7 0.5 collective-permute-start
  4.2 1.2 %collective-permute-done.got_ref = bf16[4,304,128]{2,1,0:T(8,128)(2,1)S(1)} collective-permute-done((bf16[4,304,128]{2,1,0:T(8,128)(2,1)S(1)}, bf16[4,304,128]{2,1,0:T(8,128)(2,1)S(1)}, u32[]{:S(2)}, u32[]{:S(2)}) %collective-permute-start) | collective-permute-done | bytes 311328 | tf_op jit(solution)/shard_map/ppermute | solution.py:422
  5.5 2.9 %collective-permute-start.1 = (bf16[304,128]{1,0:T(8,128)(2,1)S(1)}, bf16[304,128]{1,0:T(8,128)(2,1)S(1)}, u32[]{:S(2)}, u32[]{:S(2)}) collective-permute-start(bf16[304,128]{1,0:T(8,128)(2,1)S(1)} %get-tuple-element.50), channel_id=1, source_target_pairs={{0,8},{4,12},{8,0},{12,4},{16,24},{20,28},{24,16},{28,20},{1,9},{5... | collective-permute-start | bytes 233480 | tf_op jit(solution)/shard_map/ppermute | solution.py:422
  8.4 1.5 %collective-permute-start.2 = (bf16[304,128]{1,0:T(8,128)(2,1)S(1)}, bf16[304,128]{1,0:T(8,128)(2,1)S(1)}, u32[]{:S(2)}, u32[]{:S(2)}) collective-permute-start(bf16[304,128]{1,0:T(8,128)(2,1)S(1)} %get-tuple-element.51), channel_id=1, source_target_pairs={{0,16},{4,20},{8,24},{12,28},{16,0},{20,4},{24,8},{28,12},{1,17},{... | collective-permute-start | bytes 233480 | tf_op jit(solution)/shard_map/ppermute | solution.py:422
  11.1 1.7 %collective-permute-done.2.refs_1_ = bf16[304,128]{1,0:T(8,128)(2,1)S(1)} collective-permute-done((bf16[304,128]{1,0:T(8,128)(2,1)S(1)}, bf16[304,128]{1,0:T(8,128)(2,1)S(1)}, u32[]{:S(2)}, u32[]{:S(2)}) %collective-permute-start.2) | collective-permute-done | bytes 77856 | tf_op jit(solution)/shard_map/ppermute | solution.py:422
  12.8 2.4 %collective-permute-done.3.refs_2_ = bf16[304,128]{1,0:T(8,128)(2,1)S(1)} collective-permute-done((bf16[304,128]{1,0:T(8,128)(2,1)S(1)}, bf16[304,128]{1,0:T(8,128)(2,1)S(1)}, u32[]{:S(2)}, u32[]{:S(2)}) %collective-permute-start.3) | collective-permute-done | bytes 77856 | tf_op jit(solution)/shard_map/ppermute | solution.py:422
  15.5 0.6 collective-permute-start.5
  16.1 0.6 collective-permute-start.6
  16.8 2.3 %collective-permute-start.7 = (bf16[224,128]{1,0:T(8,128)(2,1)S(1)}, bf16[224,128]{1,0:T(8,128)(2,1)S(1)}, u32[]{:S(2)}, u32[]{:S(2)}) collective-permute-start(bf16[224,128]{1,0:T(8,128)(2,1)S(1)} %get-tuple-element.67.refs_6_), channel_id=1, source_target_pairs={{0,24},{4,28},{8,16},{12,20},{16,8},{20,12},{24,0},{28,4},{1,25},{... | collective-permute-start | bytes 172040 | tf_op jit(solution)/shard_map/ppermute | solution.py:422
  19.1 3.0 %attend_core.1 = bf16[240,128]{1,0:T(8,128)(2,1)S(1)} custom-call(bf16[8192,128]{1,0:T(8,128)(2,1)S(1)} %bitcast.5, bf16[8192,128]{1,0:T(8,128)(2,1)S(1)} %bitcast.10, f32[1,8192]{1,0:T(1,128)S(1)} %get-tuple-element.48.refs_2_, bf16[32,128]{1,0:T(8,128)(2,1)S(1)} %get-tuple-element.53.refs_3_, bf16[32,128]{1,0:T(8,128)(2,1)S(1)} %get-tuple-element.54.refs_4_, ...), custom_call_target="tpu_custom_call" | custom-call | flops 1879048192 | bytes 1048576 | tf_op jit(solution)/shard_map/attend_core/pallas_call | solution.py:83
  22.7 2.9 %attend_near.1.refs_0_ = bf16[1,240,128]{2,1,0:T(8,128)(2,1)S(1)} custom-call(bf16[8192,128]{1,0:T(8,128)(2,1)S(1)} %bitcast.6, bf16[8192,128]{1,0:T(8,128)(2,1)S(1)} %bitcast.11, f32[1,8192]{1,0:T(1,128)S(1)} %get-tuple-element.48.refs_2_, bf16[32,128]{1,0:T(8,128)(2,1)S(1)} %get-tuple-element.53.refs_3_, bf16[32,128]{1,0:T(8,128)(2,1)S(1)} %get-tuple-element.54.refs_4_, ...), custom_call_target="tpu_custom_call" | custom-call | flops 1879048192 | bytes 1048576 | tf_op jit(solution)/shard_map/attend_near/pallas_call | solution.py:83
  26.2 8.3 %attend_odd0.1 = bf16[3,240,128]{2,1,0:T(8,128)(2,1)S(1)} custom-call(bf16[8192,128]{1,0:T(8,128)(2,1)S(1)} %bitcast.7, bf16[8192,128]{1,0:T(8,128)(2,1)S(1)} %bitcast.12, f32[1,8192]{1,0:T(1,128)S(1)} %get-tuple-element.48.refs_2_, bf16[32,128]{1,0:T(8,128)(2,1)S(1)} %get-tuple-element.53.refs_3_, bf16[32,128]{1,0:T(8,128)(2,1)S(1)} %get-tuple-element.54.refs_4_, ...), custom_call_target="tpu_custom_call" | custom-call | flops 5637144576 | bytes 1048576 | tf_op jit(solution)/shard_map/attend_odd0/pallas_call | solution.py:83
  34.6 5.5 %attend_even0.1.refs_1_ = bf16[2,240,128]{2,1,0:T(8,128)(2,1)S(1)} custom-call(bf16[8192,128]{1,0:T(8,128)(2,1)S(1)} %bitcast.8, bf16[8192,128]{1,0:T(8,128)(2,1)S(1)} %bitcast.13, f32[1,8192]{1,0:T(1,128)S(1)} %get-tuple-element.48.refs_2_, bf16[32,128]{1,0:T(8,128)(2,1)S(1)} %get-tuple-element.53.refs_3_, bf16[32,128]{1,0:T(8,128)(2,1)S(1)} %get-tuple-element.54.refs_4_, ...), custom_call_target="tpu_custom_call" | custom-call | flops 3758096384 | bytes 1048576 | tf_op jit(solution)/shard_map/attend_even0/pallas_call | solution.py:83
  40.6 1.3 %collective-permute-start.13 = (bf16[240,128]{1,0:T(8,128)(2,1)S(1)}, bf16[240,128]{1,0:T(8,128)(2,1)S(1)}, u32[]{:S(2)}, u32[]{:S(2)}) collective-permute-start(bf16[240,128]{1,0:T(8,128)(2,1)S(1)} %get-tuple-element.69), channel_id=1, source_target_pairs={{0,8},{4,12},{8,0},{12,4},{16,24},{20,28},{24,16},{28,20},{1,9},{5... | collective-permute-start | bytes 184328 | tf_op jit(solution)/shard_map/ppermute | solution.py:422
  41.9 1.3 %collective-permute-start.14 = (bf16[240,128]{1,0:T(8,128)(2,1)S(1)}, bf16[240,128]{1,0:T(8,128)(2,1)S(1)}, u32[]{:S(2)}, u32[]{:S(2)}) collective-permute-start(bf16[240,128]{1,0:T(8,128)(2,1)S(1)} %get-tuple-element.70), channel_id=1, source_target_pairs={{0,16},{4,20},{8,24},{12,28},{16,0},{20,4},{24,8},{28,12},{1,17},{... | collective-permute-start | bytes 184328 | tf_op jit(solution)/shard_map/ppermute | solution.py:422
  43.2 1.0 %collective-permute-start.15 = (bf16[240,128]{1,0:T(8,128)(2,1)S(1)}, bf16[240,128]{1,0:T(8,128)(2,1)S(1)}, u32[]{:S(2)}, u32[]{:S(2)}) collective-permute-start(bf16[240,128]{1,0:T(8,128)(2,1)S(1)} %get-tuple-element.71), channel_id=1, source_target_pairs={{0,24},{4,28},{8,16},{12,20},{16,8},{20,12},{24,0},{28,4},{1,25},{... | collective-permute-start | bytes 184328 | tf_op jit(solution)/shard_map/ppermute | solution.py:422
  44.1 2.9 %attend_own.1.refs_0_ = bf16[240,128]{1,0:T(8,128)(2,1)S(1)} custom-call(bf16[8192,128]{1,0:T(8,128)(2,1)S(1)} %bitcast.9, bf16[8192,128]{1,0:T(8,128)(2,1)S(1)} %bitcast.14, f32[1,8192]{1,0:T(1,128)S(1)} %get-tuple-element.48.refs_2_, bf16[32,128]{1,0:T(8,128)(2,1)S(1)} %get-tuple-element.53.refs_3_, bf16[32,128]{1,0:T(8,128)(2,1)S(1)} %get-tuple-element.54.refs_4_, ...), custom_call_target="tpu_custom_call" | custom-call | flops 1879048192 | bytes 1048576 | tf_op jit(solution)/shard_map/attend_own/pallas_call | solution.py:83
  47.1 1.2 %collective-permute-done.15.refs_4_ = bf16[240,128]{1,0:T(8,128)(2,1)S(1)} collective-permute-done((bf16[240,128]{1,0:T(8,128)(2,1)S(1)}, bf16[240,128]{1,0:T(8,128)(2,1)S(1)}, u32[]{:S(2)}, u32[]{:S(2)}) %collective-permute-start.15) | collective-permute-done | bytes 61472 | tf_op jit(solution)/shard_map/ppermute | solution.py:422
  48.8 0.6 collective-permute-start.17
  49.4 1.0 %collective-permute-start.19 = (bf16[224,128]{1,0:T(8,128)(2,1)S(1)}, bf16[224,128]{1,0:T(8,128)(2,1)S(1)}, u32[]{:S(2)}, u32[]{:S(2)}) collective-permute-start(bf16[224,128]{1,0:T(8,128)(2,1)S(1)} %final_merge.1.refs_0_), channel_id=1, source_target_pairs={{0,16},{4,20},{8,24},{12,28},{16,0},{20,4},{24,8},{28,12},{1,17},{... | collective-permute-start | bytes 172040 | tf_op jit(solution)/shard_map/ppermute | solution.py:422
  50.4 2.0 %collective-permute-start.21 = (bf16[224,128]{1,0:T(8,128)(2,1)S(1)}, bf16[224,128]{1,0:T(8,128)(2,1)S(1)}, u32[]{:S(2)}, u32[]{:S(2)}) collective-permute-start(bf16[224,128]{1,0:T(8,128)(2,1)S(1)} %final_merge.1.refs_0_), channel_id=1, source_target_pairs={{0,24},{4,28},{8,16},{12,20},{16,8},{20,12},{24,0},{28,4},{1,25},{... | collective-permute-start | bytes 172040 | tf_op jit(solution)/shard_map/ppermute | solution.py:422
  52.3 1.0 %collective-permute-done.17.refs_2_ = bf16[224,128]{1,0:T(8,128)(2,1)S(1)} collective-permute-done((bf16[224,128]{1,0:T(8,128)(2,1)S(1)}, bf16[224,128]{1,0:T(8,128)(2,1)S(1)}, u32[]{:S(2)}, u32[]{:S(2)}) %collective-permute-start.17) | collective-permute-done | bytes 57376 | tf_op jit(solution)/shard_map/ppermute | solution.py:422
  53.3 0.8 %collective-permute-done.19.refs_4_ = bf16[224,128]{1,0:T(8,128)(2,1)S(1)} collective-permute-done((bf16[224,128]{1,0:T(8,128)(2,1)S(1)}, bf16[224,128]{1,0:T(8,128)(2,1)S(1)}, u32[]{:S(2)}, u32[]{:S(2)}) %collective-permute-start.19) | collective-permute-done | bytes 57376 | tf_op jit(solution)/shard_map/ppermute | solution.py:422
  54.1 1.4 %collective-permute-done.21.refs_6_ = bf16[224,128]{1,0:T(8,128)(2,1)S(1)} collective-permute-done((bf16[224,128]{1,0:T(8,128)(2,1)S(1)}, bf16[224,128]{1,0:T(8,128)(2,1)S(1)}, u32[]{:S(2)}, u32[]{:S(2)}) %collective-permute-start.21) | collective-permute-done | bytes 57376 | tf_op jit(solution)/shard_map/ppermute | solution.py:422
  55.5 1.2 %collective-permute-done.22.refs_7_ = bf16[224,128]{1,0:T(8,128)(2,1)S(1)} collective-permute-done((bf16[224,128]{1,0:T(8,128)(2,1)S(1)}, bf16[224,128]{1,0:T(8,128)(2,1)S(1)}, u32[]{:S(2)}, u32[]{:S(2)}) %collective-permute-start.22) | collective-permute-done | bytes 57376 | tf_op jit(solution)/shard_map/ppermute | solution.py:422
  56.7 0.7 %output.1 = (bf16[112,512]{1,0:T(8,128)(2,1)S(1)}, bf16[112,512]{1,0:T(8,128)(2,1)S(1)}, bf16[112,512]{1,0:T(8,128)(2,1)S(1)}, bf16[112,512]{1,0:T(8,128)(2,1)S(1)}) custom-call(bf16[1024,1024]{1,0:T(8,128)(2,1)S(1)} %copy-done, bf16[224,128]{1,0:T(8,128)(2,1)S(1)} %final_merge.1.refs_0_, bf16[224,128]{1,0:T(8,128)(2,1)S(1)} %collective-permute-done.16.refs_1_, ...), custom_call_target="tpu_custom_call" | custom-call | flops 469762048 | bytes 1048576 | tf_op jit(solution)/shard_map/output/pallas_call | solution.py:83
  57.4 2.7 %collective-permute-start.23 = (bf16[112,512]{1,0:T(8,128)(2,1)S(1)}, bf16[112,512]{1,0:T(8,128)(2,1)S(1)}, u32[]{:S(2)}, u32[]{:S(2)}) collective-permute-start(bf16[112,512]{1,0:T(8,128)(2,1)S(1)} %get-tuple-element.72), channel_id=1, source_target_pairs={{0,2},{1,3},{2,0},{3,1},{4,6},{5,7},{6,4},{7,5},{8,10},{9,11},{10,... | collective-permute-start | bytes 344072 | tf_op jit(solution)/shard_map/ppermute | solution.py:422
  60.0 1.4 %collective-permute-start.24 = (bf16[112,512]{1,0:T(8,128)(2,1)S(1)}, bf16[112,512]{1,0:T(8,128)(2,1)S(1)}, u32[]{:S(2)}, u32[]{:S(2)}) collective-permute-start(bf16[112,512]{1,0:T(8,128)(2,1)S(1)} %get-tuple-element.73), channel_id=1, source_target_pairs={{0,3},{1,2},{2,1},{3,0},{4,7},{5,6},{6,5},{7,4},{8,11},{9,10},{10,... | collective-permute-start | bytes 344072 | tf_op jit(solution)/shard_map/ppermute | solution.py:422
  61.6 7.7 %collective-permute-done.23.refs_0_ = bf16[112,512]{1,0:T(8,128)(2,1)S(1)} collective-permute-done((bf16[112,512]{1,0:T(8,128)(2,1)S(1)}, bf16[112,512]{1,0:T(8,128)(2,1)S(1)}, u32[]{:S(2)}, u32[]{:S(2)}) %collective-permute-start.23) | collective-permute-done | bytes 114720 | tf_op jit(solution)/shard_map/ppermute | solution.py:422
  69.3 0.6 collective-permute-done.25.refs_2_
  69.9 0.7 share_sum.1
  (41 shorter events, 3.3 us)
Async XLA Ops:
  0.6 10.0 %copy-start.3 = (s32[32]{0:T(128)S(1)}, s32[32]{0:T(128)}, u32[]{:S(2)}) copy-start(s32[32]{0:T(128)} %param.21) | copy-start | bytes 388
  0.6 18.4 %copy-start.1 = (bf16[1,8192,128]{2,1,0:T(8,128)(2,1)S(1)}, bf16[1,8192,128]{2,1,0:T(8,128)(2,1)}, u32[]{:S(2)}) copy-start(bf16[1,8192,128]{2,1,0:T(8,128)(2,1)} %param.18) | copy-start | bytes 6291460
  0.7 18.4 %copy-start.2 = (bf16[1,8192,128]{2,1,0:T(8,128)(2,1)S(1)}, bf16[1,8192,128]{2,1,0:T(8,128)(2,1)}, u32[]{:S(2)}) copy-start(bf16[1,8192,128]{2,1,0:T(8,128)(2,1)} %param.19) | copy-start | bytes 6291460
  3.7 1.8 %collective-permute-start = (bf16[4,304,128]{2,1,0:T(8,128)(2,1)S(1)}, bf16[4,304,128]{2,1,0:T(8,128)(2,1)S(1)}, u32[]{:S(2)}, u32[]{:S(2)}) collective-permute-start(bf16[4,304,128]{2,1,0:T(8,128)(2,1)S(1)} %get-tuple-element.40), channel_id=1, source_target_pairs={{0,4},{4,0},{8,12},{12,8},{16,20},{20,16},{24,28},{28,24},{1,5},{5... | collective-permute-start | bytes 933896 | tf_op jit(solution)/shard_map/ppermute | solution.py:422
  5.5 5.6 %collective-permute-start.1 = (bf16[304,128]{1,0:T(8,128)(2,1)S(1)}, bf16[304,128]{1,0:T(8,128)(2,1)S(1)}, u32[]{:S(2)}, u32[]{:S(2)}) collective-permute-start(bf16[304,128]{1,0:T(8,128)(2,1)S(1)} %get-tuple-element.50), channel_id=1, source_target_pairs={{0,8},{4,12},{8,0},{12,4},{16,24},{20,28},{24,16},{28,20},{1,9},{5... | collective-permute-start | bytes 233480 | tf_op jit(solution)/shard_map/ppermute | solution.py:422
  8.4 4.4 %collective-permute-start.2 = (bf16[304,128]{1,0:T(8,128)(2,1)S(1)}, bf16[304,128]{1,0:T(8,128)(2,1)S(1)}, u32[]{:S(2)}, u32[]{:S(2)}) collective-permute-start(bf16[304,128]{1,0:T(8,128)(2,1)S(1)} %get-tuple-element.51), channel_id=1, source_target_pairs={{0,16},{4,20},{8,24},{12,28},{16,0},{20,4},{24,8},{28,12},{1,17},{... | collective-permute-start | bytes 233480 | tf_op jit(solution)/shard_map/ppermute | solution.py:422
  10.0 5.3 %collective-permute-start.3 = (bf16[304,128]{1,0:T(8,128)(2,1)S(1)}, bf16[304,128]{1,0:T(8,128)(2,1)S(1)}, u32[]{:S(2)}, u32[]{:S(2)}) collective-permute-start(bf16[304,128]{1,0:T(8,128)(2,1)S(1)} %get-tuple-element.52), channel_id=1, source_target_pairs={{0,24},{4,28},{8,16},{12,20},{16,8},{20,12},{24,0},{28,4},{1,25},{... | collective-permute-start | bytes 233480 | tf_op jit(solution)/shard_map/ppermute | solution.py:422
  15.4 3.6 %collective-permute-start.4 = (bf16[224,128]{1,0:T(8,128)(2,1)S(1)}, bf16[224,128]{1,0:T(8,128)(2,1)S(1)}, u32[]{:S(2)}, u32[]{:S(2)}) collective-permute-start(bf16[224,128]{1,0:T(8,128)(2,1)S(1)} %get-tuple-element.67.refs_6_), channel_id=1, source_target_pairs={{0,4},{4,0},{8,12},{12,8},{16,20},{20,16},{24,28},{28,24},{1,5},{5... | collective-permute-start | bytes 172040 | tf_op jit(solution)/shard_map/ppermute | solution.py:422
  15.5 6.5 %collective-permute-start.5 = (bf16[224,128]{1,0:T(8,128)(2,1)S(1)}, bf16[224,128]{1,0:T(8,128)(2,1)S(1)}, u32[]{:S(2)}, u32[]{:S(2)}) collective-permute-start(bf16[224,128]{1,0:T(8,128)(2,1)S(1)} %get-tuple-element.67.refs_6_), channel_id=1, source_target_pairs={{0,8},{4,12},{8,0},{12,4},{16,24},{20,28},{24,16},{28,20},{1,9},{5... | collective-permute-start | bytes 172040 | tf_op jit(solution)/shard_map/ppermute | solution.py:422
  16.1 5.9 %collective-permute-start.6 = (bf16[224,128]{1,0:T(8,128)(2,1)S(1)}, bf16[224,128]{1,0:T(8,128)(2,1)S(1)}, u32[]{:S(2)}, u32[]{:S(2)}) collective-permute-start(bf16[224,128]{1,0:T(8,128)(2,1)S(1)} %get-tuple-element.67.refs_6_), channel_id=1, source_target_pairs={{0,16},{4,20},{8,24},{12,28},{16,0},{20,4},{24,8},{28,12},{1,17},{... | collective-permute-start | bytes 172040 | tf_op jit(solution)/shard_map/ppermute | solution.py:422
  16.8 5.3 %collective-permute-start.7 = (bf16[224,128]{1,0:T(8,128)(2,1)S(1)}, bf16[224,128]{1,0:T(8,128)(2,1)S(1)}, u32[]{:S(2)}, u32[]{:S(2)}) collective-permute-start(bf16[224,128]{1,0:T(8,128)(2,1)S(1)} %get-tuple-element.67.refs_6_), channel_id=1, source_target_pairs={{0,24},{4,28},{8,16},{12,20},{16,8},{20,12},{24,0},{28,4},{1,25},{... | collective-permute-start | bytes 172040 | tf_op jit(solution)/shard_map/ppermute | solution.py:422
  22.1 4.1 %collective-permute-start.10 = (bf16[224,128]{1,0:T(8,128)(2,1)S(1)}, bf16[224,128]{1,0:T(8,128)(2,1)S(1)}, u32[]{:S(2)}, u32[]{:S(2)}) collective-permute-start(bf16[224,128]{1,0:T(8,128)(2,1)S(1)} %collective-permute-done.7.refs_7_), channel_id=1, source_target_pairs={{0,4},{4,0},{8,12},{12,8},{16,20},{20,16},{24,28},{28,24},{1,5},{5... | collective-permute-start | bytes 172040 | tf_op jit(solution)/shard_map/ppermute | solution.py:422
  22.1 4.0 %collective-permute-start.8 = (bf16[224,128]{1,0:T(8,128)(2,1)S(1)}, bf16[224,128]{1,0:T(8,128)(2,1)S(1)}, u32[]{:S(2)}, u32[]{:S(2)}) collective-permute-start(bf16[224,128]{1,0:T(8,128)(2,1)S(1)} %collective-permute-done.5.refs_6_), channel_id=1, source_target_pairs={{0,4},{4,0},{8,12},{12,8},{16,20},{20,16},{24,28},{28,24},{1,5},{5... | collective-permute-start | bytes 172040 | tf_op jit(solution)/shard_map/ppermute | solution.py:422
  22.6 3.5 %collective-permute-start.9 = (bf16[224,128]{1,0:T(8,128)(2,1)S(1)}, bf16[224,128]{1,0:T(8,128)(2,1)S(1)}, u32[]{:S(2)}, u32[]{:S(2)}) collective-permute-start(bf16[224,128]{1,0:T(8,128)(2,1)S(1)} %collective-permute-done.6.refs_6_), channel_id=1, source_target_pairs={{0,4},{4,0},{8,12},{12,8},{16,20},{20,16},{24,28},{28,24},{1,5},{5... | collective-permute-start | bytes 172040 | tf_op jit(solution)/shard_map/ppermute | solution.py:422
  25.7 21.4 %collective-permute-start.12 = (bf16[240,128]{1,0:T(8,128)(2,1)S(1)}, bf16[240,128]{1,0:T(8,128)(2,1)S(1)}, u32[]{:S(2)}, u32[]{:S(2)}) collective-permute-start(bf16[240,128]{1,0:T(8,128)(2,1)S(1)} %attend_core.1), channel_id=1, source_target_pairs={{0,4},{4,0},{8,12},{12,8},{16,20},{20,16},{24,28},{28,24},{1,5},{5... | collective-permute-start | bytes 184328 | tf_op jit(solution)/shard_map/ppermute | solution.py:422
  34.5 5.6 %collective-permute-start.11 = (bf16[3,240,128]{2,1,0:T(8,128)(2,1)S(1)}, bf16[3,240,128]{2,1,0:T(8,128)(2,1)S(1)}, u32[]{:S(2)}, u32[]{:S(2)}) collective-permute-start(bf16[3,240,128]{2,1,0:T(8,128)(2,1)S(1)} %attend_odd0.1), channel_id=1, source_target_pairs={{0,4},{4,0},{8,12},{12,8},{16,20},{20,16},{24,28},{28,24},{1,5},{5... | collective-permute-start | bytes 552968 | tf_op jit(solution)/shard_map/ppermute | solution.py:422
  40.6 16.1 %copy-start = (bf16[1024,1024]{1,0:T(8,128)(2,1)S(1)}, bf16[1024,1024]{1,0:T(8,128)(2,1)}, u32[]{:S(2)}) copy-start(bf16[1024,1024]{1,0:T(8,128)(2,1)} %weight_ref.1) | copy-start | bytes 6291460
  40.6 6.5 %collective-permute-start.13 = (bf16[240,128]{1,0:T(8,128)(2,1)S(1)}, bf16[240,128]{1,0:T(8,128)(2,1)S(1)}, u32[]{:S(2)}, u32[]{:S(2)}) collective-permute-start(bf16[240,128]{1,0:T(8,128)(2,1)S(1)} %get-tuple-element.69), channel_id=1, source_target_pairs={{0,8},{4,12},{8,0},{12,4},{16,24},{20,28},{24,16},{28,20},{1,9},{5... | collective-permute-start | bytes 184328 | tf_op jit(solution)/shard_map/ppermute | solution.py:422
  41.9 5.2 %collective-permute-start.14 = (bf16[240,128]{1,0:T(8,128)(2,1)S(1)}, bf16[240,128]{1,0:T(8,128)(2,1)S(1)}, u32[]{:S(2)}, u32[]{:S(2)}) collective-permute-start(bf16[240,128]{1,0:T(8,128)(2,1)S(1)} %get-tuple-element.70), channel_id=1, source_target_pairs={{0,16},{4,20},{8,24},{12,28},{16,0},{20,4},{24,8},{28,12},{1,17},{... | collective-permute-start | bytes 184328 | tf_op jit(solution)/shard_map/ppermute | solution.py:422
  43.2 5.1 %collective-permute-start.15 = (bf16[240,128]{1,0:T(8,128)(2,1)S(1)}, bf16[240,128]{1,0:T(8,128)(2,1)S(1)}, u32[]{:S(2)}, u32[]{:S(2)}) collective-permute-start(bf16[240,128]{1,0:T(8,128)(2,1)S(1)} %get-tuple-element.71), channel_id=1, source_target_pairs={{0,24},{4,28},{8,16},{12,20},{16,8},{20,12},{24,0},{28,4},{1,25},{... | collective-permute-start | bytes 184328 | tf_op jit(solution)/shard_map/ppermute | solution.py:422
  48.8 4.5 %collective-permute-start.17 = (bf16[224,128]{1,0:T(8,128)(2,1)S(1)}, bf16[224,128]{1,0:T(8,128)(2,1)S(1)}, u32[]{:S(2)}, u32[]{:S(2)}) collective-permute-start(bf16[224,128]{1,0:T(8,128)(2,1)S(1)} %final_merge.1.refs_0_), channel_id=1, source_target_pairs={{0,8},{4,12},{8,0},{12,4},{16,24},{20,28},{24,16},{28,20},{1,9},{5... | collective-permute-start | bytes 172040 | tf_op jit(solution)/shard_map/ppermute | solution.py:422
  49.4 4.7 %collective-permute-start.19 = (bf16[224,128]{1,0:T(8,128)(2,1)S(1)}, bf16[224,128]{1,0:T(8,128)(2,1)S(1)}, u32[]{:S(2)}, u32[]{:S(2)}) collective-permute-start(bf16[224,128]{1,0:T(8,128)(2,1)S(1)} %final_merge.1.refs_0_), channel_id=1, source_target_pairs={{0,16},{4,20},{8,24},{12,28},{16,0},{20,4},{24,8},{28,12},{1,17},{... | collective-permute-start | bytes 172040 | tf_op jit(solution)/shard_map/ppermute | solution.py:422
  50.4 5.1 %collective-permute-start.21 = (bf16[224,128]{1,0:T(8,128)(2,1)S(1)}, bf16[224,128]{1,0:T(8,128)(2,1)S(1)}, u32[]{:S(2)}, u32[]{:S(2)}) collective-permute-start(bf16[224,128]{1,0:T(8,128)(2,1)S(1)} %final_merge.1.refs_0_), channel_id=1, source_target_pairs={{0,24},{4,28},{8,16},{12,20},{16,8},{20,12},{24,0},{28,4},{1,25},{... | collective-permute-start | bytes 172040 | tf_op jit(solution)/shard_map/ppermute | solution.py:422
  52.3 3.1 %collective-permute-start.16 = (bf16[224,128]{1,0:T(8,128)(2,1)S(1)}, bf16[224,128]{1,0:T(8,128)(2,1)S(1)}, u32[]{:S(2)}, u32[]{:S(2)}) collective-permute-start(bf16[224,128]{1,0:T(8,128)(2,1)S(1)} %final_merge.1.refs_0_), channel_id=1, source_target_pairs={{0,4},{4,0},{8,12},{12,8},{16,20},{20,16},{24,28},{28,24},{1,5},{5... | collective-permute-start | bytes 172040 | tf_op jit(solution)/shard_map/ppermute | solution.py:422
  53.3 2.2 %collective-permute-start.18 = (bf16[224,128]{1,0:T(8,128)(2,1)S(1)}, bf16[224,128]{1,0:T(8,128)(2,1)S(1)}, u32[]{:S(2)}, u32[]{:S(2)}) collective-permute-start(bf16[224,128]{1,0:T(8,128)(2,1)S(1)} %collective-permute-done.17.refs_2_), channel_id=1, source_target_pairs={{0,4},{4,0},{8,12},{12,8},{16,20},{20,16},{24,28},{28,24},{1,5},{5... | collective-permute-start | bytes 172040 | tf_op jit(solution)/shard_map/ppermute | solution.py:422
  54.1 1.4 %collective-permute-start.20 = (bf16[224,128]{1,0:T(8,128)(2,1)S(1)}, bf16[224,128]{1,0:T(8,128)(2,1)S(1)}, u32[]{:S(2)}, u32[]{:S(2)}) collective-permute-start(bf16[224,128]{1,0:T(8,128)(2,1)S(1)} %collective-permute-done.19.refs_4_), channel_id=1, source_target_pairs={{0,4},{4,0},{8,12},{12,8},{16,20},{20,16},{24,28},{28,24},{1,5},{5... | collective-permute-start | bytes 172040 | tf_op jit(solution)/shard_map/ppermute | solution.py:422
  55.4 1.2 %collective-permute-start.22 = (bf16[224,128]{1,0:T(8,128)(2,1)S(1)}, bf16[224,128]{1,0:T(8,128)(2,1)S(1)}, u32[]{:S(2)}, u32[]{:S(2)}) collective-permute-start(bf16[224,128]{1,0:T(8,128)(2,1)S(1)} %collective-permute-done.21.refs_6_), channel_id=1, source_target_pairs={{0,4},{4,0},{8,12},{12,8},{16,20},{20,16},{24,28},{28,24},{1,5},{5... | collective-permute-start | bytes 172040 | tf_op jit(solution)/shard_map/ppermute | solution.py:422
  57.4 11.9 %collective-permute-start.23 = (bf16[112,512]{1,0:T(8,128)(2,1)S(1)}, bf16[112,512]{1,0:T(8,128)(2,1)S(1)}, u32[]{:S(2)}, u32[]{:S(2)}) collective-permute-start(bf16[112,512]{1,0:T(8,128)(2,1)S(1)} %get-tuple-element.72), channel_id=1, source_target_pairs={{0,2},{1,3},{2,0},{3,1},{4,6},{5,7},{6,4},{7,5},{8,10},{9,11},{10,... | collective-permute-start | bytes 344072 | tf_op jit(solution)/shard_map/ppermute | solution.py:422
  60.0 9.3 %collective-permute-start.24 = (bf16[112,512]{1,0:T(8,128)(2,1)S(1)}, bf16[112,512]{1,0:T(8,128)(2,1)S(1)}, u32[]{:S(2)}, u32[]{:S(2)}) collective-permute-start(bf16[112,512]{1,0:T(8,128)(2,1)S(1)} %get-tuple-element.73), channel_id=1, source_target_pairs={{0,3},{1,2},{2,1},{3,0},{4,7},{5,6},{6,5},{7,4},{8,11},{9,10},{10,... | collective-permute-start | bytes 344072 | tf_op jit(solution)/shard_map/ppermute | solution.py:422
  61.4 8.5 %collective-permute-start.25 = (bf16[112,512]{1,0:T(8,128)(2,1)S(1)}, bf16[112,512]{1,0:T(8,128)(2,1)S(1)}, u32[]{:S(2)}, u32[]{:S(2)}) collective-permute-start(bf16[112,512]{1,0:T(8,128)(2,1)S(1)} %get-tuple-element.74), channel_id=1, source_target_pairs={{0,1},{1,0},{2,3},{3,2},{4,5},{5,4},{6,7},{7,6},{8,9},{9,8},{10,11... | collective-permute-start | bytes 344072 | tf_op jit(solution)/shard_map/ppermute | solution.py:422

commit v4 on v3

--- a/solution.py
+++ b/solution.py
@@ -11,8 +11,13 @@
 EPSILON = 1e-05
 MASKED = -1e30
 LOG2E = 1.4426950408889634
+SCALE = LOG2E / HD**0.5
 STAT_ROWS = 16
 AT_ONCE = 3
+CHUNK = 1024
+FIRST = 256
+BLOCK = 512
+TOO_LARGE = 2.0**60
 VMEM_BYTES = 20 * 2**20
 BF16 = jnp.bfloat16
 F32 = jnp.float32
@@ -27,6 +32,21 @@
     rest = x - high
     middle = rest.astype(BF16).astype(F32)
     return high, middle, rest - middle
+
+
+def pack_sums(z, total, squares):
+    query = total[0 : z.piece]
+    high = query.astype(BF16).astype(F32)
+    return jnp.concatenate(
+        [high, query - high, total[z.piece : z.body], stack_stats([squares])], axis=0
+    ).astype(BF16)
+
+
+def unpack_sums(z, sent):
+    wide = sent.astype(F32)
+    query = wide[0 : z.piece] + wide[z.piece : 2 * z.piece]
+    total = jnp.concatenate([query, wide[2 * z.piece : z.piece + z.body]], axis=0)
+    return total, read_stats(wide[z.piece + z.body :], z.square_lines, 1)[0]
 
 
 def column_to_rows(column):
@@ -121,7 +141,9 @@
         self.prompt_slots = up(self.prompt_own, 16)
         self.slots = self.prompt_slots + self.decode_slots
         self.message = self.piece + STAT_ROWS
-        self.project = self.piece + 2 * self.slots + STAT_ROWS
+        self.body = self.piece + 2 * self.slots
+        self.project = self.body + STAT_ROWS
+        self.sent = self.piece + self.project
 
 
 def project_kernel(z, gain_hbm, xp_hbm, xs_hbm, wq_hbm, wk_hbm, wv_hbm, even_ref, odd_ref, gain_ref, xp_ref, xs_ref, wq_ref, wk_ref, wv_ref, scaled_ref, query_ref, kvp_ref, kvd_ref, sems):
@@ -157,8 +179,6 @@
         scaled_ref[base : base + size, :] = (wide * gain).astype(BF16)
     square_rows = column_to_rows(jnp.concatenate(squares, axis=0))
     pad = jnp.zeros((STAT_ROWS - z.square_lines, 128), F32)
-    stats_plain = jnp.concatenate([square_rows, pad], axis=0)
-    stats_split = stack_stats([square_rows])
     decode = z.steps * z.row_total
     count = z.n * z.decode_slots
     place = lax.broadcasted_iota(jnp.int32, (count, decode), 0)
@@ -194,47 +214,38 @@
         ]
         kvp = kvp_ref[pl.ds(pl.multiple_of(owner * z.prompt_own, 8), z.prompt_own), :]
         kvd = kvd_ref[pl.ds(pl.multiple_of(owner * z.decode_slots, 8), z.decode_slots), :]
-        ref = odd_ref if d % 2 else even_ref
-        stats = stats_split if d % 2 else stats_plain
-        everything = jnp.concatenate(
-            [part, kvp[:, :HD], kvd[:, :HD], kvp[:, HD:], kvd[:, HD:], stats], axis=0
-        )
-        ref[d // 2] = everything.astype(ref.dtype)
+        total = jnp.concatenate([part, kvp[:, :HD], kvd[:, :HD], kvp[:, HD:], kvd[:, HD:]], axis=0)
+        if d % 2:
+            odd_ref[d // 2] = pack_sums(z, total, square_rows)
+        else:
+            even_ref[d // 2] = jnp.concatenate([total, square_rows, pad], axis=0)
 
 
 def pair_sum_kernel(z, even_ref, got_ref, own_ref, *send_refs):
-    body = z.project - STAT_ROWS
     for i in range(z.n // 2):
-        got = got_ref[i].astype(F32)
-        total = even_ref[i, 0:body, :] + got[0:body]
-        squares = (
-            even_ref[i, body : body + z.square_lines, :]
-            + read_stats(got[body:], z.square_lines, 1)[0]
-        )
+        total, squares = unpack_sums(z, got_ref[i])
+        total = total + even_ref[i, 0 : z.body, :]
+        squares = squares + even_ref[i, z.body : z.body + z.square_lines, :]
         if i == 0:
             pad = jnp.zeros((STAT_ROWS - z.square_lines, 128), F32)
             own_ref[...] = jnp.concatenate([total, squares, pad], axis=0)
         else:
-            send_refs[i - 1][...] = jnp.concatenate(
-                [total, stack_stats([squares])], axis=0
-            ).astype(BF16)
+            send_refs[i - 1][...] = pack_sums(z, total, squares)
 
 
 def finish_kernel(z, features, own_ref, *refs):
     got_refs = refs[: z.n // 2 - 1]
     query_ref, key_ref, value_ref = refs[z.n // 2 - 1 :]
     me = lax.axis_index("ctx")
-    body = z.project - STAT_ROWS
-    total = own_ref[0:body, :]
-    squares = own_ref[body : body + z.square_lines, :]
+    total = own_ref[0 : z.body, :]
+    squares = own_ref[z.body : z.body + z.square_lines, :]
     for ref in got_refs:
-        got = ref[...].astype(F32)
-        total = total + got[0:body]
-        squares = squares + read_stats(got[body:], z.square_lines, 1)[0]
+        got, got_squares = unpack_sums(z, ref[...])
+        total = total + got
+        squares = squares + got_squares
     inverse = lax.rsqrt(squares / features + EPSILON)
     rows = lax.broadcasted_iota(jnp.int32, (z.piece, 1), 0) + (me // z.heads) * z.piece
-    factor = HD ** (-0.5) * LOG2E
-    query_ref[...] = (total[0 : z.piece] * (rows_to_column(inverse, rows) * factor)).astype(BF16)
+    query_ref[...] = (total[0 : z.piece] * rows_to_column(inverse, rows)).astype(BF16)
     slot = lax.broadcasted_iota(jnp.int32, (z.slots, 1), 0)
     late = slot - z.prompt_slots
     index = jnp.where(
@@ -250,10 +261,25 @@
     value_ref[...] = (total[z.piece + z.slots : z.piece + 2 * z.slots] * own).astype(BF16)
 
 
-def mask_kernel(z, length_ref, visible_ref, bias_ref, extra_ref):
+def prepare_kernel(z, length_ref, visible_ref, key_hbm, value_hbm, key_ref, value_ref, live_ref, extra_ref, sems):
+    loads = [
+        pltpu.make_async_copy(key_hbm, key_ref, sems.at[0]),
+        pltpu.make_async_copy(value_hbm, value_ref, sems.at[1]),
+    ]
+    for load in loads:
+        load.start()
     me = lax.axis_index("ctx")
-    live = lax.broadcasted_iota(jnp.int32, bias_ref.shape, 1) < length_ref[0]
-    bias_ref[...] = jnp.where(live, 0.0, MASKED)
+    length = length_ref[0]
+    size = min(BLOCK, key_ref.shape[0])
+    blocks = key_ref.shape[0] // size
+    local = lax.broadcasted_iota(jnp.int32, (size, HD), 0)
+
+    def mark(i, carry):
+        rows = pl.ds(pl.multiple_of(i * size, size), size)
+        live_ref[rows, :] = jnp.where(local + i * size < length, 1.0, 0.0).astype(BF16)
+        return carry
+
+    lax.fori_loop(0, blocks, mark, 0)
     row = lax.broadcasted_iota(jnp.int32, (z.rows, 1), 0)
     late = row - z.prompt
     step = late // z.row_total
@@ -274,47 +300,97 @@
         & (late_slot // z.rows_own <= step)
     )
     extra_ref[...] = jnp.where(from_prompt | from_decode, 0.0, MASKED)
-
-
-def attention_kernel(z, pieces, stacked, chunk, *refs):
-    key_ref, value_ref, bias_ref, extra_key_ref, extra_value_ref, extra_bias_ref = refs[:6]
+    for load in loads:
+        load.wait()
+    stand_in = jnp.broadcast_to(key_ref[0:16, :].astype(F32)[0:1, :], (size, HD))
+
+    def clear(i, carry):
+        rows = pl.ds(pl.multiple_of(i * size, size), size)
+        live = local + i * size < length
+        key_ref[rows, :] = jnp.where(live, key_ref[rows, :].astype(F32), stand_in).astype(BF16)
+        value_ref[rows, :] = jnp.where(live, value_ref[rows, :].astype(F32), 0.0).astype(BF16)
+        return carry
+
+    lax.fori_loop(length // size, blocks, clear, 0)
+
+
+def beside(values, live):
+    return jnp.concatenate([values, live], axis=1)
+
+
+def attention_kernel(z, pieces, stacked, *refs):
+    key_ref, value_ref, live_ref, extra_key_ref, extra_value_ref, extra_bias_ref = refs[:6]
     query_refs = refs[6 : 6 + len(pieces)]
     out_refs = refs[6 + len(pieces) :]
     me = lax.axis_index("ctx")
     over = (((1,), (1,)), ((), ()))
-    for i, d in enumerate(pieces):
-        query = query_refs[i][...]
+    slots = key_ref.shape[0]
+
+    def scores(query, rows):
+        return lax.dot_general(query, key_ref[rows, :], over, preferred_element_type=F32)
+
+    def mix(weight, rows):
+        return jnp.dot(
+            weight.astype(BF16), beside(value_ref[rows, :], live_ref[rows, :]),
+            preferred_element_type=F32,
+        )
+
+    def extras(query, d):
         half = jnp.bitwise_xor(me, d) // z.heads
-        extra_bias = extra_bias_ref[pl.ds(pl.multiple_of(half * z.piece, 8), z.piece), :]
-        found = []
-        blocks = [
-            (key_ref, value_ref, start, chunk) for start in range(0, key_ref.shape[0], chunk)
-        ]
-        blocks.append((extra_key_ref, extra_value_ref, 0, z.slots))
-        for keys, values, start, size in blocks:
-            score = lax.dot_general(
-                query, keys[start : start + size, :], over, preferred_element_type=F32
-            )
-            if keys is key_ref:
-                score = score + bias_ref[:, start : start + size]
-            else:
-                score = score + extra_bias
-            top = jnp.max(score, axis=1, keepdims=True)
-            weight = jnp.exp2(score - top).astype(BF16)
-            beside = jnp.concatenate(
-                [values[start : start + size, :], jnp.ones((size, HD), BF16)], axis=1
-            )
-            found.append((top, jnp.dot(weight, beside, preferred_element_type=F32)))
-        highest = functools.reduce(jnp.maximum, [top for top, _ in found])
-        mixed = 0.0
-        for top, block in found:
-            mixed = mixed + block * jnp.exp2(top - highest)
-        stats = stack_stats([column_to_rows(highest), column_to_rows(mixed[:, HD : HD + 1])])
+        bias = extra_bias_ref[pl.ds(pl.multiple_of(half * z.piece, 8), z.piece), :]
+        score = lax.dot_general(query, extra_key_ref[...], over, preferred_element_type=F32)
+        return score + bias
+
+    def mix_extras(weight):
+        ones = jnp.ones((z.slots, HD), BF16)
+        return jnp.dot(
+            weight.astype(BF16), beside(extra_value_ref[...], ones), preferred_element_type=F32
+        )
+
+    def write(i, level, mixed):
+        stats = stack_stats([column_to_rows(level * SCALE), column_to_rows(mixed[:, HD : HD + 1])])
         message = jnp.concatenate([mixed[:, :HD], stats], axis=0).astype(BF16)
         if stacked:
             out_refs[0][i] = message
         else:
             out_refs[i][...] = message
+
+    first = min(FIRST, slots)
+    chunk = min(CHUNK, slots)
+    bounds = [0, first] + [k for k in range(chunk, slots + 1, chunk) if k > first]
+    worst = None
+    for i, d in enumerate(pieces):
+        query = query_refs[i][...]
+        score = scores(query, slice(0, first))
+        level = jnp.max(score, axis=1, keepdims=True)
+        mixed = mix(jnp.exp2((score - level) * SCALE), slice(0, first))
+        for start, end in zip(bounds[1:], bounds[2:]):
+            rows = slice(start, end)
+            mixed = mixed + mix(jnp.exp2((scores(query, rows) - level) * SCALE), rows)
+        mixed = mixed + mix_extras(jnp.exp2((extras(query, d) - level) * SCALE))
+        write(i, level, mixed)
+        over_limit = jnp.where(mixed[:, HD:] < TOO_LARGE, 0.0, 1.0)
+        worst = over_limit if worst is None else jnp.maximum(worst, over_limit)
+
+    @pl.when(jnp.max(worst) > 0.0)
+    def _():
+        for i, d in enumerate(pieces):
+            query = query_refs[i][...]
+            score = extras(query, d)
+            level = jnp.max(score, axis=1, keepdims=True)
+            mixed = mix_extras(jnp.exp2((score - level) * SCALE))
+
+            def step(k, carry):
+                level, mixed = carry
+                rows = pl.ds(pl.multiple_of(k * chunk, chunk), chunk)
+                score = scores(query, rows)
+                higher = jnp.maximum(level, jnp.max(score, axis=1, keepdims=True))
+                return higher, mixed * jnp.exp2((level - higher) * SCALE) + mix(
+                    jnp.exp2((score - higher) * SCALE), rows
+                )
+
+            level, mixed = lax.fori_loop(0, slots // chunk, step, (level, mixed))
+            write(i, level, mixed)
 
 
 def merge(z, messages):
@@ -353,7 +429,7 @@
 
 
 def share_order(groups):
-    return list(range(2, groups)) + [1, 0]
+    return list(range(groups - 1, -1, -1))
 
 
 def output_kernel(z, weight_ref, *refs):
@@ -441,19 +517,23 @@
     pairs = n // 2
 
     cache_slots = key_cache.shape[1]
-    def masks(lengths, seen):
+    cache = shape(cache_slots, HD, BF16)
+
+    def prepare(lengths, seen):
         return call(
-            functools.partial(mask_kernel, z),
-            [shape(1, cache_slots, F32), shape(z.rows, z.slots, F32)],
-            (lengths, seen.reshape(1, z.row_total)),
-            "masks",
+            functools.partial(prepare_kernel, z),
+            [cache, cache, cache, shape(z.rows, z.slots, F32)],
+            (lengths, seen.reshape(1, z.row_total), key_cache[0], value_cache[0]),
+            "prepare",
             1e6,
             smem=1,
+            far=2,
+            scratch=[pltpu.SemaphoreType.DMA((2,))],
         )
 
     even, odd = call(
         functools.partial(project_kernel, z),
-        [shape(z.project, HD, F32, pairs), shape(z.project, HD, BF16, pairs)],
+        [shape(z.project, HD, F32, pairs), shape(z.sent, HD, BF16, pairs)],
         (
             norm_gain.reshape(z.width // 128, 128),
             prompt_in,
@@ -482,15 +562,17 @@
     got = swap(odd, "ctx", n, 1)
     own, *sends = call(
         functools.partial(pair_sum_kernel, z),
-        [shape(z.project, HD, F32)] + [shape(z.project, HD, BF16)] * (pairs - 1),
+        [shape(z.project, HD, F32)] + [shape(z.sent, HD, BF16)] * (pairs - 1),
         (even, got),
         "pair_sum",
         1e6,
     )
     visible, *sends = lax.optimization_barrier((visible, *sends))
     gots = [swap(send, "ctx", n, 2 * (i + 1)) for i, send in enumerate(sends)]
-    bias, extra_bias = masks(cache_lengths, visible)
-    own, bias, extra_bias = lax.optimization_barrier((own, bias, extra_bias))
+    keys, values, live, extra_bias = prepare(cache_lengths, visible)
+    own, keys, values, live, extra_bias = lax.optimization_barrier(
+        (own, keys, values, live, extra_bias)
+    )
     query, extra_key, extra_value = call(
         functools.partial(finish_kernel, z, z.width * n),
         [shape(z.piece, HD, BF16), shape(z.slots, HD, BF16), shape(z.slots, HD, BF16)],
@@ -506,11 +588,10 @@
     def attend(pieces, stacked, name):
         message = shape(z.message, HD, BF16)
         outs = [shape(z.message, HD, BF16, len(pieces))] if stacked else [message] * len(pieces)
-        chunk = 1024 if cache_slots % 1024 == 0 else cache_slots
         return call(
-            functools.partial(attention_kernel, z, pieces, stacked, chunk),
+            functools.partial(attention_kernel, z, pieces, stacked),
             outs,
-            (key_cache[0], value_cache[0], bias, extra_key, extra_value, extra_bias)
+            (keys, values, live, extra_key, extra_value, extra_bias)
             + tuple(queries[d] for d in pieces),
             name,
             8 * len(pieces) * z.piece * cache_slots * HD,

time: 70.7 us -> 124 us (1.75)
  Pallas kernels: 28.3 us -> 82 us
    pallas_call x13, Pallas kernels: 28.3 us -> 82 us  [call(): pl.pallas_call(kernel, out_shape=out_shape, in_specs=[scalar] * smem + [w...]
  transfers between devices with their start and end apart: 26 -> 26, of which waited for: 11 -> 8; matrix products, arithmetic and copies ran while one was open for 0% -> 0% of each run, Pallas kernels for 33% -> 62%
where the time goes in v4:
time: 124 us
  Pallas kernels  82 us (66%)
  starting transfers between devices  22 us (18%)
  waiting for transfers between devices  18.7 us (15%)
  between operations  1.49 us (1%)
    pallas_call x13, Pallas kernels, call(): pl.pallas_call(kernel, out_shape=out_shape, in_specs=[scalar] * smem + [w...  82 us
    ppermute x26, starting transfers between devices, swap(): return lax.ppermute(x, axis, [(i, i ^ d) for i in range(size)])  22 us
    ppermute x26, waiting for transfers between devices, swap(): return lax.ppermute(x, axis, [(i, i ^ d) for i in range(size)])  18.7 us
  transfers between devices with their start and end apart: 26, of which 8 were waited for; matrix products, arithmetic and copies ran while one was open for 0% of the time, Pallas kernels for 62%

profile of v4, /device:TPU:0, one launch (start us, length us, event | category | flops | bytes accessed | tf_op | source)
XLA Modules:
  0.0 124.2 jit_solution(15253231947308636466)
XLA Ops:
  0.6 2.9 %project.1 = (f32[4,304,128]{2,1,0:T(8,128)S(1)}, bf16[4,528,128]{2,1,0:T(8,128)(2,1)S(1)}) custom-call(bf16[8,128]{1,0:T(8,128)(2,1)} %bitcast.9, bf16[128,1024]{1,0:T(8,128)(2,1)} %xp_hbm.1, bf16[96,1024]{1,0:T(8,128)(2,1)} %bitcast.8, bf16[1024,1024]{1,0:T(8,128)(2,1)} %wq_hbm.1, bf16[1024,128]{1,0:T(8,128)(2,1)} %wk_hbm.1, bf16[1024,128]{1,0:T(8,128)(2,1)} %wv_hbm.1), custom_call_target="tpu_custom_call" | custom-call | flops 587202560 | bytes 1048576 | tf_op jit(solution)/shard_map/project/pallas_call | solution.py:103
  3.5 0.5 collective-permute-start
  4.0 1.6 %collective-permute-done.got_ref = bf16[4,528,128]{2,1,0:T(8,128)(2,1)S(1)} collective-permute-done((bf16[4,528,128]{2,1,0:T(8,128)(2,1)S(1)}, bf16[4,528,128]{2,1,0:T(8,128)(2,1)S(1)}, u32[]{:S(2)}, u32[]{:S(2)}) %collective-permute-start) | collective-permute-done | bytes 540704 | tf_op jit(solution)/shard_map/ppermute | solution.py:498
  5.7 2.9 %collective-permute-start.1 = (bf16[528,128]{1,0:T(8,128)(2,1)S(1)}, bf16[528,128]{1,0:T(8,128)(2,1)S(1)}, u32[]{:S(2)}, u32[]{:S(2)}) collective-permute-start(bf16[528,128]{1,0:T(8,128)(2,1)S(1)} %get-tuple-element.58), channel_id=1, source_target_pairs={{0,8},{4,12},{8,0},{12,4},{16,24},{20,28},{24,16},{28,20},{1,9},{5... | collective-permute-start | bytes 405512 | tf_op jit(solution)/shard_map/ppermute | solution.py:498
  8.7 1.5 %collective-permute-start.2 = (bf16[528,128]{1,0:T(8,128)(2,1)S(1)}, bf16[528,128]{1,0:T(8,128)(2,1)S(1)}, u32[]{:S(2)}, u32[]{:S(2)}) collective-permute-start(bf16[528,128]{1,0:T(8,128)(2,1)S(1)} %get-tuple-element.59), channel_id=1, source_target_pairs={{0,16},{4,20},{8,24},{12,28},{16,0},{20,4},{24,8},{28,12},{1,17},{... | collective-permute-start | bytes 405512 | tf_op jit(solution)/shard_map/ppermute | solution.py:498
  10.9 2.2 %prepare.1 = (bf16[8192,128]{1,0:T(8,128)(2,1)S(1)}, bf16[8192,128]{1,0:T(8,128)(2,1)S(1)}, bf16[8192,128]{1,0:T(8,128)(2,1)S(1)}, f32[224,32]{1,0:T(8,128)S(1)}) custom-call(s32[1]{0:T(128)S(6)} %copy.13.length_ref, s32[1,32]{1,0:T(1,128)S(1)} %bitcast.5, bf16[8192,128]{1,0:T(8,128)(2,1)} %bitcast.6, bf16[8192,128]{1,0:T(8,128)(2,1)} %bitcast.7), custom_call_target="tpu_custom_call" | custom-call | flops 1000000 | bytes 1048576 | tf_op jit(solution)/shard_map/prepare/pallas_call | solution.py:103
  13.1 3.8 %collective-permute-done.2.refs_1_ = bf16[528,128]{1,0:T(8,128)(2,1)S(1)} collective-permute-done((bf16[528,128]{1,0:T(8,128)(2,1)S(1)}, bf16[528,128]{1,0:T(8,128)(2,1)S(1)}, u32[]{:S(2)}, u32[]{:S(2)}) %collective-permute-start.2) | collective-permute-done | bytes 135200 | tf_op jit(solution)/shard_map/ppermute | solution.py:498
  17.2 1.6 %collective-permute-start.7 = (bf16[224,128]{1,0:T(8,128)(2,1)S(1)}, bf16[224,128]{1,0:T(8,128)(2,1)S(1)}, u32[]{:S(2)}, u32[]{:S(2)}) collective-permute-start(bf16[224,128]{1,0:T(8,128)(2,1)S(1)} %get-tuple-element.75.refs_6_), channel_id=1, source_target_pairs={{0,24},{4,28},{8,16},{12,20},{16,8},{20,12},{24,0},{28,4},{1,25},{... | collective-permute-start | bytes 172040 | tf_op jit(solution)/shard_map/ppermute | solution.py:498
  18.7 1.2 collective-permute-start.6
  19.9 0.8 collective-permute-start.5
  20.7 9.4 %attend_core.1 = bf16[240,128]{1,0:T(8,128)(2,1)S(1)} custom-call(bf16[8192,128]{1,0:T(8,128)(2,1)S(1)} %get-tuple-element.54.refs_0_, bf16[8192,128]{1,0:T(8,128)(2,1)S(1)} %get-tuple-element.55.refs_1_, bf16[8192,128]{1,0:T(8,128)(2,1)S(1)} %get-tuple-element.56.refs_2_, bf16[32,128]{1,0:T(8,128)(2,1)S(1)} %get-tuple-element.61.refs_3_, ...), custom_call_target="tpu_custom_call" | custom-call | flops 1879048192 | bytes 1048576 | tf_op jit(solution)/shard_map/attend_core/pallas_call | solution.py:103
  30.3 0.5 collective-permute-start.9
  30.9 9.6 %attend_near.1.refs_0_ = bf16[1,240,128]{2,1,0:T(8,128)(2,1)S(1)} custom-call(bf16[8192,128]{1,0:T(8,128)(2,1)S(1)} %get-tuple-element.54.refs_0_, bf16[8192,128]{1,0:T(8,128)(2,1)S(1)} %get-tuple-element.55.refs_1_, bf16[8192,128]{1,0:T(8,128)(2,1)S(1)} %get-tuple-element.56.refs_2_, bf16[32,128]{1,0:T(8,128)(2,1)S(1)} %get-tuple-element.61.refs_3_, ...), custom_call_target="tpu_custom_call" | custom-call | flops 1879048192 | bytes 1048576 | tf_op jit(solution)/shard_map/attend_near/pallas_call | solution.py:103
  40.5 0.5 collective-permute-start.12
  41.0 27.4 %attend_odd0.1 = bf16[3,240,128]{2,1,0:T(8,128)(2,1)S(1)} custom-call(bf16[8192,128]{1,0:T(8,128)(2,1)S(1)} %get-tuple-element.54.refs_0_, bf16[8192,128]{1,0:T(8,128)(2,1)S(1)} %get-tuple-element.55.refs_1_, bf16[8192,128]{1,0:T(8,128)(2,1)S(1)} %get-tuple-element.56.refs_2_, bf16[32,128]{1,0:T(8,128)(2,1)S(1)} %get-tuple-element.61.refs_3_, ...), custom_call_target="tpu_custom_call" | custom-call | flops 5637144576 | bytes 1048576 | tf_op jit(solution)/shard_map/attend_odd0/pallas_call | solution.py:103
  68.6 18.4 %attend_even0.1.refs_1_ = bf16[2,240,128]{2,1,0:T(8,128)(2,1)S(1)} custom-call(bf16[8192,128]{1,0:T(8,128)(2,1)S(1)} %get-tuple-element.54.refs_0_, bf16[8192,128]{1,0:T(8,128)(2,1)S(1)} %get-tuple-element.55.refs_1_, bf16[8192,128]{1,0:T(8,128)(2,1)S(1)} %get-tuple-element.56.refs_2_, bf16[32,128]{1,0:T(8,128)(2,1)S(1)} %get-tuple-element.61.refs_3_, ...), custom_call_target="tpu_custom_call" | custom-call | flops 3758096384 | bytes 1048576 | tf_op jit(solution)/shard_map/attend_even0/pallas_call | solution.py:103
  87.4 1.3 %collective-permute-start.13 = (bf16[240,128]{1,0:T(8,128)(2,1)S(1)}, bf16[240,128]{1,0:T(8,128)(2,1)S(1)}, u32[]{:S(2)}, u32[]{:S(2)}) collective-permute-start(bf16[240,128]{1,0:T(8,128)(2,1)S(1)} %get-tuple-element.77), channel_id=1, source_target_pairs={{0,8},{4,12},{8,0},{12,4},{16,24},{20,28},{24,16},{28,20},{1,9},{5... | collective-permute-start | bytes 184328 | tf_op jit(solution)/shard_map/ppermute | solution.py:498
  89.1 1.9 %collective-permute-start.15 = (bf16[240,128]{1,0:T(8,128)(2,1)S(1)}, bf16[240,128]{1,0:T(8,128)(2,1)S(1)}, u32[]{:S(2)}, u32[]{:S(2)}) collective-permute-start(bf16[240,128]{1,0:T(8,128)(2,1)S(1)} %get-tuple-element.79), channel_id=1, source_target_pairs={{0,24},{4,28},{8,16},{12,20},{16,8},{20,12},{24,0},{28,4},{1,25},{... | collective-permute-start | bytes 184328 | tf_op jit(solution)/shard_map/ppermute | solution.py:498
  91.0 9.4 %attend_own.1.refs_0_ = bf16[240,128]{1,0:T(8,128)(2,1)S(1)} custom-call(bf16[8192,128]{1,0:T(8,128)(2,1)S(1)} %get-tuple-element.54.refs_0_, bf16[8192,128]{1,0:T(8,128)(2,1)S(1)} %get-tuple-element.55.refs_1_, bf16[8192,128]{1,0:T(8,128)(2,1)S(1)} %get-tuple-element.56.refs_2_, bf16[32,128]{1,0:T(8,128)(2,1)S(1)} %get-tuple-element.61.refs_3_, ...), custom_call_target="tpu_custom_call" | custom-call | flops 1879048192 | bytes 1048576 | tf_op jit(solution)/shard_map/attend_own/pallas_call | solution.py:103
  100.5 0.5 final_merge.1.refs_0_
  101.0 2.7 %collective-permute-start.19 = (bf16[224,128]{1,0:T(8,128)(2,1)S(1)}, bf16[224,128]{1,0:T(8,128)(2,1)S(1)}, u32[]{:S(2)}, u32[]{:S(2)}) collective-permute-start(bf16[224,128]{1,0:T(8,128)(2,1)S(1)} %final_merge.1.refs_0_), channel_id=1, source_target_pairs={{0,16},{4,20},{8,24},{12,28},{16,0},{20,4},{24,8},{28,12},{1,17},{... | collective-permute-start | bytes 172040 | tf_op jit(solution)/shard_map/ppermute | solution.py:498
  103.7 0.8 collective-permute-start.17
  104.5 2.2 %collective-permute-done.21.refs_6_ = bf16[224,128]{1,0:T(8,128)(2,1)S(1)} collective-permute-done((bf16[224,128]{1,0:T(8,128)(2,1)S(1)}, bf16[224,128]{1,0:T(8,128)(2,1)S(1)}, u32[]{:S(2)}, u32[]{:S(2)}) %collective-permute-start.21) | collective-permute-done | bytes 57376 | tf_op jit(solution)/shard_map/ppermute | solution.py:498
  106.7 0.5 collective-permute-start.20
  107.2 0.7 collective-permute-done.17.refs_2_
  108.1 1.1 collective-permute-done.18.refs_3_
  109.1 0.7 output.1
  109.8 3.7 %collective-permute-start.23 = (bf16[112,512]{1,0:T(8,128)(2,1)S(1)}, bf16[112,512]{1,0:T(8,128)(2,1)S(1)}, u32[]{:S(2)}, u32[]{:S(2)}) collective-permute-start(bf16[112,512]{1,0:T(8,128)(2,1)S(1)} %get-tuple-element.80), channel_id=1, source_target_pairs={{0,3},{1,2},{2,1},{3,0},{4,7},{5,6},{6,5},{7,4},{8,11},{9,10},{10,... | collective-permute-start | bytes 344072 | tf_op jit(solution)/shard_map/ppermute | solution.py:498
  113.5 0.8 collective-permute-start.25
  114.3 3.5 %collective-permute-done.23.refs_0_ = bf16[112,512]{1,0:T(8,128)(2,1)S(1)} collective-permute-done((bf16[112,512]{1,0:T(8,128)(2,1)S(1)}, bf16[112,512]{1,0:T(8,128)(2,1)S(1)}, u32[]{:S(2)}, u32[]{:S(2)}) %collective-permute-start.23) | collective-permute-done | bytes 114720 | tf_op jit(solution)/shard_map/ppermute | solution.py:498
  117.8 5.7 %collective-permute-done.24.refs_1_ = bf16[112,512]{1,0:T(8,128)(2,1)S(1)} collective-permute-done((bf16[112,512]{1,0:T(8,128)(2,1)S(1)}, bf16[112,512]{1,0:T(8,128)(2,1)S(1)}, u32[]{:S(2)}, u32[]{:S(2)}) %collective-permute-start.24) | collective-permute-done | bytes 114720 | tf_op jit(solution)/shard_map/ppermute | solution.py:498
  123.5 0.7 share_sum.1
  (37 shorter events, 1.8 us)
Async XLA Ops:
  0.6 10.2 %copy-start.1 = (s32[32]{0:T(128)S(1)}, s32[32]{0:T(128)}, u32[]{:S(2)}) copy-start(s32[32]{0:T(128)} %param.21) | copy-start | bytes 388
  3.5 2.1 %collective-permute-start = (bf16[4,528,128]{2,1,0:T(8,128)(2,1)S(1)}, bf16[4,528,128]{2,1,0:T(8,128)(2,1)S(1)}, u32[]{:S(2)}, u32[]{:S(2)}) collective-permute-start(bf16[4,528,128]{2,1,0:T(8,128)(2,1)S(1)} %get-tuple-element.44), channel_id=1, source_target_pairs={{0,4},{4,0},{8,12},{12,8},{16,20},{20,16},{24,28},{28,24},{1,5},{5... | collective-permute-start | bytes 1622024 | tf_op jit(solution)/shard_map/ppermute | solution.py:498
  5.7 7.4 %collective-permute-start.1 = (bf16[528,128]{1,0:T(8,128)(2,1)S(1)}, bf16[528,128]{1,0:T(8,128)(2,1)S(1)}, u32[]{:S(2)}, u32[]{:S(2)}) collective-permute-start(bf16[528,128]{1,0:T(8,128)(2,1)S(1)} %get-tuple-element.58), channel_id=1, source_target_pairs={{0,8},{4,12},{8,0},{12,4},{16,24},{20,28},{24,16},{28,20},{1,9},{5... | collective-permute-start | bytes 405512 | tf_op jit(solution)/shard_map/ppermute | solution.py:498
  8.7 8.2 %collective-permute-start.2 = (bf16[528,128]{1,0:T(8,128)(2,1)S(1)}, bf16[528,128]{1,0:T(8,128)(2,1)S(1)}, u32[]{:S(2)}, u32[]{:S(2)}) collective-permute-start(bf16[528,128]{1,0:T(8,128)(2,1)S(1)} %get-tuple-element.59), channel_id=1, source_target_pairs={{0,16},{4,20},{8,24},{12,28},{16,0},{20,4},{24,8},{28,12},{1,17},{... | collective-permute-start | bytes 405512 | tf_op jit(solution)/shard_map/ppermute | solution.py:498
  10.2 6.7 %collective-permute-start.3 = (bf16[528,128]{1,0:T(8,128)(2,1)S(1)}, bf16[528,128]{1,0:T(8,128)(2,1)S(1)}, u32[]{:S(2)}, u32[]{:S(2)}) collective-permute-start(bf16[528,128]{1,0:T(8,128)(2,1)S(1)} %get-tuple-element.60), channel_id=1, source_target_pairs={{0,24},{4,28},{8,16},{12,20},{16,8},{20,12},{24,0},{28,4},{1,25},{... | collective-permute-start | bytes 405512 | tf_op jit(solution)/shard_map/ppermute | solution.py:498
  17.1 3.6 %collective-permute-start.4 = (bf16[224,128]{1,0:T(8,128)(2,1)S(1)}, bf16[224,128]{1,0:T(8,128)(2,1)S(1)}, u32[]{:S(2)}, u32[]{:S(2)}) collective-permute-start(bf16[224,128]{1,0:T(8,128)(2,1)S(1)} %get-tuple-element.75.refs_6_), channel_id=1, source_target_pairs={{0,4},{4,0},{8,12},{12,8},{16,20},{20,16},{24,28},{28,24},{1,5},{5... | collective-permute-start | bytes 172040 | tf_op jit(solution)/shard_map/ppermute | solution.py:498
  17.2 13.0 %collective-permute-start.7 = (bf16[224,128]{1,0:T(8,128)(2,1)S(1)}, bf16[224,128]{1,0:T(8,128)(2,1)S(1)}, u32[]{:S(2)}, u32[]{:S(2)}) collective-permute-start(bf16[224,128]{1,0:T(8,128)(2,1)S(1)} %get-tuple-element.75.refs_6_), channel_id=1, source_target_pairs={{0,24},{4,28},{8,16},{12,20},{16,8},{20,12},{24,0},{28,4},{1,25},{... | collective-permute-start | bytes 172040 | tf_op jit(solution)/shard_map/ppermute | solution.py:498
  18.7 11.5 %collective-permute-start.6 = (bf16[224,128]{1,0:T(8,128)(2,1)S(1)}, bf16[224,128]{1,0:T(8,128)(2,1)S(1)}, u32[]{:S(2)}, u32[]{:S(2)}) collective-permute-start(bf16[224,128]{1,0:T(8,128)(2,1)S(1)} %get-tuple-element.75.refs_6_), channel_id=1, source_target_pairs={{0,16},{4,20},{8,24},{12,28},{16,0},{20,4},{24,8},{28,12},{1,17},{... | collective-permute-start | bytes 172040 | tf_op jit(solution)/shard_map/ppermute | solution.py:498
  19.9 10.3 %collective-permute-start.5 = (bf16[224,128]{1,0:T(8,128)(2,1)S(1)}, bf16[224,128]{1,0:T(8,128)(2,1)S(1)}, u32[]{:S(2)}, u32[]{:S(2)}) collective-permute-start(bf16[224,128]{1,0:T(8,128)(2,1)S(1)} %get-tuple-element.75.refs_6_), channel_id=1, source_target_pairs={{0,8},{4,12},{8,0},{12,4},{16,24},{20,28},{24,16},{28,20},{1,9},{5... | collective-permute-start | bytes 172040 | tf_op jit(solution)/shard_map/ppermute | solution.py:498
  30.2 10.8 %collective-permute-start.8 = (bf16[224,128]{1,0:T(8,128)(2,1)S(1)}, bf16[224,128]{1,0:T(8,128)(2,1)S(1)}, u32[]{:S(2)}, u32[]{:S(2)}) collective-permute-start(bf16[224,128]{1,0:T(8,128)(2,1)S(1)} %collective-permute-done.5.refs_6_), channel_id=1, source_target_pairs={{0,4},{4,0},{8,12},{12,8},{16,20},{20,16},{24,28},{28,24},{1,5},{5... | collective-permute-start | bytes 172040 | tf_op jit(solution)/shard_map/ppermute | solution.py:498
  30.3 10.7 %collective-permute-start.9 = (bf16[224,128]{1,0:T(8,128)(2,1)S(1)}, bf16[224,128]{1,0:T(8,128)(2,1)S(1)}, u32[]{:S(2)}, u32[]{:S(2)}) collective-permute-start(bf16[224,128]{1,0:T(8,128)(2,1)S(1)} %collective-permute-done.6.refs_6_), channel_id=1, source_target_pairs={{0,4},{4,0},{8,12},{12,8},{16,20},{20,16},{24,28},{28,24},{1,5},{5... | collective-permute-start | bytes 172040 | tf_op jit(solution)/shard_map/ppermute | solution.py:498
  30.8 10.2 %collective-permute-start.10 = (bf16[224,128]{1,0:T(8,128)(2,1)S(1)}, bf16[224,128]{1,0:T(8,128)(2,1)S(1)}, u32[]{:S(2)}, u32[]{:S(2)}) collective-permute-start(bf16[224,128]{1,0:T(8,128)(2,1)S(1)} %collective-permute-done.7.refs_7_), channel_id=1, source_target_pairs={{0,4},{4,0},{8,12},{12,8},{16,20},{20,16},{24,28},{28,24},{1,5},{5... | collective-permute-start | bytes 172040 | tf_op jit(solution)/shard_map/ppermute | solution.py:498
  40.5 59.9 %collective-permute-start.12 = (bf16[240,128]{1,0:T(8,128)(2,1)S(1)}, bf16[240,128]{1,0:T(8,128)(2,1)S(1)}, u32[]{:S(2)}, u32[]{:S(2)}) collective-permute-start(bf16[240,128]{1,0:T(8,128)(2,1)S(1)} %attend_core.1), channel_id=1, source_target_pairs={{0,4},{4,0},{8,12},{12,8},{16,20},{20,16},{24,28},{28,24},{1,5},{5... | collective-permute-start | bytes 184328 | tf_op jit(solution)/shard_map/ppermute | solution.py:498
  68.5 18.5 %collective-permute-start.11 = (bf16[3,240,128]{2,1,0:T(8,128)(2,1)S(1)}, bf16[3,240,128]{2,1,0:T(8,128)(2,1)S(1)}, u32[]{:S(2)}, u32[]{:S(2)}) collective-permute-start(bf16[3,240,128]{2,1,0:T(8,128)(2,1)S(1)} %attend_odd0.1), channel_id=1, source_target_pairs={{0,4},{4,0},{8,12},{12,8},{16,20},{20,16},{24,28},{28,24},{1,5},{5... | collective-permute-start | bytes 552968 | tf_op jit(solution)/shard_map/ppermute | solution.py:498
  87.4 21.7 %copy-start = (bf16[1024,1024]{1,0:T(8,128)(2,1)S(1)}, bf16[1024,1024]{1,0:T(8,128)(2,1)}, u32[]{:S(2)}) copy-start(bf16[1024,1024]{1,0:T(8,128)(2,1)} %weight_ref.1) | copy-start | bytes 6291460
  87.4 13.0 %collective-permute-start.13 = (bf16[240,128]{1,0:T(8,128)(2,1)S(1)}, bf16[240,128]{1,0:T(8,128)(2,1)S(1)}, u32[]{:S(2)}, u32[]{:S(2)}) collective-permute-start(bf16[240,128]{1,0:T(8,128)(2,1)S(1)} %get-tuple-element.77), channel_id=1, source_target_pairs={{0,8},{4,12},{8,0},{12,4},{16,24},{20,28},{24,16},{28,20},{1,9},{5... | collective-permute-start | bytes 184328 | tf_op jit(solution)/shard_map/ppermute | solution.py:498
  88.7 11.7 %collective-permute-start.14 = (bf16[240,128]{1,0:T(8,128)(2,1)S(1)}, bf16[240,128]{1,0:T(8,128)(2,1)S(1)}, u32[]{:S(2)}, u32[]{:S(2)}) collective-permute-start(bf16[240,128]{1,0:T(8,128)(2,1)S(1)} %get-tuple-element.78), channel_id=1, source_target_pairs={{0,16},{4,20},{8,24},{12,28},{16,0},{20,4},{24,8},{28,12},{1,17},{... | collective-permute-start | bytes 184328 | tf_op jit(solution)/shard_map/ppermute | solution.py:498
  89.1 11.4 %collective-permute-start.15 = (bf16[240,128]{1,0:T(8,128)(2,1)S(1)}, bf16[240,128]{1,0:T(8,128)(2,1)S(1)}, u32[]{:S(2)}, u32[]{:S(2)}) collective-permute-start(bf16[240,128]{1,0:T(8,128)(2,1)S(1)} %get-tuple-element.79), channel_id=1, source_target_pairs={{0,24},{4,28},{8,16},{12,20},{16,8},{20,12},{24,0},{28,4},{1,25},{... | collective-permute-start | bytes 184328 | tf_op jit(solution)/shard_map/ppermute | solution.py:498
  100.9 5.7 %collective-permute-start.21 = (bf16[224,128]{1,0:T(8,128)(2,1)S(1)}, bf16[224,128]{1,0:T(8,128)(2,1)S(1)}, u32[]{:S(2)}, u32[]{:S(2)}) collective-permute-start(bf16[224,128]{1,0:T(8,128)(2,1)S(1)} %final_merge.1.refs_0_), channel_id=1, source_target_pairs={{0,24},{4,28},{8,16},{12,20},{16,8},{20,12},{24,0},{28,4},{1,25},{... | collective-permute-start | bytes 172040 | tf_op jit(solution)/shard_map/ppermute | solution.py:498
  101.0 5.6 %collective-permute-start.19 = (bf16[224,128]{1,0:T(8,128)(2,1)S(1)}, bf16[224,128]{1,0:T(8,128)(2,1)S(1)}, u32[]{:S(2)}, u32[]{:S(2)}) collective-permute-start(bf16[224,128]{1,0:T(8,128)(2,1)S(1)} %final_merge.1.refs_0_), channel_id=1, source_target_pairs={{0,16},{4,20},{8,24},{12,28},{16,0},{20,4},{24,8},{28,12},{1,17},{... | collective-permute-start | bytes 172040 | tf_op jit(solution)/shard_map/ppermute | solution.py:498
  103.7 4.2 %collective-permute-start.17 = (bf16[224,128]{1,0:T(8,128)(2,1)S(1)}, bf16[224,128]{1,0:T(8,128)(2,1)S(1)}, u32[]{:S(2)}, u32[]{:S(2)}) collective-permute-start(bf16[224,128]{1,0:T(8,128)(2,1)S(1)} %final_merge.1.refs_0_), channel_id=1, source_target_pairs={{0,8},{4,12},{8,0},{12,4},{16,24},{20,28},{24,16},{28,20},{1,9},{5... | collective-permute-start | bytes 172040 | tf_op jit(solution)/shard_map/ppermute | solution.py:498
  104.5 3.4 %collective-permute-start.16 = (bf16[224,128]{1,0:T(8,128)(2,1)S(1)}, bf16[224,128]{1,0:T(8,128)(2,1)S(1)}, u32[]{:S(2)}, u32[]{:S(2)}) collective-permute-start(bf16[224,128]{1,0:T(8,128)(2,1)S(1)} %final_merge.1.refs_0_), channel_id=1, source_target_pairs={{0,4},{4,0},{8,12},{12,8},{16,20},{20,16},{24,28},{28,24},{1,5},{5... | collective-permute-start | bytes 172040 | tf_op jit(solution)/shard_map/ppermute | solution.py:498
  106.6 1.2 %collective-permute-start.22 = (bf16[224,128]{1,0:T(8,128)(2,1)S(1)}, bf16[224,128]{1,0:T(8,128)(2,1)S(1)}, u32[]{:S(2)}, u32[]{:S(2)}) collective-permute-start(bf16[224,128]{1,0:T(8,128)(2,1)S(1)} %collective-permute-done.21.refs_6_), channel_id=1, source_target_pairs={{0,4},{4,0},{8,12},{12,8},{16,20},{20,16},{24,28},{28,24},{1,5},{5... | collective-permute-start | bytes 172040 | tf_op jit(solution)/shard_map/ppermute | solution.py:498
  106.7 1.4 %collective-permute-start.20 = (bf16[224,128]{1,0:T(8,128)(2,1)S(1)}, bf16[224,128]{1,0:T(8,128)(2,1)S(1)}, u32[]{:S(2)}, u32[]{:S(2)}) collective-permute-start(bf16[224,128]{1,0:T(8,128)(2,1)S(1)} %collective-permute-done.19.refs_4_), channel_id=1, source_target_pairs={{0,4},{4,0},{8,12},{12,8},{16,20},{20,16},{24,28},{28,24},{1,5},{5... | collective-permute-start | bytes 172040 | tf_op jit(solution)/shard_map/ppermute | solution.py:498
  107.9 1.2 %collective-permute-start.18 = (bf16[224,128]{1,0:T(8,128)(2,1)S(1)}, bf16[224,128]{1,0:T(8,128)(2,1)S(1)}, u32[]{:S(2)}, u32[]{:S(2)}) collective-permute-start(bf16[224,128]{1,0:T(8,128)(2,1)S(1)} %collective-permute-done.17.refs_2_), channel_id=1, source_target_pairs={{0,4},{4,0},{8,12},{12,8},{16,20},{20,16},{24,28},{28,24},{1,5},{5... | collective-permute-start | bytes 172040 | tf_op jit(solution)/shard_map/ppermute | solution.py:498
  109.8 7.9 %collective-permute-start.23 = (bf16[112,512]{1,0:T(8,128)(2,1)S(1)}, bf16[112,512]{1,0:T(8,128)(2,1)S(1)}, u32[]{:S(2)}, u32[]{:S(2)}) collective-permute-start(bf16[112,512]{1,0:T(8,128)(2,1)S(1)} %get-tuple-element.80), channel_id=1, source_target_pairs={{0,3},{1,2},{2,1},{3,0},{4,7},{5,6},{6,5},{7,4},{8,11},{9,10},{10,... | collective-permute-start | bytes 344072 | tf_op jit(solution)/shard_map/ppermute | solution.py:498
  113.5 10.0 %collective-permute-start.24 = (bf16[112,512]{1,0:T(8,128)(2,1)S(1)}, bf16[112,512]{1,0:T(8,128)(2,1)S(1)}, u32[]{:S(2)}, u32[]{:S(2)}) collective-permute-start(bf16[112,512]{1,0:T(8,128)(2,1)S(1)} %get-tuple-element.81), channel_id=1, source_target_pairs={{0,2},{1,3},{2,0},{3,1},{4,6},{5,7},{6,4},{7,5},{8,10},{9,11},{10,... | collective-permute-start | bytes 344072 | tf_op jit(solution)/shard_map/ppermute | solution.py:498
  113.5 10.0 %collective-permute-start.25 = (bf16[112,512]{1,0:T(8,128)(2,1)S(1)}, bf16[112,512]{1,0:T(8,128)(2,1)S(1)}, u32[]{:S(2)}, u32[]{:S(2)}) collective-permute-start(bf16[112,512]{1,0:T(8,128)(2,1)S(1)} %get-tuple-element.82), channel_id=1, source_target_pairs={{0,1},{1,0},{2,3},{3,2},{4,5},{5,4},{6,7},{7,6},{8,9},{9,8},{10,11... | collective-permute-start | bytes 344072 | tf_op jit(solution)/shard_map/ppermute | solution.py:498

commit v5 on v4

--- a/solution.py
+++ b/solution.py
@@ -318,10 +318,14 @@
     return jnp.concatenate([values, live], axis=1)
 
 
-def attention_kernel(z, pieces, stacked, *refs):
+def attention_kernel(z, pieces, stacked, offset, *refs):
     key_ref, value_ref, live_ref, extra_key_ref, extra_value_ref, extra_bias_ref = refs[:6]
-    query_refs = refs[6 : 6 + len(pieces)]
-    out_refs = refs[6 + len(pieces) :]
+    if offset is None:
+        query_refs = refs[6 : 6 + len(pieces)]
+        out_refs = refs[6 + len(pieces) :]
+    else:
+        query_refs = [refs[6].at[offset + i] for i in range(len(pieces))]
+        out_refs = refs[7:]
     me = lax.axis_index("ctx")
     over = (((1,), (1,)), ((), ()))
     slots = key_ref.shape[0]
@@ -428,38 +432,40 @@
     out_ref[...] = (mixed / rows_to_column(total, index)).astype(BF16)
 
 
+def pack_kernel(*refs):
+    for i, ref in enumerate(refs[:-1]):
+        refs[-1][i] = ref[...]
+
+
 def share_order(groups):
     return list(range(groups - 1, -1, -1))
 
 
-def output_kernel(z, weight_ref, *refs):
-    piece_refs = refs[: z.n]
-    *out_refs, sum_ref = refs[z.n :]
+def output_products(z, weight_ref, sum_ref, pieces):
     me = lax.axis_index("ctx")
-    if z.halves > 1:
-        sum_ref[...] = jnp.zeros_like(sum_ref)
-    total = None
-    swapped = me % 2 == 1
-    for d in range(0, z.n, 2):
-        owner = jnp.bitwise_xor(me, d)
-        first, second = piece_refs[d][...], piece_refs[d + 1][...]
-        both = jnp.where(
-            swapped,
-            jnp.concatenate([second, first], axis=1),
-            jnp.concatenate([first, second], axis=1),
+    for (d, first), (e, second) in zip(pieces[::2], pieces[1::2]):
+        owners = [jnp.bitwise_xor(me, d), jnp.bitwise_xor(me, e)]
+        weight = jnp.concatenate(
+            [weight_ref[pl.ds(pl.multiple_of(x % z.heads * HD, HD), HD), :] for x in owners], axis=0
         )
         product = jnp.dot(
-            both,
-            weight_ref[pl.ds(pl.multiple_of(owner % z.heads // 2 * 2 * HD, 2 * HD), 2 * HD), :],
-            preferred_element_type=F32,
-        )
-        if z.halves == 1:
-            total = product if total is None else total + product
-        else:
-            where = pl.ds(pl.multiple_of((owner // z.heads) * z.piece, 8), z.piece)
-            sum_ref[where, :] = sum_ref[where, :] + product
-    if z.halves == 1:
-        sum_ref[...] = total
+            jnp.concatenate([first[...], second[...]], axis=1), weight, preferred_element_type=F32
+        )
+        where = pl.ds(pl.multiple_of(owners[0] // z.heads * z.piece, 8), z.piece)
+        sum_ref[where, :] = sum_ref[where, :] + product
+
+
+def output_even_kernel(z, weight_ref, *refs):
+    *piece_refs, sum_ref = refs
+    sum_ref[...] = jnp.zeros_like(sum_ref)
+    output_products(z, weight_ref, sum_ref, list(zip(range(0, z.n, 2), piece_refs)))
+
+
+def output_odd_kernel(z, weight_ref, even_ref, first_ref, rest_ref, *refs):
+    *out_refs, sum_ref = refs
+    sum_ref[...] = even_ref[...]
+    pieces = [(1, first_ref)] + [(2 * i + 3, rest_ref.at[i]) for i in range(z.n // 2 - 1)]
+    output_products(z, weight_ref, sum_ref, pieces)
     place = lax.axis_index("kv")
     columns = sum_ref.shape[1]
     prompt_share = z.prompt // z.groups
@@ -585,14 +591,14 @@
     for i in range(1, pairs):
         queries[2 * i] = swap(query, "ctx", n, 2 * i)
 
-    def attend(pieces, stacked, name):
+    def attend(pieces, stacked, name, packed=None, offset=None):
         message = shape(z.message, HD, BF16)
         outs = [shape(z.message, HD, BF16, len(pieces))] if stacked else [message] * len(pieces)
         return call(
-            functools.partial(attention_kernel, z, pieces, stacked),
+            functools.partial(attention_kernel, z, pieces, stacked, offset),
             outs,
             (keys, values, live, extra_key, extra_value, extra_bias)
-            + tuple(queries[d] for d in pieces),
+            + (tuple(queries[d] for d in pieces) if packed is None else (packed,)),
             name,
             8 * len(pieces) * z.piece * cache_slots * HD,
             )
@@ -603,15 +609,19 @@
     )
     for i in range(1, pairs):
         queries[2 * i] = passed[i - 1]
-        queries[2 * i + 1] = swap(queries[2 * i], "ctx", n, 1)
+    packed = shape(z.piece, HD, BF16, pairs - 1)
+    (relay,) = call(pack_kernel, [packed], tuple(passed), "pack_queries", 1e5)
+    relayed = swap(relay, "ctx", n, 1)
     odd = [tuple(range(3, n, 2)[k : k + AT_ONCE]) for k in range(0, pairs - 1, AT_ONCE)]
     even = [(2,)] + [
         tuple(range(4, n, 2)[k : k + AT_ONCE]) for k in range(0, pairs - 2, AT_ONCE)
     ]
     early = attend(even[0], True, "attend_near")
-    early, *passed = lax.optimization_barrier((early, *[queries[d] for d in range(3, n, 2)]))
-    queries.update(zip(range(3, n, 2), passed))
-    rest_odd = [attend(pieces, True, f"attend_odd{k}")[0] for k, pieces in enumerate(odd)]
+    early, relayed = lax.optimization_barrier((early, relayed))
+    rest_odd = [
+        attend(pieces, True, f"attend_odd{k}", relayed, k * AT_ONCE)[0]
+        for k, pieces in enumerate(odd)
+    ]
     got_first = swap(first_odd, "ctx", n, 1)
     got_rest = [swap(block, "ctx", n, 1) for block in rest_odd]
     rest = list(early) + [
@@ -639,22 +649,29 @@
         "final_merge",
         1e6,
     )
-    heads = {0: attended}
-    for i in range(1, pairs):
-        heads[2 * i] = swap(attended, "ctx", n, 2 * i)
-    heads[1] = swap(attended, "ctx", n, 1)
-    for i in range(1, pairs):
-        heads[2 * i + 1] = swap(heads[2 * i], "ctx", n, 1)
+    even = [attended] + [swap(attended, "ctx", n, 2 * i) for i in range(1, pairs)]
+    first_odd = swap(attended, "ctx", n, 1)
+    (relay,) = call(pack_kernel, [packed], tuple(even[1:]), "pack_heads", 1e5)
+    relay, *even = lax.optimization_barrier((relay, *even))
+    rest_odd = swap(relay, "ctx", n, 1)
 
     columns = out_weight.shape[1]
     share_rows = 2 * z.rows // groups
     share = shape(share_rows, columns // 2, BF16)
+    flops = z.rows * z.heads * HD * columns
+    (total,) = call(
+        functools.partial(output_even_kernel, z),
+        [shape(z.rows, columns, F32)],
+        (out_weight, *even),
+        "output_even",
+        flops,
+    )
     shares = call(
-        functools.partial(output_kernel, z),
+        functools.partial(output_odd_kernel, z),
         [share] * groups,
-        (out_weight,) + tuple(heads[d] for d in range(n)),
-        "output",
-        2 * z.rows * z.heads * HD * columns,
+        (out_weight, total, first_odd, rest_odd),
+        "output_odd",
+        flops,
         scratch=[pltpu.VMEM((z.rows, columns), F32)],
     )
     shares = [

time: 124 us -> 124 us (level)
    pallas_call x13 -> x16, Pallas kernels: 82 us -> 82.6 us  [call(): pl.pallas_call(kernel, out_shape=out_shape, in_specs=[scalar] * smem + [w...]
    ppermute x26 -> x22, starting transfers between devices: 22 us -> 21.4 us  [swap(): return lax.ppermute(x, axis, [(i, i ^ d) for i in range(size)])]
    ppermute x26 -> x22, waiting for transfers between devices: 18.7 us -> 18.2 us  [swap(): return lax.ppermute(x, axis, [(i, i ^ d) for i in range(size)])]
  transfers between devices with their start and end apart: 26 -> 22, of which waited for: 8 -> 8; matrix products, arithmetic and copies ran while one was open for 0% -> 0% of each run, Pallas kernels for 62% -> 63%
where the time goes in v5:
time: 124 us
  Pallas kernels  82.6 us (67%)
  starting transfers between devices  21.4 us (17%)
  waiting for transfers between devices  18.2 us (15%)
  between operations  1.51 us (1%)
    pallas_call x16, Pallas kernels, call(): pl.pallas_call(kernel, out_shape=out_shape, in_specs=[scalar] * smem + [w...  82.6 us
    ppermute x22, starting transfers between devices, swap(): return lax.ppermute(x, axis, [(i, i ^ d) for i in range(size)])  21.4 us
    ppermute x22, waiting for transfers between devices, swap(): return lax.ppermute(x, axis, [(i, i ^ d) for i in range(size)])  18.2 us
  transfers between devices with their start and end apart: 22, of which 8 were waited for; matrix products, arithmetic and copies ran while one was open for 0% of the time, Pallas kernels for 63%

profile of v5, /device:TPU:0, one launch (start us, length us, event | category | flops | bytes accessed | tf_op | source)
XLA Modules:
  0.0 123.8 jit_solution(13250365838765616051)
XLA Ops:
  0.6 2.9 %project.1 = (f32[4,304,128]{2,1,0:T(8,128)S(1)}, bf16[4,528,128]{2,1,0:T(8,128)(2,1)S(1)}) custom-call(bf16[8,128]{1,0:T(8,128)(2,1)} %bitcast.9, bf16[128,1024]{1,0:T(8,128)(2,1)} %xp_hbm.1, bf16[96,1024]{1,0:T(8,128)(2,1)} %bitcast.8, bf16[1024,1024]{1,0:T(8,128)(2,1)} %wq_hbm.1, bf16[1024,128]{1,0:T(8,128)(2,1)} %wk_hbm.1, bf16[1024,128]{1,0:T(8,128)(2,1)} %wv_hbm.1), custom_call_target="tpu_custom_call" | custom-call | flops 587202560 | bytes 1048576 | tf_op jit(solution)/shard_map/project/pallas_call | solution.py:103
  3.5 0.5 collective-permute-start
  4.0 1.6 %collective-permute-done.got_ref = bf16[4,528,128]{2,1,0:T(8,128)(2,1)S(1)} collective-permute-done((bf16[4,528,128]{2,1,0:T(8,128)(2,1)S(1)}, bf16[4,528,128]{2,1,0:T(8,128)(2,1)S(1)}, u32[]{:S(2)}, u32[]{:S(2)}) %collective-permute-start) | collective-permute-done | bytes 540704 | tf_op jit(solution)/shard_map/ppermute | solution.py:504
  5.7 2.9 %collective-permute-start.1 = (bf16[528,128]{1,0:T(8,128)(2,1)S(1)}, bf16[528,128]{1,0:T(8,128)(2,1)S(1)}, u32[]{:S(2)}, u32[]{:S(2)}) collective-permute-start(bf16[528,128]{1,0:T(8,128)(2,1)S(1)} %get-tuple-element.61), channel_id=1, source_target_pairs={{0,8},{4,12},{8,0},{12,4},{16,24},{20,28},{24,16},{28,20},{1,9},{5... | collective-permute-start | bytes 405512 | tf_op jit(solution)/shard_map/ppermute | solution.py:504
  8.7 1.5 %collective-permute-start.2 = (bf16[528,128]{1,0:T(8,128)(2,1)S(1)}, bf16[528,128]{1,0:T(8,128)(2,1)S(1)}, u32[]{:S(2)}, u32[]{:S(2)}) collective-permute-start(bf16[528,128]{1,0:T(8,128)(2,1)S(1)} %get-tuple-element.62), channel_id=1, source_target_pairs={{0,16},{4,20},{8,24},{12,28},{16,0},{20,4},{24,8},{28,12},{1,17},{... | collective-permute-start | bytes 405512 | tf_op jit(solution)/shard_map/ppermute | solution.py:504
  10.9 2.6 %prepare.1 = (bf16[8192,128]{1,0:T(8,128)(2,1)S(1)}, bf16[8192,128]{1,0:T(8,128)(2,1)S(1)}, bf16[8192,128]{1,0:T(8,128)(2,1)S(1)}, f32[224,32]{1,0:T(8,128)S(1)}) custom-call(s32[1]{0:T(128)S(6)} %copy.13.length_ref, s32[1,32]{1,0:T(1,128)S(1)} %bitcast.5, bf16[8192,128]{1,0:T(8,128)(2,1)} %bitcast.6, bf16[8192,128]{1,0:T(8,128)(2,1)} %bitcast.7), custom_call_target="tpu_custom_call" | custom-call | flops 1000000 | bytes 1048576 | tf_op jit(solution)/shard_map/prepare/pallas_call | solution.py:103
  13.5 3.4 %collective-permute-done.2.refs_1_ = bf16[528,128]{1,0:T(8,128)(2,1)S(1)} collective-permute-done((bf16[528,128]{1,0:T(8,128)(2,1)S(1)}, bf16[528,128]{1,0:T(8,128)(2,1)S(1)}, u32[]{:S(2)}, u32[]{:S(2)}) %collective-permute-start.2) | collective-permute-done | bytes 135200 | tf_op jit(solution)/shard_map/ppermute | solution.py:504
  17.2 1.6 %collective-permute-start.7 = (bf16[224,128]{1,0:T(8,128)(2,1)S(1)}, bf16[224,128]{1,0:T(8,128)(2,1)S(1)}, u32[]{:S(2)}, u32[]{:S(2)}) collective-permute-start(bf16[224,128]{1,0:T(8,128)(2,1)S(1)} %get-tuple-element.76.refs_6_), channel_id=1, source_target_pairs={{0,24},{4,28},{8,16},{12,20},{16,8},{20,12},{24,0},{28,4},{1,25},{... | collective-permute-start | bytes 172040 | tf_op jit(solution)/shard_map/ppermute | solution.py:504
  18.7 1.2 collective-permute-start.6
  19.9 0.8 collective-permute-start.5
  20.7 9.4 %attend_core.1 = bf16[240,128]{1,0:T(8,128)(2,1)S(1)} custom-call(bf16[8192,128]{1,0:T(8,128)(2,1)S(1)} %get-tuple-element.57.refs_0_, bf16[8192,128]{1,0:T(8,128)(2,1)S(1)} %get-tuple-element.58.refs_1_, bf16[8192,128]{1,0:T(8,128)(2,1)S(1)} %get-tuple-element.59.refs_2_, bf16[32,128]{1,0:T(8,128)(2,1)S(1)} %get-tuple-element.64.refs_3_, ...), custom_call_target="tpu_custom_call" | custom-call | flops 1879048192 | bytes 1048576 | tf_op jit(solution)/shard_map/attend_core/pallas_call | solution.py:103
  30.3 0.6 collective-permute-start.8
  30.9 9.6 %attend_near.1.refs_0_ = bf16[1,240,128]{2,1,0:T(8,128)(2,1)S(1)} custom-call(bf16[8192,128]{1,0:T(8,128)(2,1)S(1)} %get-tuple-element.57.refs_0_, bf16[8192,128]{1,0:T(8,128)(2,1)S(1)} %get-tuple-element.58.refs_1_, bf16[8192,128]{1,0:T(8,128)(2,1)S(1)} %get-tuple-element.59.refs_2_, bf16[32,128]{1,0:T(8,128)(2,1)S(1)} %get-tuple-element.64.refs_3_, ...), custom_call_target="tpu_custom_call" | custom-call | flops 1879048192 | bytes 1048576 | tf_op jit(solution)/shard_map/attend_near/pallas_call | solution.py:103
  40.5 27.4 %attend_odd0.1 = bf16[3,240,128]{2,1,0:T(8,128)(2,1)S(1)} custom-call(bf16[8192,128]{1,0:T(8,128)(2,1)S(1)} %get-tuple-element.57.refs_0_, bf16[8192,128]{1,0:T(8,128)(2,1)S(1)} %get-tuple-element.58.refs_1_, bf16[8192,128]{1,0:T(8,128)(2,1)S(1)} %get-tuple-element.59.refs_2_, bf16[32,128]{1,0:T(8,128)(2,1)S(1)} %get-tuple-element.64.refs_3_, ...), custom_call_target="tpu_custom_call" | custom-call | flops 5637144576 | bytes 1048576 | tf_op jit(solution)/shard_map/attend_odd0/pallas_call | solution.py:103
  68.0 18.4 %attend_even0.1.refs_1_ = bf16[2,240,128]{2,1,0:T(8,128)(2,1)S(1)} custom-call(bf16[8192,128]{1,0:T(8,128)(2,1)S(1)} %get-tuple-element.57.refs_0_, bf16[8192,128]{1,0:T(8,128)(2,1)S(1)} %get-tuple-element.58.refs_1_, bf16[8192,128]{1,0:T(8,128)(2,1)S(1)} %get-tuple-element.59.refs_2_, bf16[32,128]{1,0:T(8,128)(2,1)S(1)} %get-tuple-element.64.refs_3_, ...), custom_call_target="tpu_custom_call" | custom-call | flops 3758096384 | bytes 1048576 | tf_op jit(solution)/shard_map/attend_even0/pallas_call | solution.py:103
  86.8 1.3 %collective-permute-start.11 = (bf16[240,128]{1,0:T(8,128)(2,1)S(1)}, bf16[240,128]{1,0:T(8,128)(2,1)S(1)}, u32[]{:S(2)}, u32[]{:S(2)}) collective-permute-start(bf16[240,128]{1,0:T(8,128)(2,1)S(1)} %get-tuple-element.78), channel_id=1, source_target_pairs={{0,8},{4,12},{8,0},{12,4},{16,24},{20,28},{24,16},{28,20},{1,9},{5... | collective-permute-start | bytes 184328 | tf_op jit(solution)/shard_map/ppermute | solution.py:504
  88.1 0.8 collective-permute-start.12
  88.9 1.4 %collective-permute-start.13 = (bf16[240,128]{1,0:T(8,128)(2,1)S(1)}, bf16[240,128]{1,0:T(8,128)(2,1)S(1)}, u32[]{:S(2)}, u32[]{:S(2)}) collective-permute-start(bf16[240,128]{1,0:T(8,128)(2,1)S(1)} %get-tuple-element.80), channel_id=1, source_target_pairs={{0,24},{4,28},{8,16},{12,20},{16,8},{20,12},{24,0},{28,4},{1,25},{... | collective-permute-start | bytes 184328 | tf_op jit(solution)/shard_map/ppermute | solution.py:504
  90.4 9.4 %attend_own.1.refs_0_ = bf16[240,128]{1,0:T(8,128)(2,1)S(1)} custom-call(bf16[8192,128]{1,0:T(8,128)(2,1)S(1)} %get-tuple-element.57.refs_0_, bf16[8192,128]{1,0:T(8,128)(2,1)S(1)} %get-tuple-element.58.refs_1_, bf16[8192,128]{1,0:T(8,128)(2,1)S(1)} %get-tuple-element.59.refs_2_, bf16[32,128]{1,0:T(8,128)(2,1)S(1)} %get-tuple-element.64.refs_3_, ...), custom_call_target="tpu_custom_call" | custom-call | flops 1879048192 | bytes 1048576 | tf_op jit(solution)/shard_map/attend_own/pallas_call | solution.py:103
  100.3 1.6 %collective-permute-start.16 = (bf16[224,128]{1,0:T(8,128)(2,1)S(1)}, bf16[224,128]{1,0:T(8,128)(2,1)S(1)}, u32[]{:S(2)}, u32[]{:S(2)}) collective-permute-start(bf16[224,128]{1,0:T(8,128)(2,1)S(1)} %final_merge.1.refs_0_), channel_id=1, source_target_pairs={{0,24},{4,28},{8,16},{12,20},{16,8},{20,12},{24,0},{28,4},{1,25},{... | collective-permute-start | bytes 172040 | tf_op jit(solution)/shard_map/ppermute | solution.py:504
  101.9 1.2 collective-permute-start.15
  103.1 0.8 collective-permute-start.14
  103.9 2.0 %collective-permute-done.16.refs_2_.refs_3_ = bf16[224,128]{1,0:T(8,128)(2,1)S(1)} collective-permute-done((bf16[224,128]{1,0:T(8,128)(2,1)S(1)}, bf16[224,128]{1,0:T(8,128)(2,1)S(1)}, u32[]{:S(2)}, u32[]{:S(2)}) %collective-permute-start.16) | collective-permute-done | bytes 57376 | tf_op jit(solution)/shard_map/ppermute | solution.py:504
  106.3 1.0 collective-permute-done.14.refs_0_.refs_1_
  107.3 0.5 collective-permute-start.17
  108.3 0.5 collective-permute-done.17.first_ref
  108.8 0.5 output_odd.1
  109.3 3.7 %collective-permute-start.19 = (bf16[112,512]{1,0:T(8,128)(2,1)S(1)}, bf16[112,512]{1,0:T(8,128)(2,1)S(1)}, u32[]{:S(2)}, u32[]{:S(2)}) collective-permute-start(bf16[112,512]{1,0:T(8,128)(2,1)S(1)} %get-tuple-element.86), channel_id=1, source_target_pairs={{0,3},{1,2},{2,1},{3,0},{4,7},{5,6},{6,5},{7,4},{8,11},{9,10},{10,... | collective-permute-start | bytes 344072 | tf_op jit(solution)/shard_map/ppermute | solution.py:504
  113.0 0.8 collective-permute-start.21
  113.8 3.5 %collective-permute-done.19.refs_0_ = bf16[112,512]{1,0:T(8,128)(2,1)S(1)} collective-permute-done((bf16[112,512]{1,0:T(8,128)(2,1)S(1)}, bf16[112,512]{1,0:T(8,128)(2,1)S(1)}, u32[]{:S(2)}, u32[]{:S(2)}) %collective-permute-start.19) | collective-permute-done | bytes 114720 | tf_op jit(solution)/shard_map/ppermute | solution.py:504
  117.2 5.8 %collective-permute-done.20.refs_1_ = bf16[112,512]{1,0:T(8,128)(2,1)S(1)} collective-permute-done((bf16[112,512]{1,0:T(8,128)(2,1)S(1)}, bf16[112,512]{1,0:T(8,128)(2,1)S(1)}, u32[]{:S(2)}, u32[]{:S(2)}) %collective-permute-start.20) | collective-permute-done | bytes 114720 | tf_op jit(solution)/shard_map/ppermute | solution.py:504
  123.1 0.7 share_sum.1
  (32 shorter events, 2.4 us)
Async XLA Ops:
  0.6 10.2 %copy-start.1 = (s32[32]{0:T(128)S(1)}, s32[32]{0:T(128)}, u32[]{:S(2)}) copy-start(s32[32]{0:T(128)} %param.21) | copy-start | bytes 388
  3.5 2.1 %collective-permute-start = (bf16[4,528,128]{2,1,0:T(8,128)(2,1)S(1)}, bf16[4,528,128]{2,1,0:T(8,128)(2,1)S(1)}, u32[]{:S(2)}, u32[]{:S(2)}) collective-permute-start(bf16[4,528,128]{2,1,0:T(8,128)(2,1)S(1)} %get-tuple-element.47), channel_id=1, source_target_pairs={{0,4},{4,0},{8,12},{12,8},{16,20},{20,16},{24,28},{28,24},{1,5},{5... | collective-permute-start | bytes 1622024 | tf_op jit(solution)/shard_map/ppermute | solution.py:504
  5.7 7.8 %collective-permute-start.1 = (bf16[528,128]{1,0:T(8,128)(2,1)S(1)}, bf16[528,128]{1,0:T(8,128)(2,1)S(1)}, u32[]{:S(2)}, u32[]{:S(2)}) collective-permute-start(bf16[528,128]{1,0:T(8,128)(2,1)S(1)} %get-tuple-element.61), channel_id=1, source_target_pairs={{0,8},{4,12},{8,0},{12,4},{16,24},{20,28},{24,16},{28,20},{1,9},{5... | collective-permute-start | bytes 405512 | tf_op jit(solution)/shard_map/ppermute | solution.py:504
  8.7 8.2 %collective-permute-start.2 = (bf16[528,128]{1,0:T(8,128)(2,1)S(1)}, bf16[528,128]{1,0:T(8,128)(2,1)S(1)}, u32[]{:S(2)}, u32[]{:S(2)}) collective-permute-start(bf16[528,128]{1,0:T(8,128)(2,1)S(1)} %get-tuple-element.62), channel_id=1, source_target_pairs={{0,16},{4,20},{8,24},{12,28},{16,0},{20,4},{24,8},{28,12},{1,17},{... | collective-permute-start | bytes 405512 | tf_op jit(solution)/shard_map/ppermute | solution.py:504
  10.2 6.7 %collective-permute-start.3 = (bf16[528,128]{1,0:T(8,128)(2,1)S(1)}, bf16[528,128]{1,0:T(8,128)(2,1)S(1)}, u32[]{:S(2)}, u32[]{:S(2)}) collective-permute-start(bf16[528,128]{1,0:T(8,128)(2,1)S(1)} %get-tuple-element.63), channel_id=1, source_target_pairs={{0,24},{4,28},{8,16},{12,20},{16,8},{20,12},{24,0},{28,4},{1,25},{... | collective-permute-start | bytes 405512 | tf_op jit(solution)/shard_map/ppermute | solution.py:504
  17.1 3.6 %collective-permute-start.4 = (bf16[224,128]{1,0:T(8,128)(2,1)S(1)}, bf16[224,128]{1,0:T(8,128)(2,1)S(1)}, u32[]{:S(2)}, u32[]{:S(2)}) collective-permute-start(bf16[224,128]{1,0:T(8,128)(2,1)S(1)} %get-tuple-element.76.refs_6_), channel_id=1, source_target_pairs={{0,4},{4,0},{8,12},{12,8},{16,20},{20,16},{24,28},{28,24},{1,5},{5... | collective-permute-start | bytes 172040 | tf_op jit(solution)/shard_map/ppermute | solution.py:504
  17.2 13.0 %collective-permute-start.7 = (bf16[224,128]{1,0:T(8,128)(2,1)S(1)}, bf16[224,128]{1,0:T(8,128)(2,1)S(1)}, u32[]{:S(2)}, u32[]{:S(2)}) collective-permute-start(bf16[224,128]{1,0:T(8,128)(2,1)S(1)} %get-tuple-element.76.refs_6_), channel_id=1, source_target_pairs={{0,24},{4,28},{8,16},{12,20},{16,8},{20,12},{24,0},{28,4},{1,25},{... | collective-permute-start | bytes 172040 | tf_op jit(solution)/shard_map/ppermute | solution.py:504
  18.7 11.5 %collective-permute-start.6 = (bf16[224,128]{1,0:T(8,128)(2,1)S(1)}, bf16[224,128]{1,0:T(8,128)(2,1)S(1)}, u32[]{:S(2)}, u32[]{:S(2)}) collective-permute-start(bf16[224,128]{1,0:T(8,128)(2,1)S(1)} %get-tuple-element.76.refs_6_), channel_id=1, source_target_pairs={{0,16},{4,20},{8,24},{12,28},{16,0},{20,4},{24,8},{28,12},{1,17},{... | collective-permute-start | bytes 172040 | tf_op jit(solution)/shard_map/ppermute | solution.py:504
  19.9 10.3 %collective-permute-start.5 = (bf16[224,128]{1,0:T(8,128)(2,1)S(1)}, bf16[224,128]{1,0:T(8,128)(2,1)S(1)}, u32[]{:S(2)}, u32[]{:S(2)}) collective-permute-start(bf16[224,128]{1,0:T(8,128)(2,1)S(1)} %get-tuple-element.76.refs_6_), channel_id=1, source_target_pairs={{0,8},{4,12},{8,0},{12,4},{16,24},{20,28},{24,16},{28,20},{1,9},{5... | collective-permute-start | bytes 172040 | tf_op jit(solution)/shard_map/ppermute | solution.py:504
  30.2 69.6 %collective-permute-start.10 = (bf16[240,128]{1,0:T(8,128)(2,1)S(1)}, bf16[240,128]{1,0:T(8,128)(2,1)S(1)}, u32[]{:S(2)}, u32[]{:S(2)}) collective-permute-start(bf16[240,128]{1,0:T(8,128)(2,1)S(1)} %attend_core.1), channel_id=1, source_target_pairs={{0,4},{4,0},{8,12},{12,8},{16,20},{20,16},{24,28},{28,24},{1,5},{5... | collective-permute-start | bytes 184328 | tf_op jit(solution)/shard_map/ppermute | solution.py:504
  30.3 10.2 %collective-permute-start.8 = (bf16[3,224,128]{2,1,0:T(8,128)(2,1)S(1)}, bf16[3,224,128]{2,1,0:T(8,128)(2,1)S(1)}, u32[]{:S(2)}, u32[]{:S(2)}) collective-permute-start(bf16[3,224,128]{2,1,0:T(8,128)(2,1)S(1)} %pack_queries.1), channel_id=1, source_target_pairs={{0,4},{4,0},{8,12},{12,8},{16,20},{20,16},{24,28},{28,24},{1,5},{5... | collective-permute-start | bytes 516104 | tf_op jit(solution)/shard_map/ppermute | solution.py:504
  67.9 18.5 %collective-permute-start.9 = (bf16[3,240,128]{2,1,0:T(8,128)(2,1)S(1)}, bf16[3,240,128]{2,1,0:T(8,128)(2,1)S(1)}, u32[]{:S(2)}, u32[]{:S(2)}) collective-permute-start(bf16[3,240,128]{2,1,0:T(8,128)(2,1)S(1)} %attend_odd0.1), channel_id=1, source_target_pairs={{0,4},{4,0},{8,12},{12,8},{16,20},{20,16},{24,28},{28,24},{1,5},{5... | collective-permute-start | bytes 552968 | tf_op jit(solution)/shard_map/ppermute | solution.py:504
  86.8 21.0 %copy-start = (bf16[1024,1024]{1,0:T(8,128)(2,1)S(1)}, bf16[1024,1024]{1,0:T(8,128)(2,1)}, u32[]{:S(2)}) copy-start(bf16[1024,1024]{1,0:T(8,128)(2,1)} %weight_ref.3) | copy-start | bytes 6291460
  86.8 13.0 %collective-permute-start.11 = (bf16[240,128]{1,0:T(8,128)(2,1)S(1)}, bf16[240,128]{1,0:T(8,128)(2,1)S(1)}, u32[]{:S(2)}, u32[]{:S(2)}) collective-permute-start(bf16[240,128]{1,0:T(8,128)(2,1)S(1)} %get-tuple-element.78), channel_id=1, source_target_pairs={{0,8},{4,12},{8,0},{12,4},{16,24},{20,28},{24,16},{28,20},{1,9},{5... | collective-permute-start | bytes 184328 | tf_op jit(solution)/shard_map/ppermute | solution.py:504
  88.1 11.7 %collective-permute-start.12 = (bf16[240,128]{1,0:T(8,128)(2,1)S(1)}, bf16[240,128]{1,0:T(8,128)(2,1)S(1)}, u32[]{:S(2)}, u32[]{:S(2)}) collective-permute-start(bf16[240,128]{1,0:T(8,128)(2,1)S(1)} %get-tuple-element.79), channel_id=1, source_target_pairs={{0,16},{4,20},{8,24},{12,28},{16,0},{20,4},{24,8},{28,12},{1,17},{... | collective-permute-start | bytes 184328 | tf_op jit(solution)/shard_map/ppermute | solution.py:504
  88.9 10.9 %collective-permute-start.13 = (bf16[240,128]{1,0:T(8,128)(2,1)S(1)}, bf16[240,128]{1,0:T(8,128)(2,1)S(1)}, u32[]{:S(2)}, u32[]{:S(2)}) collective-permute-start(bf16[240,128]{1,0:T(8,128)(2,1)S(1)} %get-tuple-element.80), channel_id=1, source_target_pairs={{0,24},{4,28},{8,16},{12,20},{16,8},{20,12},{24,0},{28,4},{1,25},{... | collective-permute-start | bytes 184328 | tf_op jit(solution)/shard_map/ppermute | solution.py:504
  100.3 5.6 %collective-permute-start.16 = (bf16[224,128]{1,0:T(8,128)(2,1)S(1)}, bf16[224,128]{1,0:T(8,128)(2,1)S(1)}, u32[]{:S(2)}, u32[]{:S(2)}) collective-permute-start(bf16[224,128]{1,0:T(8,128)(2,1)S(1)} %final_merge.1.refs_0_), channel_id=1, source_target_pairs={{0,24},{4,28},{8,16},{12,20},{16,8},{20,12},{24,0},{28,4},{1,25},{... | collective-permute-start | bytes 172040 | tf_op jit(solution)/shard_map/ppermute | solution.py:504
  101.9 4.4 %collective-permute-start.15 = (bf16[224,128]{1,0:T(8,128)(2,1)S(1)}, bf16[224,128]{1,0:T(8,128)(2,1)S(1)}, u32[]{:S(2)}, u32[]{:S(2)}) collective-permute-start(bf16[224,128]{1,0:T(8,128)(2,1)S(1)} %final_merge.1.refs_0_), channel_id=1, source_target_pairs={{0,16},{4,20},{8,24},{12,28},{16,0},{20,4},{24,8},{28,12},{1,17},{... | collective-permute-start | bytes 172040 | tf_op jit(solution)/shard_map/ppermute | solution.py:504
  103.1 4.2 %collective-permute-start.14 = (bf16[224,128]{1,0:T(8,128)(2,1)S(1)}, bf16[224,128]{1,0:T(8,128)(2,1)S(1)}, u32[]{:S(2)}, u32[]{:S(2)}) collective-permute-start(bf16[224,128]{1,0:T(8,128)(2,1)S(1)} %final_merge.1.refs_0_), channel_id=1, source_target_pairs={{0,8},{4,12},{8,0},{12,4},{16,24},{20,28},{24,16},{28,20},{1,9},{5... | collective-permute-start | bytes 172040 | tf_op jit(solution)/shard_map/ppermute | solution.py:504
  107.3 1.6 %collective-permute-start.18 = (bf16[3,224,128]{2,1,0:T(8,128)(2,1)S(1)}, bf16[3,224,128]{2,1,0:T(8,128)(2,1)S(1)}, u32[]{:S(2)}, u32[]{:S(2)}) collective-permute-start(bf16[3,224,128]{2,1,0:T(8,128)(2,1)S(1)} %pack_heads.1), channel_id=1, source_target_pairs={{0,4},{4,0},{8,12},{12,8},{16,20},{20,16},{24,28},{28,24},{1,5},{5... | collective-permute-start | bytes 516104 | tf_op jit(solution)/shard_map/ppermute | solution.py:504
  107.3 1.5 %collective-permute-start.17 = (bf16[224,128]{1,0:T(8,128)(2,1)S(1)}, bf16[224,128]{1,0:T(8,128)(2,1)S(1)}, u32[]{:S(2)}, u32[]{:S(2)}) collective-permute-start(bf16[224,128]{1,0:T(8,128)(2,1)S(1)} %final_merge.1.refs_0_), channel_id=1, source_target_pairs={{0,4},{4,0},{8,12},{12,8},{16,20},{20,16},{24,28},{28,24},{1,5},{5... | collective-permute-start | bytes 172040 | tf_op jit(solution)/shard_map/ppermute | solution.py:504
  109.3 7.9 %collective-permute-start.19 = (bf16[112,512]{1,0:T(8,128)(2,1)S(1)}, bf16[112,512]{1,0:T(8,128)(2,1)S(1)}, u32[]{:S(2)}, u32[]{:S(2)}) collective-permute-start(bf16[112,512]{1,0:T(8,128)(2,1)S(1)} %get-tuple-element.86), channel_id=1, source_target_pairs={{0,3},{1,2},{2,1},{3,0},{4,7},{5,6},{6,5},{7,4},{8,11},{9,10},{10,... | collective-permute-start | bytes 344072 | tf_op jit(solution)/shard_map/ppermute | solution.py:504
  113.0 10.1 %collective-permute-start.20 = (bf16[112,512]{1,0:T(8,128)(2,1)S(1)}, bf16[112,512]{1,0:T(8,128)(2,1)S(1)}, u32[]{:S(2)}, u32[]{:S(2)}) collective-permute-start(bf16[112,512]{1,0:T(8,128)(2,1)S(1)} %get-tuple-element.87), channel_id=1, source_target_pairs={{0,2},{1,3},{2,0},{3,1},{4,6},{5,7},{6,4},{7,5},{8,10},{9,11},{10,... | collective-permute-start | bytes 344072 | tf_op jit(solution)/shard_map/ppermute | solution.py:504
  113.0 10.1 %collective-permute-start.21 = (bf16[112,512]{1,0:T(8,128)(2,1)S(1)}, bf16[112,512]{1,0:T(8,128)(2,1)S(1)}, u32[]{:S(2)}, u32[]{:S(2)}) collective-permute-start(bf16[112,512]{1,0:T(8,128)(2,1)S(1)} %get-tuple-element.88), channel_id=1, source_target_pairs={{0,1},{1,0},{2,3},{3,2},{4,5},{5,4},{6,7},{7,6},{8,9},{9,8},{10,11... | collective-permute-start | bytes 344072 | tf_op jit(solution)/shard_map/ppermute | solution.py:504

commit v6 on v5

--- a/solution.py
+++ b/solution.py
@@ -438,7 +438,7 @@
 
 
 def share_order(groups):
-    return list(range(groups - 1, -1, -1))
+    return list(range(2, groups)) + [1, 0]
 
 
 def output_products(z, weight_ref, sum_ref, pieces):

time: 124 us -> 123 us (level)
  no operation moved by 1% of the time
where the time goes in v6:
time: 123 us
  Pallas kernels  82.3 us (67%)
  starting transfers between devices  21.2 us (17%)
  waiting for transfers between devices  17.6 us (14%)
  between operations  1.51 us (1%)
    pallas_call x16, Pallas kernels, call(): pl.pallas_call(kernel, out_shape=out_shape, in_specs=[scalar] * smem + [w...  82.3 us
    ppermute x22, starting transfers between devices, swap(): return lax.ppermute(x, axis, [(i, i ^ d) for i in range(size)])  21.2 us
    ppermute x22, waiting for transfers between devices, swap(): return lax.ppermute(x, axis, [(i, i ^ d) for i in range(size)])  17.6 us
  transfers between devices with their start and end apart: 22, of which 8 were waited for; matrix products, arithmetic and copies ran while one was open for 0% of the time, Pallas kernels for 63%

profile of v6, /device:TPU:0, one launch (start us, length us, event | category | flops | bytes accessed | tf_op | source)
XLA Modules:
  0.0 122.6 jit_solution(16228945863630642169)
XLA Ops:
  0.6 2.9 %project.1 = (f32[4,304,128]{2,1,0:T(8,128)S(1)}, bf16[4,528,128]{2,1,0:T(8,128)(2,1)S(1)}) custom-call(bf16[8,128]{1,0:T(8,128)(2,1)} %bitcast.9, bf16[128,1024]{1,0:T(8,128)(2,1)} %xp_hbm.1, bf16[96,1024]{1,0:T(8,128)(2,1)} %bitcast.8, bf16[1024,1024]{1,0:T(8,128)(2,1)} %wq_hbm.1, bf16[1024,128]{1,0:T(8,128)(2,1)} %wk_hbm.1, bf16[1024,128]{1,0:T(8,128)(2,1)} %wv_hbm.1), custom_call_target="tpu_custom_call" | custom-call | flops 587202560 | bytes 1048576 | tf_op jit(solution)/shard_map/project/pallas_call | solution.py:103
  3.5 0.5 collective-permute-start
  4.0 1.6 %collective-permute-done.got_ref = bf16[4,528,128]{2,1,0:T(8,128)(2,1)S(1)} collective-permute-done((bf16[4,528,128]{2,1,0:T(8,128)(2,1)S(1)}, bf16[4,528,128]{2,1,0:T(8,128)(2,1)S(1)}, u32[]{:S(2)}, u32[]{:S(2)}) %collective-permute-start) | collective-permute-done | bytes 540704 | tf_op jit(solution)/shard_map/ppermute | solution.py:504
  5.7 2.9 %collective-permute-start.1 = (bf16[528,128]{1,0:T(8,128)(2,1)S(1)}, bf16[528,128]{1,0:T(8,128)(2,1)S(1)}, u32[]{:S(2)}, u32[]{:S(2)}) collective-permute-start(bf16[528,128]{1,0:T(8,128)(2,1)S(1)} %get-tuple-element.61), channel_id=1, source_target_pairs={{0,8},{4,12},{8,0},{12,4},{16,24},{20,28},{24,16},{28,20},{1,9},{5... | collective-permute-start | bytes 405512 | tf_op jit(solution)/shard_map/ppermute | solution.py:504
  8.7 1.5 %collective-permute-start.2 = (bf16[528,128]{1,0:T(8,128)(2,1)S(1)}, bf16[528,128]{1,0:T(8,128)(2,1)S(1)}, u32[]{:S(2)}, u32[]{:S(2)}) collective-permute-start(bf16[528,128]{1,0:T(8,128)(2,1)S(1)} %get-tuple-element.62), channel_id=1, source_target_pairs={{0,16},{4,20},{8,24},{12,28},{16,0},{20,4},{24,8},{28,12},{1,17},{... | collective-permute-start | bytes 405512 | tf_op jit(solution)/shard_map/ppermute | solution.py:504
  10.9 2.3 %prepare.1 = (bf16[8192,128]{1,0:T(8,128)(2,1)S(1)}, bf16[8192,128]{1,0:T(8,128)(2,1)S(1)}, bf16[8192,128]{1,0:T(8,128)(2,1)S(1)}, f32[224,32]{1,0:T(8,128)S(1)}) custom-call(s32[1]{0:T(128)S(6)} %copy.13.length_ref, s32[1,32]{1,0:T(1,128)S(1)} %bitcast.5, bf16[8192,128]{1,0:T(8,128)(2,1)} %bitcast.6, bf16[8192,128]{1,0:T(8,128)(2,1)} %bitcast.7), custom_call_target="tpu_custom_call" | custom-call | flops 1000000 | bytes 1048576 | tf_op jit(solution)/shard_map/prepare/pallas_call | solution.py:103
  13.2 3.7 %collective-permute-done.2.refs_1_ = bf16[528,128]{1,0:T(8,128)(2,1)S(1)} collective-permute-done((bf16[528,128]{1,0:T(8,128)(2,1)S(1)}, bf16[528,128]{1,0:T(8,128)(2,1)S(1)}, u32[]{:S(2)}, u32[]{:S(2)}) %collective-permute-start.2) | collective-permute-done | bytes 135200 | tf_op jit(solution)/shard_map/ppermute | solution.py:504
  17.2 1.6 %collective-permute-start.7 = (bf16[224,128]{1,0:T(8,128)(2,1)S(1)}, bf16[224,128]{1,0:T(8,128)(2,1)S(1)}, u32[]{:S(2)}, u32[]{:S(2)}) collective-permute-start(bf16[224,128]{1,0:T(8,128)(2,1)S(1)} %get-tuple-element.76.refs_6_), channel_id=1, source_target_pairs={{0,24},{4,28},{8,16},{12,20},{16,8},{20,12},{24,0},{28,4},{1,25},{... | collective-permute-start | bytes 172040 | tf_op jit(solution)/shard_map/ppermute | solution.py:504
  18.7 1.2 collective-permute-start.6
  19.9 0.8 collective-permute-start.5
  20.7 9.4 %attend_core.1 = bf16[240,128]{1,0:T(8,128)(2,1)S(1)} custom-call(bf16[8192,128]{1,0:T(8,128)(2,1)S(1)} %get-tuple-element.57.refs_0_, bf16[8192,128]{1,0:T(8,128)(2,1)S(1)} %get-tuple-element.58.refs_1_, bf16[8192,128]{1,0:T(8,128)(2,1)S(1)} %get-tuple-element.59.refs_2_, bf16[32,128]{1,0:T(8,128)(2,1)S(1)} %get-tuple-element.64.refs_3_, ...), custom_call_target="tpu_custom_call" | custom-call | flops 1879048192 | bytes 1048576 | tf_op jit(solution)/shard_map/attend_core/pallas_call | solution.py:103
  30.3 0.6 collective-permute-start.8
  30.9 9.6 %attend_near.1.refs_0_ = bf16[1,240,128]{2,1,0:T(8,128)(2,1)S(1)} custom-call(bf16[8192,128]{1,0:T(8,128)(2,1)S(1)} %get-tuple-element.57.refs_0_, bf16[8192,128]{1,0:T(8,128)(2,1)S(1)} %get-tuple-element.58.refs_1_, bf16[8192,128]{1,0:T(8,128)(2,1)S(1)} %get-tuple-element.59.refs_2_, bf16[32,128]{1,0:T(8,128)(2,1)S(1)} %get-tuple-element.64.refs_3_, ...), custom_call_target="tpu_custom_call" | custom-call | flops 1879048192 | bytes 1048576 | tf_op jit(solution)/shard_map/attend_near/pallas_call | solution.py:103
  40.5 27.4 %attend_odd0.1 = bf16[3,240,128]{2,1,0:T(8,128)(2,1)S(1)} custom-call(bf16[8192,128]{1,0:T(8,128)(2,1)S(1)} %get-tuple-element.57.refs_0_, bf16[8192,128]{1,0:T(8,128)(2,1)S(1)} %get-tuple-element.58.refs_1_, bf16[8192,128]{1,0:T(8,128)(2,1)S(1)} %get-tuple-element.59.refs_2_, bf16[32,128]{1,0:T(8,128)(2,1)S(1)} %get-tuple-element.64.refs_3_, ...), custom_call_target="tpu_custom_call" | custom-call | flops 5637144576 | bytes 1048576 | tf_op jit(solution)/shard_map/attend_odd0/pallas_call | solution.py:103
  68.0 18.4 %attend_even0.1.refs_1_ = bf16[2,240,128]{2,1,0:T(8,128)(2,1)S(1)} custom-call(bf16[8192,128]{1,0:T(8,128)(2,1)S(1)} %get-tuple-element.57.refs_0_, bf16[8192,128]{1,0:T(8,128)(2,1)S(1)} %get-tuple-element.58.refs_1_, bf16[8192,128]{1,0:T(8,128)(2,1)S(1)} %get-tuple-element.59.refs_2_, bf16[32,128]{1,0:T(8,128)(2,1)S(1)} %get-tuple-element.64.refs_3_, ...), custom_call_target="tpu_custom_call" | custom-call | flops 3758096384 | bytes 1048576 | tf_op jit(solution)/shard_map/attend_even0/pallas_call | solution.py:103
  86.8 1.3 %collective-permute-start.11 = (bf16[240,128]{1,0:T(8,128)(2,1)S(1)}, bf16[240,128]{1,0:T(8,128)(2,1)S(1)}, u32[]{:S(2)}, u32[]{:S(2)}) collective-permute-start(bf16[240,128]{1,0:T(8,128)(2,1)S(1)} %get-tuple-element.78), channel_id=1, source_target_pairs={{0,8},{4,12},{8,0},{12,4},{16,24},{20,28},{24,16},{28,20},{1,9},{5... | collective-permute-start | bytes 184328 | tf_op jit(solution)/shard_map/ppermute | solution.py:504
  88.1 0.8 collective-permute-start.12
  88.9 1.4 %collective-permute-start.13 = (bf16[240,128]{1,0:T(8,128)(2,1)S(1)}, bf16[240,128]{1,0:T(8,128)(2,1)S(1)}, u32[]{:S(2)}, u32[]{:S(2)}) collective-permute-start(bf16[240,128]{1,0:T(8,128)(2,1)S(1)} %get-tuple-element.80), channel_id=1, source_target_pairs={{0,24},{4,28},{8,16},{12,20},{16,8},{20,12},{24,0},{28,4},{1,25},{... | collective-permute-start | bytes 184328 | tf_op jit(solution)/shard_map/ppermute | solution.py:504
  90.4 9.4 %attend_own.1.refs_0_ = bf16[240,128]{1,0:T(8,128)(2,1)S(1)} custom-call(bf16[8192,128]{1,0:T(8,128)(2,1)S(1)} %get-tuple-element.57.refs_0_, bf16[8192,128]{1,0:T(8,128)(2,1)S(1)} %get-tuple-element.58.refs_1_, bf16[8192,128]{1,0:T(8,128)(2,1)S(1)} %get-tuple-element.59.refs_2_, bf16[32,128]{1,0:T(8,128)(2,1)S(1)} %get-tuple-element.64.refs_3_, ...), custom_call_target="tpu_custom_call" | custom-call | flops 1879048192 | bytes 1048576 | tf_op jit(solution)/shard_map/attend_own/pallas_call | solution.py:103
  100.3 1.6 %collective-permute-start.16 = (bf16[224,128]{1,0:T(8,128)(2,1)S(1)}, bf16[224,128]{1,0:T(8,128)(2,1)S(1)}, u32[]{:S(2)}, u32[]{:S(2)}) collective-permute-start(bf16[224,128]{1,0:T(8,128)(2,1)S(1)} %final_merge.1.refs_0_), channel_id=1, source_target_pairs={{0,24},{4,28},{8,16},{12,20},{16,8},{20,12},{24,0},{28,4},{1,25},{... | collective-permute-start | bytes 172040 | tf_op jit(solution)/shard_map/ppermute | solution.py:504
  101.9 1.2 collective-permute-start.15
  103.1 0.8 collective-permute-start.14
  103.9 2.0 %collective-permute-done.16.refs_2_.refs_3_ = bf16[224,128]{1,0:T(8,128)(2,1)S(1)} collective-permute-done((bf16[224,128]{1,0:T(8,128)(2,1)S(1)}, bf16[224,128]{1,0:T(8,128)(2,1)S(1)}, u32[]{:S(2)}, u32[]{:S(2)}) %collective-permute-start.16) | collective-permute-done | bytes 57376 | tf_op jit(solution)/shard_map/ppermute | solution.py:504
  106.3 1.0 collective-permute-done.14.refs_0_.refs_1_
  107.3 0.5 collective-permute-start.17
  108.3 0.5 collective-permute-done.17.first_ref
  108.8 0.5 output_odd.1
  109.3 2.2 %collective-permute-start.19 = (bf16[112,512]{1,0:T(8,128)(2,1)S(1)}, bf16[112,512]{1,0:T(8,128)(2,1)S(1)}, u32[]{:S(2)}, u32[]{:S(2)}) collective-permute-start(bf16[112,512]{1,0:T(8,128)(2,1)S(1)} %get-tuple-element.86), channel_id=1, source_target_pairs={{0,2},{1,3},{2,0},{3,1},{4,6},{5,7},{6,4},{7,5},{8,10},{9,11},{10,... | collective-permute-start | bytes 344072 | tf_op jit(solution)/shard_map/ppermute | solution.py:504
  111.6 1.8 %collective-permute-start.20 = (bf16[112,512]{1,0:T(8,128)(2,1)S(1)}, bf16[112,512]{1,0:T(8,128)(2,1)S(1)}, u32[]{:S(2)}, u32[]{:S(2)}) collective-permute-start(bf16[112,512]{1,0:T(8,128)(2,1)S(1)} %get-tuple-element.87), channel_id=1, source_target_pairs={{0,3},{1,2},{2,1},{3,0},{4,7},{5,6},{6,5},{7,4},{8,11},{9,10},{10,... | collective-permute-start | bytes 344072 | tf_op jit(solution)/shard_map/ppermute | solution.py:504
  113.5 7.7 %collective-permute-done.19.refs_0_ = bf16[112,512]{1,0:T(8,128)(2,1)S(1)} collective-permute-done((bf16[112,512]{1,0:T(8,128)(2,1)S(1)}, bf16[112,512]{1,0:T(8,128)(2,1)S(1)}, u32[]{:S(2)}, u32[]{:S(2)}) %collective-permute-start.19) | collective-permute-done | bytes 114720 | tf_op jit(solution)/shard_map/ppermute | solution.py:504
  121.2 0.7 collective-permute-done.21.refs_2_
  121.9 0.7 share_sum.1
  (32 shorter events, 2.6 us)
Async XLA Ops:
  0.6 10.2 %copy-start.1 = (s32[32]{0:T(128)S(1)}, s32[32]{0:T(128)}, u32[]{:S(2)}) copy-start(s32[32]{0:T(128)} %param.21) | copy-start | bytes 388
  3.5 2.1 %collective-permute-start = (bf16[4,528,128]{2,1,0:T(8,128)(2,1)S(1)}, bf16[4,528,128]{2,1,0:T(8,128)(2,1)S(1)}, u32[]{:S(2)}, u32[]{:S(2)}) collective-permute-start(bf16[4,528,128]{2,1,0:T(8,128)(2,1)S(1)} %get-tuple-element.47), channel_id=1, source_target_pairs={{0,4},{4,0},{8,12},{12,8},{16,20},{20,16},{24,28},{28,24},{1,5},{5... | collective-permute-start | bytes 1622024 | tf_op jit(solution)/shard_map/ppermute | solution.py:504
  5.7 7.5 %collective-permute-start.1 = (bf16[528,128]{1,0:T(8,128)(2,1)S(1)}, bf16[528,128]{1,0:T(8,128)(2,1)S(1)}, u32[]{:S(2)}, u32[]{:S(2)}) collective-permute-start(bf16[528,128]{1,0:T(8,128)(2,1)S(1)} %get-tuple-element.61), channel_id=1, source_target_pairs={{0,8},{4,12},{8,0},{12,4},{16,24},{20,28},{24,16},{28,20},{1,9},{5... | collective-permute-start | bytes 405512 | tf_op jit(solution)/shard_map/ppermute | solution.py:504
  8.7 8.2 %collective-permute-start.2 = (bf16[528,128]{1,0:T(8,128)(2,1)S(1)}, bf16[528,128]{1,0:T(8,128)(2,1)S(1)}, u32[]{:S(2)}, u32[]{:S(2)}) collective-permute-start(bf16[528,128]{1,0:T(8,128)(2,1)S(1)} %get-tuple-element.62), channel_id=1, source_target_pairs={{0,16},{4,20},{8,24},{12,28},{16,0},{20,4},{24,8},{28,12},{1,17},{... | collective-permute-start | bytes 405512 | tf_op jit(solution)/shard_map/ppermute | solution.py:504
  10.2 6.7 %collective-permute-start.3 = (bf16[528,128]{1,0:T(8,128)(2,1)S(1)}, bf16[528,128]{1,0:T(8,128)(2,1)S(1)}, u32[]{:S(2)}, u32[]{:S(2)}) collective-permute-start(bf16[528,128]{1,0:T(8,128)(2,1)S(1)} %get-tuple-element.63), channel_id=1, source_target_pairs={{0,24},{4,28},{8,16},{12,20},{16,8},{20,12},{24,0},{28,4},{1,25},{... | collective-permute-start | bytes 405512 | tf_op jit(solution)/shard_map/ppermute | solution.py:504
  17.1 3.6 %collective-permute-start.4 = (bf16[224,128]{1,0:T(8,128)(2,1)S(1)}, bf16[224,128]{1,0:T(8,128)(2,1)S(1)}, u32[]{:S(2)}, u32[]{:S(2)}) collective-permute-start(bf16[224,128]{1,0:T(8,128)(2,1)S(1)} %get-tuple-element.76.refs_6_), channel_id=1, source_target_pairs={{0,4},{4,0},{8,12},{12,8},{16,20},{20,16},{24,28},{28,24},{1,5},{5... | collective-permute-start | bytes 172040 | tf_op jit(solution)/shard_map/ppermute | solution.py:504
  17.2 13.0 %collective-permute-start.7 = (bf16[224,128]{1,0:T(8,128)(2,1)S(1)}, bf16[224,128]{1,0:T(8,128)(2,1)S(1)}, u32[]{:S(2)}, u32[]{:S(2)}) collective-permute-start(bf16[224,128]{1,0:T(8,128)(2,1)S(1)} %get-tuple-element.76.refs_6_), channel_id=1, source_target_pairs={{0,24},{4,28},{8,16},{12,20},{16,8},{20,12},{24,0},{28,4},{1,25},{... | collective-permute-start | bytes 172040 | tf_op jit(solution)/shard_map/ppermute | solution.py:504
  18.7 11.5 %collective-permute-start.6 = (bf16[224,128]{1,0:T(8,128)(2,1)S(1)}, bf16[224,128]{1,0:T(8,128)(2,1)S(1)}, u32[]{:S(2)}, u32[]{:S(2)}) collective-permute-start(bf16[224,128]{1,0:T(8,128)(2,1)S(1)} %get-tuple-element.76.refs_6_), channel_id=1, source_target_pairs={{0,16},{4,20},{8,24},{12,28},{16,0},{20,4},{24,8},{28,12},{1,17},{... | collective-permute-start | bytes 172040 | tf_op jit(solution)/shard_map/ppermute | solution.py:504
  19.9 10.3 %collective-permute-start.5 = (bf16[224,128]{1,0:T(8,128)(2,1)S(1)}, bf16[224,128]{1,0:T(8,128)(2,1)S(1)}, u32[]{:S(2)}, u32[]{:S(2)}) collective-permute-start(bf16[224,128]{1,0:T(8,128)(2,1)S(1)} %get-tuple-element.76.refs_6_), channel_id=1, source_target_pairs={{0,8},{4,12},{8,0},{12,4},{16,24},{20,28},{24,16},{28,20},{1,9},{5... | collective-permute-start | bytes 172040 | tf_op jit(solution)/shard_map/ppermute | solution.py:504
  30.2 69.6 %collective-permute-start.10 = (bf16[240,128]{1,0:T(8,128)(2,1)S(1)}, bf16[240,128]{1,0:T(8,128)(2,1)S(1)}, u32[]{:S(2)}, u32[]{:S(2)}) collective-permute-start(bf16[240,128]{1,0:T(8,128)(2,1)S(1)} %attend_core.1), channel_id=1, source_target_pairs={{0,4},{4,0},{8,12},{12,8},{16,20},{20,16},{24,28},{28,24},{1,5},{5... | collective-permute-start | bytes 184328 | tf_op jit(solution)/shard_map/ppermute | solution.py:504
  30.3 10.2 %collective-permute-start.8 = (bf16[3,224,128]{2,1,0:T(8,128)(2,1)S(1)}, bf16[3,224,128]{2,1,0:T(8,128)(2,1)S(1)}, u32[]{:S(2)}, u32[]{:S(2)}) collective-permute-start(bf16[3,224,128]{2,1,0:T(8,128)(2,1)S(1)} %pack_queries.1), channel_id=1, source_target_pairs={{0,4},{4,0},{8,12},{12,8},{16,20},{20,16},{24,28},{28,24},{1,5},{5... | collective-permute-start | bytes 516104 | tf_op jit(solution)/shard_map/ppermute | solution.py:504
  67.9 18.5 %collective-permute-start.9 = (bf16[3,240,128]{2,1,0:T(8,128)(2,1)S(1)}, bf16[3,240,128]{2,1,0:T(8,128)(2,1)S(1)}, u32[]{:S(2)}, u32[]{:S(2)}) collective-permute-start(bf16[3,240,128]{2,1,0:T(8,128)(2,1)S(1)} %attend_odd0.1), channel_id=1, source_target_pairs={{0,4},{4,0},{8,12},{12,8},{16,20},{20,16},{24,28},{28,24},{1,5},{5... | collective-permute-start | bytes 552968 | tf_op jit(solution)/shard_map/ppermute | solution.py:504
  86.8 21.0 %copy-start = (bf16[1024,1024]{1,0:T(8,128)(2,1)S(1)}, bf16[1024,1024]{1,0:T(8,128)(2,1)}, u32[]{:S(2)}) copy-start(bf16[1024,1024]{1,0:T(8,128)(2,1)} %weight_ref.3) | copy-start | bytes 6291460
  86.8 13.0 %collective-permute-start.11 = (bf16[240,128]{1,0:T(8,128)(2,1)S(1)}, bf16[240,128]{1,0:T(8,128)(2,1)S(1)}, u32[]{:S(2)}, u32[]{:S(2)}) collective-permute-start(bf16[240,128]{1,0:T(8,128)(2,1)S(1)} %get-tuple-element.78), channel_id=1, source_target_pairs={{0,8},{4,12},{8,0},{12,4},{16,24},{20,28},{24,16},{28,20},{1,9},{5... | collective-permute-start | bytes 184328 | tf_op jit(solution)/shard_map/ppermute | solution.py:504
  88.1 11.7 %collective-permute-start.12 = (bf16[240,128]{1,0:T(8,128)(2,1)S(1)}, bf16[240,128]{1,0:T(8,128)(2,1)S(1)}, u32[]{:S(2)}, u32[]{:S(2)}) collective-permute-start(bf16[240,128]{1,0:T(8,128)(2,1)S(1)} %get-tuple-element.79), channel_id=1, source_target_pairs={{0,16},{4,20},{8,24},{12,28},{16,0},{20,4},{24,8},{28,12},{1,17},{... | collective-permute-start | bytes 184328 | tf_op jit(solution)/shard_map/ppermute | solution.py:504
  88.9 10.9 %collective-permute-start.13 = (bf16[240,128]{1,0:T(8,128)(2,1)S(1)}, bf16[240,128]{1,0:T(8,128)(2,1)S(1)}, u32[]{:S(2)}, u32[]{:S(2)}) collective-permute-start(bf16[240,128]{1,0:T(8,128)(2,1)S(1)} %get-tuple-element.80), channel_id=1, source_target_pairs={{0,24},{4,28},{8,16},{12,20},{16,8},{20,12},{24,0},{28,4},{1,25},{... | collective-permute-start | bytes 184328 | tf_op jit(solution)/shard_map/ppermute | solution.py:504
  100.3 5.6 %collective-permute-start.16 = (bf16[224,128]{1,0:T(8,128)(2,1)S(1)}, bf16[224,128]{1,0:T(8,128)(2,1)S(1)}, u32[]{:S(2)}, u32[]{:S(2)}) collective-permute-start(bf16[224,128]{1,0:T(8,128)(2,1)S(1)} %final_merge.1.refs_0_), channel_id=1, source_target_pairs={{0,24},{4,28},{8,16},{12,20},{16,8},{20,12},{24,0},{28,4},{1,25},{... | collective-permute-start | bytes 172040 | tf_op jit(solution)/shard_map/ppermute | solution.py:504
  101.9 4.4 %collective-permute-start.15 = (bf16[224,128]{1,0:T(8,128)(2,1)S(1)}, bf16[224,128]{1,0:T(8,128)(2,1)S(1)}, u32[]{:S(2)}, u32[]{:S(2)}) collective-permute-start(bf16[224,128]{1,0:T(8,128)(2,1)S(1)} %final_merge.1.refs_0_), channel_id=1, source_target_pairs={{0,16},{4,20},{8,24},{12,28},{16,0},{20,4},{24,8},{28,12},{1,17},{... | collective-permute-start | bytes 172040 | tf_op jit(solution)/shard_map/ppermute | solution.py:504
  103.1 4.2 %collective-permute-start.14 = (bf16[224,128]{1,0:T(8,128)(2,1)S(1)}, bf16[224,128]{1,0:T(8,128)(2,1)S(1)}, u32[]{:S(2)}, u32[]{:S(2)}) collective-permute-start(bf16[224,128]{1,0:T(8,128)(2,1)S(1)} %final_merge.1.refs_0_), channel_id=1, source_target_pairs={{0,8},{4,12},{8,0},{12,4},{16,24},{20,28},{24,16},{28,20},{1,9},{5... | collective-permute-start | bytes 172040 | tf_op jit(solution)/shard_map/ppermute | solution.py:504
  107.3 1.6 %collective-permute-start.18 = (bf16[3,224,128]{2,1,0:T(8,128)(2,1)S(1)}, bf16[3,224,128]{2,1,0:T(8,128)(2,1)S(1)}, u32[]{:S(2)}, u32[]{:S(2)}) collective-permute-start(bf16[3,224,128]{2,1,0:T(8,128)(2,1)S(1)} %pack_heads.1), channel_id=1, source_target_pairs={{0,4},{4,0},{8,12},{12,8},{16,20},{20,16},{24,28},{28,24},{1,5},{5... | collective-permute-start | bytes 516104 | tf_op jit(solution)/shard_map/ppermute | solution.py:504
  107.3 1.5 %collective-permute-start.17 = (bf16[224,128]{1,0:T(8,128)(2,1)S(1)}, bf16[224,128]{1,0:T(8,128)(2,1)S(1)}, u32[]{:S(2)}, u32[]{:S(2)}) collective-permute-start(bf16[224,128]{1,0:T(8,128)(2,1)S(1)} %final_merge.1.refs_0_), channel_id=1, source_target_pairs={{0,4},{4,0},{8,12},{12,8},{16,20},{20,16},{24,28},{28,24},{1,5},{5... | collective-permute-start | bytes 172040 | tf_op jit(solution)/shard_map/ppermute | solution.py:504
  109.3 11.9 %collective-permute-start.19 = (bf16[112,512]{1,0:T(8,128)(2,1)S(1)}, bf16[112,512]{1,0:T(8,128)(2,1)S(1)}, u32[]{:S(2)}, u32[]{:S(2)}) collective-permute-start(bf16[112,512]{1,0:T(8,128)(2,1)S(1)} %get-tuple-element.86), channel_id=1, source_target_pairs={{0,2},{1,3},{2,0},{3,1},{4,6},{5,7},{6,4},{7,5},{8,10},{9,11},{10,... | collective-permute-start | bytes 344072 | tf_op jit(solution)/shard_map/ppermute | solution.py:504
  111.6 9.7 %collective-permute-start.20 = (bf16[112,512]{1,0:T(8,128)(2,1)S(1)}, bf16[112,512]{1,0:T(8,128)(2,1)S(1)}, u32[]{:S(2)}, u32[]{:S(2)}) collective-permute-start(bf16[112,512]{1,0:T(8,128)(2,1)S(1)} %get-tuple-element.87), channel_id=1, source_target_pairs={{0,3},{1,2},{2,1},{3,0},{4,7},{5,6},{6,5},{7,4},{8,11},{9,10},{10,... | collective-permute-start | bytes 344072 | tf_op jit(solution)/shard_map/ppermute | solution.py:504
  113.3 8.6 %collective-permute-start.21 = (bf16[112,512]{1,0:T(8,128)(2,1)S(1)}, bf16[112,512]{1,0:T(8,128)(2,1)S(1)}, u32[]{:S(2)}, u32[]{:S(2)}) collective-permute-start(bf16[112,512]{1,0:T(8,128)(2,1)S(1)} %get-tuple-element.88), channel_id=1, source_target_pairs={{0,1},{1,0},{2,3},{3,2},{4,5},{5,4},{6,7},{7,6},{8,9},{9,8},{10,11... | collective-permute-start | bytes 344072 | tf_op jit(solution)/shard_map/ppermute | solution.py:504

commit v7 on v6

--- a/solution.py
+++ b/solution.py
@@ -230,7 +230,7 @@
             pad = jnp.zeros((STAT_ROWS - z.square_lines, 128), F32)
             own_ref[...] = jnp.concatenate([total, squares, pad], axis=0)
         else:
-            send_refs[i - 1][...] = pack_sums(z, total, squares)
+            send_refs[-i][...] = pack_sums(z, total, squares)
 
 
 def finish_kernel(z, features, own_ref, *refs):
@@ -420,7 +420,7 @@
         [ref.at[k] for ref, size in zip(block, sizes) for k in range(size)]
         for block, sizes in ((refs, mine_sets), (refs[len(mine_sets) :], got_sets))
     ]
-    for send_ref, mine_ref, got_ref in zip(refs[count:], *places):
+    for send_ref, mine_ref, got_ref in zip(refs[count:][::-1], *places):
         highest, total, mixed = merge(z, [mine_ref[...], got_ref[...]])
         send_ref[...] = jnp.concatenate([mixed, stack_stats([highest, total])], axis=0).astype(BF16)
 
@@ -574,7 +574,7 @@
         1e6,
     )
     visible, *sends = lax.optimization_barrier((visible, *sends))
-    gots = [swap(send, "ctx", n, 2 * (i + 1)) for i, send in enumerate(sends)]
+    gots = [swap(send, "ctx", n, n - 2 * (i + 1)) for i, send in enumerate(sends)]
     keys, values, live, extra_bias = prepare(cache_lengths, visible)
     own, keys, values, live, extra_bias = lax.optimization_barrier(
         (own, keys, values, live, extra_bias)
@@ -639,7 +639,7 @@
         1e6,
     )
     query, *sends = lax.optimization_barrier((query, *sends))
-    gots = [swap(send, "ctx", n, 2 * (i + 1)) for i, send in enumerate(sends)]
+    gots = [swap(send, "ctx", n, n - 2 * (i + 1)) for i, send in enumerate(sends)]
     queries[0] = query
     (own,) = attend((0,), False, "attend_own")
     (attended,) = call(

time: 123 us -> 123 us (level)
  transfers between devices with their start and end apart: 22 -> 22, of which waited for: 8 -> 9; matrix products, arithmetic and copies ran while one was open for 0% -> 0% of each run, Pallas kernels for 63% -> 63%
where the time goes in v7:
time: 123 us
  Pallas kernels  82.2 us (67%)
  starting transfers between devices  21.3 us (17%)
  waiting for transfers between devices  17.6 us (14%)
  between operations  1.52 us (1%)
    pallas_call x16, Pallas kernels, call(): pl.pallas_call(kernel, out_shape=out_shape, in_specs=[scalar] * smem + [w...  82.2 us
    ppermute x22, starting transfers between devices, swap(): return lax.ppermute(x, axis, [(i, i ^ d) for i in range(size)])  21.3 us
    ppermute x22, waiting for transfers between devices, swap(): return lax.ppermute(x, axis, [(i, i ^ d) for i in range(size)])  17.6 us
  transfers between devices with their start and end apart: 22, of which 9 were waited for; matrix products, arithmetic and copies ran while one was open for 0% of the time, Pallas kernels for 63%

profile of v7, /device:TPU:0, one launch (start us, length us, event | category | flops | bytes accessed | tf_op | source)
XLA Modules:
  0.0 122.6 jit_solution(95075413210046091)
XLA Ops:
  0.6 2.9 %project.1 = (f32[4,304,128]{2,1,0:T(8,128)S(1)}, bf16[4,528,128]{2,1,0:T(8,128)(2,1)S(1)}) custom-call(bf16[8,128]{1,0:T(8,128)(2,1)} %bitcast.9, bf16[128,1024]{1,0:T(8,128)(2,1)} %xp_hbm.1, bf16[96,1024]{1,0:T(8,128)(2,1)} %bitcast.8, bf16[1024,1024]{1,0:T(8,128)(2,1)} %wq_hbm.1, bf16[1024,128]{1,0:T(8,128)(2,1)} %wk_hbm.1, bf16[1024,128]{1,0:T(8,128)(2,1)} %wv_hbm.1), custom_call_target="tpu_custom_call" | custom-call | flops 587202560 | bytes 1048576 | tf_op jit(solution)/shard_map/project/pallas_call | solution.py:103
  3.5 0.5 collective-permute-start
  4.0 1.6 %collective-permute-done.got_ref = bf16[4,528,128]{2,1,0:T(8,128)(2,1)S(1)} collective-permute-done((bf16[4,528,128]{2,1,0:T(8,128)(2,1)S(1)}, bf16[4,528,128]{2,1,0:T(8,128)(2,1)S(1)}, u32[]{:S(2)}, u32[]{:S(2)}) %collective-permute-start) | collective-permute-done | bytes 540704 | tf_op jit(solution)/shard_map/ppermute | solution.py:504
  5.7 3.9 %collective-permute-start.1 = (bf16[528,128]{1,0:T(8,128)(2,1)S(1)}, bf16[528,128]{1,0:T(8,128)(2,1)S(1)}, u32[]{:S(2)}, u32[]{:S(2)}) collective-permute-start(bf16[528,128]{1,0:T(8,128)(2,1)S(1)} %get-tuple-element.61), channel_id=1, source_target_pairs={{0,24},{4,28},{8,16},{12,20},{16,8},{20,12},{24,0},{28,4},{1,25},{... | collective-permute-start | bytes 405512 | tf_op jit(solution)/shard_map/ppermute | solution.py:504
  9.6 0.5 collective-permute-start.2
  10.9 2.2 %prepare.1 = (bf16[8192,128]{1,0:T(8,128)(2,1)S(1)}, bf16[8192,128]{1,0:T(8,128)(2,1)S(1)}, bf16[8192,128]{1,0:T(8,128)(2,1)S(1)}, f32[224,32]{1,0:T(8,128)S(1)}) custom-call(s32[1]{0:T(128)S(6)} %copy.13.length_ref, s32[1,32]{1,0:T(1,128)S(1)} %bitcast.5, bf16[8192,128]{1,0:T(8,128)(2,1)} %bitcast.6, bf16[8192,128]{1,0:T(8,128)(2,1)} %bitcast.7), custom_call_target="tpu_custom_call" | custom-call | flops 1000000 | bytes 1048576 | tf_op jit(solution)/shard_map/prepare/pallas_call | solution.py:103
  13.2 0.5 collective-permute-done.1.refs_0_
  13.7 2.7 %collective-permute-done.2.refs_1_ = bf16[528,128]{1,0:T(8,128)(2,1)S(1)} collective-permute-done((bf16[528,128]{1,0:T(8,128)(2,1)S(1)}, bf16[528,128]{1,0:T(8,128)(2,1)S(1)}, u32[]{:S(2)}, u32[]{:S(2)}) %collective-permute-start.2) | collective-permute-done | bytes 135200 | tf_op jit(solution)/shard_map/ppermute | solution.py:504
  16.9 1.6 %collective-permute-start.7 = (bf16[224,128]{1,0:T(8,128)(2,1)S(1)}, bf16[224,128]{1,0:T(8,128)(2,1)S(1)}, u32[]{:S(2)}, u32[]{:S(2)}) collective-permute-start(bf16[224,128]{1,0:T(8,128)(2,1)S(1)} %get-tuple-element.76.refs_6_), channel_id=1, source_target_pairs={{0,24},{4,28},{8,16},{12,20},{16,8},{20,12},{24,0},{28,4},{1,25},{... | collective-permute-start | bytes 172040 | tf_op jit(solution)/shard_map/ppermute | solution.py:504
  18.5 1.4 %collective-permute-start.6 = (bf16[224,128]{1,0:T(8,128)(2,1)S(1)}, bf16[224,128]{1,0:T(8,128)(2,1)S(1)}, u32[]{:S(2)}, u32[]{:S(2)}) collective-permute-start(bf16[224,128]{1,0:T(8,128)(2,1)S(1)} %get-tuple-element.76.refs_6_), channel_id=1, source_target_pairs={{0,16},{4,20},{8,24},{12,28},{16,0},{20,4},{24,8},{28,12},{1,17},{... | collective-permute-start | bytes 172040 | tf_op jit(solution)/shard_map/ppermute | solution.py:504
  20.0 0.5 collective-permute-start.5
  20.5 9.4 %attend_core.1 = bf16[240,128]{1,0:T(8,128)(2,1)S(1)} custom-call(bf16[8192,128]{1,0:T(8,128)(2,1)S(1)} %get-tuple-element.57.refs_0_, bf16[8192,128]{1,0:T(8,128)(2,1)S(1)} %get-tuple-element.58.refs_1_, bf16[8192,128]{1,0:T(8,128)(2,1)S(1)} %get-tuple-element.59.refs_2_, bf16[32,128]{1,0:T(8,128)(2,1)S(1)} %get-tuple-element.64.refs_3_, ...), custom_call_target="tpu_custom_call" | custom-call | flops 1879048192 | bytes 1048576 | tf_op jit(solution)/shard_map/attend_core/pallas_call | solution.py:103
  30.1 0.6 collective-permute-start.8
  30.6 9.6 %attend_near.1.refs_0_ = bf16[1,240,128]{2,1,0:T(8,128)(2,1)S(1)} custom-call(bf16[8192,128]{1,0:T(8,128)(2,1)S(1)} %get-tuple-element.57.refs_0_, bf16[8192,128]{1,0:T(8,128)(2,1)S(1)} %get-tuple-element.58.refs_1_, bf16[8192,128]{1,0:T(8,128)(2,1)S(1)} %get-tuple-element.59.refs_2_, bf16[32,128]{1,0:T(8,128)(2,1)S(1)} %get-tuple-element.64.refs_3_, ...), custom_call_target="tpu_custom_call" | custom-call | flops 1879048192 | bytes 1048576 | tf_op jit(solution)/shard_map/attend_near/pallas_call | solution.py:103
  40.3 27.4 %attend_odd0.1 = bf16[3,240,128]{2,1,0:T(8,128)(2,1)S(1)} custom-call(bf16[8192,128]{1,0:T(8,128)(2,1)S(1)} %get-tuple-element.57.refs_0_, bf16[8192,128]{1,0:T(8,128)(2,1)S(1)} %get-tuple-element.58.refs_1_, bf16[8192,128]{1,0:T(8,128)(2,1)S(1)} %get-tuple-element.59.refs_2_, bf16[32,128]{1,0:T(8,128)(2,1)S(1)} %get-tuple-element.64.refs_3_, ...), custom_call_target="tpu_custom_call" | custom-call | flops 5637144576 | bytes 1048576 | tf_op jit(solution)/shard_map/attend_odd0/pallas_call | solution.py:103
  67.7 18.4 %attend_even0.1.refs_1_ = bf16[2,240,128]{2,1,0:T(8,128)(2,1)S(1)} custom-call(bf16[8192,128]{1,0:T(8,128)(2,1)S(1)} %get-tuple-element.57.refs_0_, bf16[8192,128]{1,0:T(8,128)(2,1)S(1)} %get-tuple-element.58.refs_1_, bf16[8192,128]{1,0:T(8,128)(2,1)S(1)} %get-tuple-element.59.refs_2_, bf16[32,128]{1,0:T(8,128)(2,1)S(1)} %get-tuple-element.64.refs_3_, ...), custom_call_target="tpu_custom_call" | custom-call | flops 3758096384 | bytes 1048576 | tf_op jit(solution)/shard_map/attend_even0/pallas_call | solution.py:103
  86.7 2.9 %collective-permute-start.12 = (bf16[240,128]{1,0:T(8,128)(2,1)S(1)}, bf16[240,128]{1,0:T(8,128)(2,1)S(1)}, u32[]{:S(2)}, u32[]{:S(2)}) collective-permute-start(bf16[240,128]{1,0:T(8,128)(2,1)S(1)} %get-tuple-element.79), channel_id=1, source_target_pairs={{0,16},{4,20},{8,24},{12,28},{16,0},{20,4},{24,8},{28,12},{1,17},{... | collective-permute-start | bytes 184328 | tf_op jit(solution)/shard_map/ppermute | solution.py:504
  89.6 0.5 collective-permute-start.13
  90.1 9.4 %attend_own.1.refs_0_ = bf16[240,128]{1,0:T(8,128)(2,1)S(1)} custom-call(bf16[8192,128]{1,0:T(8,128)(2,1)S(1)} %get-tuple-element.57.refs_0_, bf16[8192,128]{1,0:T(8,128)(2,1)S(1)} %get-tuple-element.58.refs_1_, bf16[8192,128]{1,0:T(8,128)(2,1)S(1)} %get-tuple-element.59.refs_2_, bf16[32,128]{1,0:T(8,128)(2,1)S(1)} %get-tuple-element.64.refs_3_, ...), custom_call_target="tpu_custom_call" | custom-call | flops 1879048192 | bytes 1048576 | tf_op jit(solution)/shard_map/attend_own/pallas_call | solution.py:103
  99.6 0.5 final_merge.1.refs_0_
  100.2 2.9 %collective-permute-start.15 = (bf16[224,128]{1,0:T(8,128)(2,1)S(1)}, bf16[224,128]{1,0:T(8,128)(2,1)S(1)}, u32[]{:S(2)}, u32[]{:S(2)}) collective-permute-start(bf16[224,128]{1,0:T(8,128)(2,1)S(1)} %final_merge.1.refs_0_), channel_id=1, source_target_pairs={{0,16},{4,20},{8,24},{12,28},{16,0},{20,4},{24,8},{28,12},{1,17},{... | collective-permute-start | bytes 172040 | tf_op jit(solution)/shard_map/ppermute | solution.py:504
  103.1 0.5 collective-permute-start.14
  103.6 2.2 %collective-permute-done.16.refs_2_.refs_3_ = bf16[224,128]{1,0:T(8,128)(2,1)S(1)} collective-permute-done((bf16[224,128]{1,0:T(8,128)(2,1)S(1)}, bf16[224,128]{1,0:T(8,128)(2,1)S(1)}, u32[]{:S(2)}, u32[]{:S(2)}) %collective-permute-start.16) | collective-permute-done | bytes 57376 | tf_op jit(solution)/shard_map/ppermute | solution.py:504
  105.9 1.4 %collective-permute-done.14.refs_0_.refs_1_ = bf16[224,128]{1,0:T(8,128)(2,1)S(1)} collective-permute-done((bf16[224,128]{1,0:T(8,128)(2,1)S(1)}, bf16[224,128]{1,0:T(8,128)(2,1)S(1)}, u32[]{:S(2)}, u32[]{:S(2)}) %collective-permute-start.14) | collective-permute-done | bytes 57376 | tf_op jit(solution)/shard_map/ppermute | solution.py:504
  107.4 0.5 collective-permute-start.17
  108.3 0.5 collective-permute-done.17.first_ref
  108.9 0.5 output_odd.1
  109.4 1.4 %collective-permute-start.19 = (bf16[112,512]{1,0:T(8,128)(2,1)S(1)}, bf16[112,512]{1,0:T(8,128)(2,1)S(1)}, u32[]{:S(2)}, u32[]{:S(2)}) collective-permute-start(bf16[112,512]{1,0:T(8,128)(2,1)S(1)} %get-tuple-element.86), channel_id=1, source_target_pairs={{0,2},{1,3},{2,0},{3,1},{4,6},{5,7},{6,4},{7,5},{8,10},{9,11},{10,... | collective-permute-start | bytes 344072 | tf_op jit(solution)/shard_map/ppermute | solution.py:504
  110.8 2.6 %collective-permute-start.20 = (bf16[112,512]{1,0:T(8,128)(2,1)S(1)}, bf16[112,512]{1,0:T(8,128)(2,1)S(1)}, u32[]{:S(2)}, u32[]{:S(2)}) collective-permute-start(bf16[112,512]{1,0:T(8,128)(2,1)S(1)} %get-tuple-element.87), channel_id=1, source_target_pairs={{0,3},{1,2},{2,1},{3,0},{4,7},{5,6},{6,5},{7,4},{8,11},{9,10},{10,... | collective-permute-start | bytes 344072 | tf_op jit(solution)/shard_map/ppermute | solution.py:504
  113.6 7.7 %collective-permute-done.19.refs_0_ = bf16[112,512]{1,0:T(8,128)(2,1)S(1)} collective-permute-done((bf16[112,512]{1,0:T(8,128)(2,1)S(1)}, bf16[112,512]{1,0:T(8,128)(2,1)S(1)}, u32[]{:S(2)}, u32[]{:S(2)}) %collective-permute-start.19) | collective-permute-done | bytes 114720 | tf_op jit(solution)/shard_map/ppermute | solution.py:504
  121.3 0.7 collective-permute-done.21.refs_2_
  121.9 0.7 share_sum.1
  (32 shorter events, 2.3 us)
Async XLA Ops:
  0.6 10.3 %copy-start.1 = (s32[32]{0:T(128)S(1)}, s32[32]{0:T(128)}, u32[]{:S(2)}) copy-start(s32[32]{0:T(128)} %param.21) | copy-start | bytes 388
  3.5 2.1 %collective-permute-start = (bf16[4,528,128]{2,1,0:T(8,128)(2,1)S(1)}, bf16[4,528,128]{2,1,0:T(8,128)(2,1)S(1)}, u32[]{:S(2)}, u32[]{:S(2)}) collective-permute-start(bf16[4,528,128]{2,1,0:T(8,128)(2,1)S(1)} %get-tuple-element.47), channel_id=1, source_target_pairs={{0,4},{4,0},{8,12},{12,8},{16,20},{20,16},{24,28},{28,24},{1,5},{5... | collective-permute-start | bytes 1622024 | tf_op jit(solution)/shard_map/ppermute | solution.py:504
  5.7 8.0 %collective-permute-start.1 = (bf16[528,128]{1,0:T(8,128)(2,1)S(1)}, bf16[528,128]{1,0:T(8,128)(2,1)S(1)}, u32[]{:S(2)}, u32[]{:S(2)}) collective-permute-start(bf16[528,128]{1,0:T(8,128)(2,1)S(1)} %get-tuple-element.61), channel_id=1, source_target_pairs={{0,24},{4,28},{8,16},{12,20},{16,8},{20,12},{24,0},{28,4},{1,25},{... | collective-permute-start | bytes 405512 | tf_op jit(solution)/shard_map/ppermute | solution.py:504
  9.6 6.8 %collective-permute-start.2 = (bf16[528,128]{1,0:T(8,128)(2,1)S(1)}, bf16[528,128]{1,0:T(8,128)(2,1)S(1)}, u32[]{:S(2)}, u32[]{:S(2)}) collective-permute-start(bf16[528,128]{1,0:T(8,128)(2,1)S(1)} %get-tuple-element.62), channel_id=1, source_target_pairs={{0,16},{4,20},{8,24},{12,28},{16,0},{20,4},{24,8},{28,12},{1,17},{... | collective-permute-start | bytes 405512 | tf_op jit(solution)/shard_map/ppermute | solution.py:504
  10.1 6.6 %collective-permute-start.3 = (bf16[528,128]{1,0:T(8,128)(2,1)S(1)}, bf16[528,128]{1,0:T(8,128)(2,1)S(1)}, u32[]{:S(2)}, u32[]{:S(2)}) collective-permute-start(bf16[528,128]{1,0:T(8,128)(2,1)S(1)} %get-tuple-element.63), channel_id=1, source_target_pairs={{0,8},{4,12},{8,0},{12,4},{16,24},{20,28},{24,16},{28,20},{1,9},{5... | collective-permute-start | bytes 405512 | tf_op jit(solution)/shard_map/ppermute | solution.py:504
  16.9 3.6 %collective-permute-start.4 = (bf16[224,128]{1,0:T(8,128)(2,1)S(1)}, bf16[224,128]{1,0:T(8,128)(2,1)S(1)}, u32[]{:S(2)}, u32[]{:S(2)}) collective-permute-start(bf16[224,128]{1,0:T(8,128)(2,1)S(1)} %get-tuple-element.76.refs_6_), channel_id=1, source_target_pairs={{0,4},{4,0},{8,12},{12,8},{16,20},{20,16},{24,28},{28,24},{1,5},{5... | collective-permute-start | bytes 172040 | tf_op jit(solution)/shard_map/ppermute | solution.py:504
  16.9 13.0 %collective-permute-start.7 = (bf16[224,128]{1,0:T(8,128)(2,1)S(1)}, bf16[224,128]{1,0:T(8,128)(2,1)S(1)}, u32[]{:S(2)}, u32[]{:S(2)}) collective-permute-start(bf16[224,128]{1,0:T(8,128)(2,1)S(1)} %get-tuple-element.76.refs_6_), channel_id=1, source_target_pairs={{0,24},{4,28},{8,16},{12,20},{16,8},{20,12},{24,0},{28,4},{1,25},{... | collective-permute-start | bytes 172040 | tf_op jit(solution)/shard_map/ppermute | solution.py:504
  18.5 11.4 %collective-permute-start.6 = (bf16[224,128]{1,0:T(8,128)(2,1)S(1)}, bf16[224,128]{1,0:T(8,128)(2,1)S(1)}, u32[]{:S(2)}, u32[]{:S(2)}) collective-permute-start(bf16[224,128]{1,0:T(8,128)(2,1)S(1)} %get-tuple-element.76.refs_6_), channel_id=1, source_target_pairs={{0,16},{4,20},{8,24},{12,28},{16,0},{20,4},{24,8},{28,12},{1,17},{... | collective-permute-start | bytes 172040 | tf_op jit(solution)/shard_map/ppermute | solution.py:504
  20.0 10.0 %collective-permute-start.5 = (bf16[224,128]{1,0:T(8,128)(2,1)S(1)}, bf16[224,128]{1,0:T(8,128)(2,1)S(1)}, u32[]{:S(2)}, u32[]{:S(2)}) collective-permute-start(bf16[224,128]{1,0:T(8,128)(2,1)S(1)} %get-tuple-element.76.refs_6_), channel_id=1, source_target_pairs={{0,8},{4,12},{8,0},{12,4},{16,24},{20,28},{24,16},{28,20},{1,9},{5... | collective-permute-start | bytes 172040 | tf_op jit(solution)/shard_map/ppermute | solution.py:504
  30.0 69.6 %collective-permute-start.10 = (bf16[240,128]{1,0:T(8,128)(2,1)S(1)}, bf16[240,128]{1,0:T(8,128)(2,1)S(1)}, u32[]{:S(2)}, u32[]{:S(2)}) collective-permute-start(bf16[240,128]{1,0:T(8,128)(2,1)S(1)} %attend_core.1), channel_id=1, source_target_pairs={{0,4},{4,0},{8,12},{12,8},{16,20},{20,16},{24,28},{28,24},{1,5},{5... | collective-permute-start | bytes 184328 | tf_op jit(solution)/shard_map/ppermute | solution.py:504
  30.1 10.2 %collective-permute-start.8 = (bf16[3,224,128]{2,1,0:T(8,128)(2,1)S(1)}, bf16[3,224,128]{2,1,0:T(8,128)(2,1)S(1)}, u32[]{:S(2)}, u32[]{:S(2)}) collective-permute-start(bf16[3,224,128]{2,1,0:T(8,128)(2,1)S(1)} %pack_queries.1), channel_id=1, source_target_pairs={{0,4},{4,0},{8,12},{12,8},{16,20},{20,16},{24,28},{28,24},{1,5},{5... | collective-permute-start | bytes 516104 | tf_op jit(solution)/shard_map/ppermute | solution.py:504
  67.7 18.5 %collective-permute-start.9 = (bf16[3,240,128]{2,1,0:T(8,128)(2,1)S(1)}, bf16[3,240,128]{2,1,0:T(8,128)(2,1)S(1)}, u32[]{:S(2)}, u32[]{:S(2)}) collective-permute-start(bf16[3,240,128]{2,1,0:T(8,128)(2,1)S(1)} %attend_odd0.1), channel_id=1, source_target_pairs={{0,4},{4,0},{8,12},{12,8},{16,20},{20,16},{24,28},{28,24},{1,5},{5... | collective-permute-start | bytes 552968 | tf_op jit(solution)/shard_map/ppermute | solution.py:504
  86.6 21.3 %copy-start = (bf16[1024,1024]{1,0:T(8,128)(2,1)S(1)}, bf16[1024,1024]{1,0:T(8,128)(2,1)}, u32[]{:S(2)}) copy-start(bf16[1024,1024]{1,0:T(8,128)(2,1)} %weight_ref.3) | copy-start | bytes 6291460
  86.6 13.0 %collective-permute-start.11 = (bf16[240,128]{1,0:T(8,128)(2,1)S(1)}, bf16[240,128]{1,0:T(8,128)(2,1)S(1)}, u32[]{:S(2)}, u32[]{:S(2)}) collective-permute-start(bf16[240,128]{1,0:T(8,128)(2,1)S(1)} %get-tuple-element.78), channel_id=1, source_target_pairs={{0,24},{4,28},{8,16},{12,20},{16,8},{20,12},{24,0},{28,4},{1,25},{... | collective-permute-start | bytes 184328 | tf_op jit(solution)/shard_map/ppermute | solution.py:504
  86.7 12.9 %collective-permute-start.12 = (bf16[240,128]{1,0:T(8,128)(2,1)S(1)}, bf16[240,128]{1,0:T(8,128)(2,1)S(1)}, u32[]{:S(2)}, u32[]{:S(2)}) collective-permute-start(bf16[240,128]{1,0:T(8,128)(2,1)S(1)} %get-tuple-element.79), channel_id=1, source_target_pairs={{0,16},{4,20},{8,24},{12,28},{16,0},{20,4},{24,8},{28,12},{1,17},{... | collective-permute-start | bytes 184328 | tf_op jit(solution)/shard_map/ppermute | solution.py:504
  89.6 10.0 %collective-permute-start.13 = (bf16[240,128]{1,0:T(8,128)(2,1)S(1)}, bf16[240,128]{1,0:T(8,128)(2,1)S(1)}, u32[]{:S(2)}, u32[]{:S(2)}) collective-permute-start(bf16[240,128]{1,0:T(8,128)(2,1)S(1)} %get-tuple-element.80), channel_id=1, source_target_pairs={{0,8},{4,12},{8,0},{12,4},{16,24},{20,28},{24,16},{28,20},{1,9},{5... | collective-permute-start | bytes 184328 | tf_op jit(solution)/shard_map/ppermute | solution.py:504
  100.1 5.8 %collective-permute-start.16 = (bf16[224,128]{1,0:T(8,128)(2,1)S(1)}, bf16[224,128]{1,0:T(8,128)(2,1)S(1)}, u32[]{:S(2)}, u32[]{:S(2)}) collective-permute-start(bf16[224,128]{1,0:T(8,128)(2,1)S(1)} %final_merge.1.refs_0_), channel_id=1, source_target_pairs={{0,24},{4,28},{8,16},{12,20},{16,8},{20,12},{24,0},{28,4},{1,25},{... | collective-permute-start | bytes 172040 | tf_op jit(solution)/shard_map/ppermute | solution.py:504
  100.2 5.7 %collective-permute-start.15 = (bf16[224,128]{1,0:T(8,128)(2,1)S(1)}, bf16[224,128]{1,0:T(8,128)(2,1)S(1)}, u32[]{:S(2)}, u32[]{:S(2)}) collective-permute-start(bf16[224,128]{1,0:T(8,128)(2,1)S(1)} %final_merge.1.refs_0_), channel_id=1, source_target_pairs={{0,16},{4,20},{8,24},{12,28},{16,0},{20,4},{24,8},{28,12},{1,17},{... | collective-permute-start | bytes 172040 | tf_op jit(solution)/shard_map/ppermute | solution.py:504
  103.1 4.2 %collective-permute-start.14 = (bf16[224,128]{1,0:T(8,128)(2,1)S(1)}, bf16[224,128]{1,0:T(8,128)(2,1)S(1)}, u32[]{:S(2)}, u32[]{:S(2)}) collective-permute-start(bf16[224,128]{1,0:T(8,128)(2,1)S(1)} %final_merge.1.refs_0_), channel_id=1, source_target_pairs={{0,8},{4,12},{8,0},{12,4},{16,24},{20,28},{24,16},{28,20},{1,9},{5... | collective-permute-start | bytes 172040 | tf_op jit(solution)/shard_map/ppermute | solution.py:504
  107.3 1.6 %collective-permute-start.18 = (bf16[3,224,128]{2,1,0:T(8,128)(2,1)S(1)}, bf16[3,224,128]{2,1,0:T(8,128)(2,1)S(1)}, u32[]{:S(2)}, u32[]{:S(2)}) collective-permute-start(bf16[3,224,128]{2,1,0:T(8,128)(2,1)S(1)} %pack_heads.1), channel_id=1, source_target_pairs={{0,4},{4,0},{8,12},{12,8},{16,20},{20,16},{24,28},{28,24},{1,5},{5... | collective-permute-start | bytes 516104 | tf_op jit(solution)/shard_map/ppermute | solution.py:504
  107.4 1.5 %collective-permute-start.17 = (bf16[224,128]{1,0:T(8,128)(2,1)S(1)}, bf16[224,128]{1,0:T(8,128)(2,1)S(1)}, u32[]{:S(2)}, u32[]{:S(2)}) collective-permute-start(bf16[224,128]{1,0:T(8,128)(2,1)S(1)} %final_merge.1.refs_0_), channel_id=1, source_target_pairs={{0,4},{4,0},{8,12},{12,8},{16,20},{20,16},{24,28},{28,24},{1,5},{5... | collective-permute-start | bytes 172040 | tf_op jit(solution)/shard_map/ppermute | solution.py:504
  109.4 11.9 %collective-permute-start.19 = (bf16[112,512]{1,0:T(8,128)(2,1)S(1)}, bf16[112,512]{1,0:T(8,128)(2,1)S(1)}, u32[]{:S(2)}, u32[]{:S(2)}) collective-permute-start(bf16[112,512]{1,0:T(8,128)(2,1)S(1)} %get-tuple-element.86), channel_id=1, source_target_pairs={{0,2},{1,3},{2,0},{3,1},{4,6},{5,7},{6,4},{7,5},{8,10},{9,11},{10,... | collective-permute-start | bytes 344072 | tf_op jit(solution)/shard_map/ppermute | solution.py:504
  110.8 10.5 %collective-permute-start.20 = (bf16[112,512]{1,0:T(8,128)(2,1)S(1)}, bf16[112,512]{1,0:T(8,128)(2,1)S(1)}, u32[]{:S(2)}, u32[]{:S(2)}) collective-permute-start(bf16[112,512]{1,0:T(8,128)(2,1)S(1)} %get-tuple-element.87), channel_id=1, source_target_pairs={{0,3},{1,2},{2,1},{3,0},{4,7},{5,6},{6,5},{7,4},{8,11},{9,10},{10,... | collective-permute-start | bytes 344072 | tf_op jit(solution)/shard_map/ppermute | solution.py:504
  113.4 8.6 %collective-permute-start.21 = (bf16[112,512]{1,0:T(8,128)(2,1)S(1)}, bf16[112,512]{1,0:T(8,128)(2,1)S(1)}, u32[]{:S(2)}, u32[]{:S(2)}) collective-permute-start(bf16[112,512]{1,0:T(8,128)(2,1)S(1)} %get-tuple-element.88), channel_id=1, source_target_pairs={{0,1},{1,0},{2,3},{3,2},{4,5},{5,4},{6,7},{7,6},{8,9},{9,8},{10,11... | collective-permute-start | bytes 344072 | tf_op jit(solution)/shard_map/ppermute | solution.py:504
